TPU v7x, 32 devices: a whole 2x2x4 slice. The times are simulated.
32 devices in a mesh: tile: 8 (over z, core), scan: 4 (over y, x).
Axes of the slice: x: 2, y: 2, z: 4, core: 2. Of those that a mesh axis runs over, the one named last changes fastest.
Arguments:
- consensus: float32 [8, 2, 256, 256], P('tile'), may hold values from -4 to 4
- duals: float32 [4, 8, 2, 256, 256], P('scan', 'tile'), may hold values from -3 to 3
- probes: float32 [4, 2, 256, 256], P('scan'), may hold values from -4 to 4
- amplitudes: bfloat16 [4, 8, 4, 256, 256], P('scan', 'tile'), may hold values from 0.19921875 to 2
- offsets: int32 [4, 8, 4, 2], P('scan', 'tile'), may hold values from 0 to 128
- counts: int32 [4, 8], P('scan', 'tile'), may hold values from 1 to 4, as said below
Outputs:
- consensus_new: float32 [8, 2, 256, 256], P('tile')
- duals_new: float32 [4, 8, 2, 256, 256], P('scan', 'tile')
- probes_new: float32 [4, 2, 256, 256], P('scan')
Inputs may be any that keep to these rules, and one draw needn't show every extreme that they name: counts: some group has 4 scan positions in some tile; slots at or past the count are unused. offsets: first the row, then the column.
All inputs are finite; a program needn't handle non-finite values.
Results may differ from a plain program's by a relative error of at most 0.015.
Values may be sent and summed in bfloat16 or wider, within the bound.
No kernel may reach another device: no remote copies, remote signals or barrier semaphores. Data moves between devices by JAX's collectives and lax.ppermute only.
A program may use at most 64 MiB of HBM per device.

v0:
```python
import math

import jax
import jax.numpy as jnp
from jax import lax
from jax.sharding import PartitionSpec as P

PS = 256
TS = 256
OVER = 128
TGW = 4
INNER = 2


penalty = 0.5
smoothing = 0.05
probe_step = 3.0


def passed_along(value, axis, by):
    length = lax.axis_size(axis)
    pairs = [(i, i + by) for i in range(length) if 0 <= i + by < length]
    return lax.ppermute(value, axis, pairs)


def dft_tables(length):
    indices = jnp.arange(length, dtype=jnp.int32)
    phase_index = indices[:, None] * indices[None, :] % length
    angles = phase_index.astype(jnp.float32) * (2.0 * math.pi / length)
    norm_scale = 1.0 / math.sqrt(length)
    real_part = (jnp.cos(angles) * norm_scale).astype(jnp.bfloat16)
    imag_part = (-jnp.sin(angles) * norm_scale).astype(jnp.bfloat16)
    return (real_part, imag_part)


def forward_wave(wave_real, wave_imag, stacked, spread, length):
    section_one = jnp.dot(
        stacked, jnp.concatenate([wave_real, wave_imag], 1), preferred_element_type=jnp.float32
    )
    inner_real = (section_one[:length, :length] - section_one[length:, length:]).astype(
        jnp.bfloat16
    )
    inner_imag = (section_one[:length, length:] + section_one[length:, :length]).astype(
        jnp.bfloat16
    )
    section_two = jnp.dot(
        jnp.concatenate([inner_real, inner_imag], 0), spread, preferred_element_type=jnp.float32
    )
    return (
        section_two[:length, :length] - section_two[length:, length:],
        section_two[:length, length:] + section_two[length:, :length],
    )


def inverse_wave(wave_real, wave_imag, stacked, spread, length):
    section_one = jnp.dot(
        stacked, jnp.concatenate([wave_real, wave_imag], 1), preferred_element_type=jnp.float32
    )
    inner_real = (section_one[:length, :length] + section_one[length:, length:]).astype(
        jnp.bfloat16
    )
    inner_imag = (section_one[:length, length:] - section_one[length:, :length]).astype(
        jnp.bfloat16
    )
    section_two = jnp.dot(
        jnp.concatenate([inner_real, inner_imag], 0), spread, preferred_element_type=jnp.float32
    )
    return (
        section_two[:length, :length] + section_two[length:, length:],
        section_two[length:, :length] - section_two[:length, length:],
    )


def patch_terms(window, probe_field, measured, stacked, spread):
    length = window.shape[1]
    object_real = window[0].astype(jnp.float32)
    object_imag = window[1].astype(jnp.float32)
    probe_real = probe_field[0]
    probe_imag = probe_field[1]
    exit_real = (probe_real * object_real - probe_imag * object_imag).astype(jnp.bfloat16)
    exit_imag = (probe_real * object_imag + probe_imag * object_real).astype(jnp.bfloat16)
    wave_real, wave_imag = forward_wave(exit_real, exit_imag, stacked, spread, length)
    modulus = jnp.sqrt(wave_real * wave_real + wave_imag * wave_imag + smoothing)
    factor = measured.astype(jnp.float32) / modulus - 1.0
    resid_real = (wave_real * factor).astype(jnp.bfloat16)
    resid_imag = (wave_imag * factor).astype(jnp.bfloat16)
    back_real, back_imag = inverse_wave(resid_real, resid_imag, stacked, spread, length)
    object_terms = jnp.stack(
        [
            probe_real * back_real + probe_imag * back_imag,
            probe_real * back_imag - probe_imag * back_real,
            probe_real * probe_real + probe_imag * probe_imag,
        ]
    )
    probe_terms = jnp.stack(
        [
            object_real * back_real + object_imag * back_imag,
            object_real * back_imag - object_imag * back_real,
            object_real * object_real + object_imag * object_imag,
        ]
    )
    return (object_terms, probe_terms)


def pull_rim(window, distance):
    return passed_along(window, "tile", distance)


def push_rim(window, distance):
    return passed_along(window.astype(jnp.bfloat16), "tile", distance).astype(window.dtype)


def project_modulus(average):
    magnitude = jnp.sqrt(average[0] * average[0] + average[1] * average[1])
    return average / jnp.maximum(magnitude, 1.0)[None]


def shards(consensus, duals, probes, amplitudes, offsets, counts):
    real_part, imag_part = dft_tables(PS)
    stacked = jnp.concatenate([real_part, imag_part], 0)
    spread = jnp.concatenate([real_part, imag_part], 1)
    column = lax.axis_index("tile") % TGW
    grid_consensus = consensus[0]
    dual_tile = duals[0, 0]
    probe_field = probes[0]
    measured = amplitudes[0, 0]
    corners = offsets[0, 0]
    slot_count = counts[0, 0]
    zero_index = jnp.zeros((), jnp.int32)
    span = TS + OVER
    estimate = grid_consensus
    probe_sum = jnp.zeros((3, PS, PS), jnp.float32)
    for sweep_index in range(INNER):
        rounded = estimate.astype(jnp.bfloat16)
        from_right = pull_rim(rounded[:, :, :OVER], -1)
        from_right = jnp.where(column == TGW - 1, jnp.zeros_like(from_right), from_right)
        widened = jnp.concatenate([rounded, from_right], 2)
        from_below = pull_rim(widened[:, :OVER, :], -TGW)
        extended = jnp.concatenate([widened, from_below], 1)

        def visit_slot(slot_index, inner_state):
            local_totals, local_probe = inner_state
            top_row = corners[slot_index, 0]
            left_col = corners[slot_index, 1]
            window = lax.dynamic_slice(extended, (zero_index, top_row, left_col), (2, PS, PS))
            object_terms, probe_terms = patch_terms(
                window, probe_field, measured[slot_index], stacked, spread
            )
            region = lax.dynamic_slice(local_totals, (zero_index, top_row, left_col), (3, PS, PS))
            local_totals = lax.dynamic_update_slice(
                local_totals, region + object_terms, (zero_index, top_row, left_col)
            )
            return (local_totals, local_probe + probe_terms)

        start_totals = jnp.zeros((3, span, span), jnp.float32)
        local_totals, probe_sum = lax.fori_loop(
            0, slot_count, visit_slot, (start_totals, probe_sum)
        )
        from_above = push_rim(local_totals[:, TS:, :], TGW)
        central = jnp.concatenate(
            [local_totals[:, :OVER, :] + from_above, local_totals[:, OVER:TS, :]], 1
        )
        from_left = push_rim(central[:, :, TS:], 1)
        from_left = jnp.where(column == 0, jnp.zeros_like(from_left), from_left)
        returned = jnp.concatenate([central[:, :, :OVER] + from_left, central[:, :, OVER:TS]], 2)
        estimate = estimate + (
            returned[0:2] + penalty * (grid_consensus - dual_tile - estimate)
        ) / (returned[2] + penalty)
    combined = estimate + dual_tile
    summed = lax.psum(combined.astype(jnp.bfloat16), "scan").astype(jnp.float32)
    settled = project_modulus(summed / lax.axis_size("scan"))
    probe_totals = lax.psum(probe_sum, "tile")
    probe_new = probe_field + probe_step * probe_totals[0:2] / jnp.sqrt(probe_totals[2] + 1.0)
    dual_new = dual_tile + estimate - settled
    return (settled[None], dual_new[None, None], probe_new[None])


def solution(mesh):
    placed = (
        P("tile", None, None, None),
        P("scan", "tile", None, None, None),
        P("scan", None, None, None),
        P("scan", "tile", None, None, None),
        P("scan", "tile", None, None),
        P("scan", "tile"),
    )
    return jax.shard_map(
        shards,
        mesh=mesh,
        in_specs=placed,
        out_specs=(
            P("tile", None, None, None),
            P("scan", "tile", None, None, None),
            P("scan", None, None, None),
        ),
        check_vma=False,
    )
```

profile of v0, /device:TPU:0, one launch (start us, length us, event | category | flops | bytes accessed | tf_op | source)
XLA Modules:
  0.0 339.9 jit_solution(4475962711617258629)
XLA Ops:
  9.2 1.4 collective-permute-start
  14.3 13.0 %collective-permute-done.1 = bf16[2,128,384]{2,1,0:T(8,128)(2,1)S(1)} collective-permute-done((bf16[2,128,384]{2,1,0:T(8,128)(2,1)S(1)}, bf16[2,128,384]{2,1,0:T(8,128)(2,1)S(1)}, u32[]{:S(2)}, u32[]{:S(2)}) %collective-permute-start.1) | collective-permute-done | bytes 196640 | tf_op jit(solution)/shard_map/ppermute | solution.py:23
  27.4 1.4 broadcast.59.clone
  28.7 77.6 %while.28 = (s32[]{:T(128)}, f32[3,384,384]{2,1,0:T(8,128)}, f32[3,256,256]{2,1,0:T(8,128)S(1)}, s32[]{:T(128)}, s32[4,2]{0,1:T(2,128)S(1)}, /*index=5*/f32[2,25...) while((s32[]{:T(128)}, f32[3,384,384]{2,1,0:T(8,128)}, ...), condition=%wide.region_1.2_spmd, body=%wide.region_0.1_spmd.sunk | while | flops 543686656 | bytes 22413668 | solution.py:156
  37.3 1.8 maximum_add_fusion.6
  39.1 8.9 %dynamic_update_slice.14 = f32[3,384,384]{2,1,0:T(8,128)} dynamic-update-slice(f32[3,384,384]{2,1,0:T(8,128)} %get-tuple-element.596, f32[3,256,256]{2,1,0:T(8,128)S(1)} %get-tuple-element.548, s32[]{:T(128)} %constant.102.clone.1..sunk, s32[]{:T(128)S(6)} %select_n.123, s32[]{:T(128)S(6)} %select_n.124) | dynamic-update-slice | bytes 1572868 | tf_op jit(solution)/shard_map/while/body/dynamic_update_slice | solution.py:150
  56.7 1.8 maximum_add_fusion.6
  58.5 8.5 %dynamic_update_slice.14 = f32[3,384,384]{2,1,0:T(8,128)} dynamic-update-slice(f32[3,384,384]{2,1,0:T(8,128)} %get-tuple-element.596, f32[3,256,256]{2,1,0:T(8,128)S(1)} %get-tuple-element.548, s32[]{:T(128)} %constant.102.clone.1..sunk, s32[]{:T(128)S(6)} %select_n.123, s32[]{:T(128)S(6)} %select_n.124) | dynamic-update-slice | bytes 1572868 | tf_op jit(solution)/shard_map/while/body/dynamic_update_slice | solution.py:150
  75.6 1.8 maximum_add_fusion.6
  77.4 9.0 %dynamic_update_slice.14 = f32[3,384,384]{2,1,0:T(8,128)} dynamic-update-slice(f32[3,384,384]{2,1,0:T(8,128)} %get-tuple-element.596, f32[3,256,256]{2,1,0:T(8,128)S(1)} %get-tuple-element.548, s32[]{:T(128)} %constant.102.clone.1..sunk, s32[]{:T(128)S(6)} %select_n.123, s32[]{:T(128)S(6)} %select_n.124) | dynamic-update-slice | bytes 1572868 | tf_op jit(solution)/shard_map/while/body/dynamic_update_slice | solution.py:150
  95.0 1.8 maximum_add_fusion.6
  96.8 8.9 %dynamic_update_slice.14 = f32[3,384,384]{2,1,0:T(8,128)} dynamic-update-slice(f32[3,384,384]{2,1,0:T(8,128)} %get-tuple-element.596, f32[3,256,256]{2,1,0:T(8,128)S(1)} %get-tuple-element.548, s32[]{:T(128)} %constant.102.clone.1..sunk, s32[]{:T(128)S(6)} %select_n.123, s32[]{:T(128)S(6)} %select_n.124) | dynamic-update-slice | bytes 1572868 | tf_op jit(solution)/shard_map/while/body/dynamic_update_slice | solution.py:150
  108.8 4.2 %collective-permute-done.2 = bf16[3,128,384]{2,1,0:T(8,128)(2,1)S(1)} collective-permute-done((bf16[3,128,384]{2,1,0:T(8,128)(2,1)S(1)}, bf16[3,128,384]{2,1,0:T(8,128)(2,1)S(1)}, u32[]{:S(2)}, u32[]{:S(2)}) %collective-permute-start.2) | collective-permute-done | bytes 294944 | tf_op jit(solution)/shard_map/ppermute | solution.py:23
  113.0 1.3 convert_add_fusion.1
  121.1 1.9 collective-permute-done.4
  124.4 17.4 %collective-permute-done.5 = bf16[2,128,384]{2,1,0:T(8,128)(2,1)S(1)} collective-permute-done((bf16[2,128,384]{2,1,0:T(8,128)(2,1)S(1)}, bf16[2,128,384]{2,1,0:T(8,128)(2,1)S(1)}, u32[]{:S(2)}, u32[]{:S(2)}) %collective-permute-start.5) | collective-permute-done | bytes 196640 | tf_op jit(solution)/shard_map/ppermute | solution.py:23
  141.9 1.4 broadcast.59
  143.2 76.7 %while.29 = (s32[]{:T(128)}, f32[3,384,384]{2,1,0:T(8,128)}, f32[3,256,256]{2,1,0:T(8,128)S(1)}, s32[]{:T(128)}, s32[4,2]{0,1:T(2,128)S(1)}, /*index=5*/f32[2,25...) while((s32[]{:T(128)}, f32[3,384,384]{2,1,0:T(8,128)}, ...), condition=%wide.region_3.4_spmd, body=%wide.region_2.3_spmd.sunk | while | flops 543686656 | bytes 22413668 | solution.py:156
  151.6 1.8 maximum_add_fusion.7
  153.4 8.9 %dynamic_update_slice.15 = f32[3,384,384]{2,1,0:T(8,128)} dynamic-update-slice(f32[3,384,384]{2,1,0:T(8,128)} %get-tuple-element.644, f32[3,256,256]{2,1,0:T(8,128)S(1)} %get-tuple-element.577, s32[]{:T(128)} %constant.102.clone.1..sunk.1, s32[]{:T(128)S(6)} %select_n.126, s32[]{:T(128)S(6)} %select_n.127) | dynamic-update-slice | bytes 1572868 | tf_op jit(solution)/shard_map/while/body/dynamic_update_slice | solution.py:150
  170.7 1.8 maximum_add_fusion.7
  172.5 8.5 %dynamic_update_slice.15 = f32[3,384,384]{2,1,0:T(8,128)} dynamic-update-slice(f32[3,384,384]{2,1,0:T(8,128)} %get-tuple-element.644, f32[3,256,256]{2,1,0:T(8,128)S(1)} %get-tuple-element.577, s32[]{:T(128)} %constant.102.clone.1..sunk.1, s32[]{:T(128)S(6)} %select_n.126, s32[]{:T(128)S(6)} %select_n.127) | dynamic-update-slice | bytes 1572868 | tf_op jit(solution)/shard_map/while/body/dynamic_update_slice | solution.py:150
  189.4 1.8 maximum_add_fusion.7
  191.2 9.0 %dynamic_update_slice.15 = f32[3,384,384]{2,1,0:T(8,128)} dynamic-update-slice(f32[3,384,384]{2,1,0:T(8,128)} %get-tuple-element.644, f32[3,256,256]{2,1,0:T(8,128)S(1)} %get-tuple-element.577, s32[]{:T(128)} %constant.102.clone.1..sunk.1, s32[]{:T(128)S(6)} %select_n.126, s32[]{:T(128)S(6)} %select_n.127) | dynamic-update-slice | bytes 1572868 | tf_op jit(solution)/shard_map/while/body/dynamic_update_slice | solution.py:150
  208.6 1.8 maximum_add_fusion.7
  210.4 8.9 %dynamic_update_slice.15 = f32[3,384,384]{2,1,0:T(8,128)} dynamic-update-slice(f32[3,384,384]{2,1,0:T(8,128)} %get-tuple-element.644, f32[3,256,256]{2,1,0:T(8,128)S(1)} %get-tuple-element.577, s32[]{:T(128)} %constant.102.clone.1..sunk.1, s32[]{:T(128)S(6)} %select_n.126, s32[]{:T(128)S(6)} %select_n.127) | dynamic-update-slice | bytes 1572868 | tf_op jit(solution)/shard_map/while/body/dynamic_update_slice | solution.py:150
  219.9 1.4 slice.586
  222.7 4.1 %collective-permute-done.6 = bf16[3,128,384]{2,1,0:T(8,128)(2,1)S(1)} collective-permute-done((bf16[3,128,384]{2,1,0:T(8,128)(2,1)S(1)}, bf16[3,128,384]{2,1,0:T(8,128)(2,1)S(1)}, u32[]{:S(2)}, u32[]{:S(2)}) %collective-permute-start.6) | collective-permute-done | bytes 294944 | tf_op jit(solution)/shard_map/ppermute | solution.py:23
  226.8 1.3 convert_add_fusion
  229.5 54.7 %all-reduce.5.cloned.1.call-done = f32[3,256,256]{2,1,0:T(8,128)} async-done(((f32[3,256,256]{2,1,0:T(8,128)}), f32[3,256,256]{2,1,0:T(8,128)}) %all-reduce.5.cloned.1.call-update) | async-done | bytes 786448 | tf_op jit(solution)/shard_map/psum | solution.py:172
  288.8 40.6 %all-reduce.3.cloned.1.call-done = bf16[2,256,256]{2,1,0:T(8,128)(2,1)} async-done(((bf16[2,256,256]{2,1,0:T(8,128)(2,1)}), bf16[2,256,256]{2,1,0:T(8,128)(2,1)}) %all-reduce.3.cloned.1.call-update) | async-done | bytes 262160 | tf_op jit(solution)/shard_map/psum | solution.py:170
  330.5 2.0 subtract_bitcast_fusion
  (166 shorter events, 54.6 us)
Async XLA Ops:
  8.0 3.8 %copy-start.11 = (bf16[1,1,4,256,256]{4,3,2,1,0:T(8,128)(2,1)S(1)}, bf16[1,1,4,256,256]{4,3,2,1,0:T(8,128)(2,1)}, u32[]{:S(2)}) copy-start(bf16[1,1,4,256,256]{4,3,2,1,0:T(8,128)(2,1)} %param.13) | copy-start | bytes 1572868
  8.0 276.2 %all-reduce.5.cloned.1.call-start = ((), (), s32[]{:S(2)}) async-start(), calls=%async_computation.1 | async-start | bytes 1572864 | tf_op jit(solution)/shard_map/psum | solution.py:172
  9.2 5.0 %copy-start = (f32[1,2,256,256]{3,2,1,0:T(8,128)S(1)}, f32[1,2,256,256]{3,2,1,0:T(8,128)}, u32[]{:S(2)}) copy-start(f32[1,2,256,256]{3,2,1,0:T(8,128)} %param.12) | copy-start | bytes 1572868
  9.2 3.6 %collective-permute-start = (bf16[2,256,128]{2,1,0:T(8,128)(2,1)S(1)}, bf16[2,256,128]{2,1,0:T(8,128)(2,1)S(1)}, u32[]{:S(2)}, u32[]{:S(2)}) collective-permute-start(bf16[2,256,128]{2,1,0:T(8,128)(2,1)S(1)} %slice.386), channel_id=1, source_target_pairs={{4,0},{8,4},{12,8},{16,12},{20,16},{24,20},{28,24},{5,1},{9,5},{13... | collective-permute-start | bytes 393224 | tf_op jit(solution)/shard_map/ppermute | solution.py:23
  12.9 14.3 %collective-permute-start.1 = (bf16[2,128,384]{2,1,0:T(8,128)(2,1)S(1)}, bf16[2,128,384]{2,1,0:T(8,128)(2,1)S(1)}, u32[]{:S(2)}, u32[]{:S(2)}) collective-permute-start(bf16[2,128,384]{2,1,0:T(8,128)(2,1)S(1)} %pad_maximum_fusion.5), channel_id=1, source_target_pairs={{16,0},{20,4},{24,8},{28,12},{17,1},{21,5},{25,9},{29,13},{18,2},{... | collective-permute-start | bytes 589832 | tf_op jit(solution)/shard_map/ppermute | solution.py:23
  14.2 14.5 %copy-start.12 = (s32[1,1,4,2]{2,3,1,0:T(2,128)S(1)}, s32[1,1,4,2]{2,3,1,0:T(2,128)}, u32[]{:S(2)}) copy-start(s32[1,1,4,2]{2,3,1,0:T(2,128)} %param.14) | copy-start | bytes 100
  107.4 5.5 %collective-permute-start.2 = (bf16[3,128,384]{2,1,0:T(8,128)(2,1)S(1)}, bf16[3,128,384]{2,1,0:T(8,128)(2,1)S(1)}, u32[]{:S(2)}, u32[]{:S(2)}) collective-permute-start(bf16[3,128,384]{2,1,0:T(8,128)(2,1)S(1)} %slice.587), channel_id=1, source_target_pairs={{0,16},{4,20},{8,24},{12,28},{1,17},{5,21},{9,25},{13,29},{2,18},{... | collective-permute-start | bytes 884744 | tf_op jit(solution)/shard_map/ppermute | solution.py:23
  115.0 2.5 collective-permute-start.3
  117.6 1.2 copy-start.4
  117.6 1.5 copy-start.8
  117.7 5.4 %copy-start.2 = (f32[3,256,256]{2,1,0:T(8,128)}, f32[3,256,256]{2,1,0:T(8,128)S(1)}, u32[]{:S(2)}) copy-start(f32[3,256,256]{2,1,0:T(8,128)S(1)} %fusion.89) | copy-start | bytes 2359300
  119.1 0.7 copy-start.6
  119.8 3.2 collective-permute-start.4
  123.1 18.7 %collective-permute-start.5 = (bf16[2,128,384]{2,1,0:T(8,128)(2,1)S(1)}, bf16[2,128,384]{2,1,0:T(8,128)(2,1)S(1)}, u32[]{:S(2)}, u32[]{:S(2)}) collective-permute-start(bf16[2,128,384]{2,1,0:T(8,128)(2,1)S(1)} %pad_maximum_fusion.4), channel_id=1, source_target_pairs={{16,0},{20,4},{24,8},{28,12},{17,1},{21,5},{25,9},{29,13},{18,2},{... | collective-permute-start | bytes 589832 | tf_op jit(solution)/shard_map/ppermute | solution.py:23
  219.9 2.7 copy-start.1
  221.3 5.5 %collective-permute-start.6 = (bf16[3,128,384]{2,1,0:T(8,128)(2,1)S(1)}, bf16[3,128,384]{2,1,0:T(8,128)(2,1)S(1)}, u32[]{:S(2)}, u32[]{:S(2)}) collective-permute-start(bf16[3,128,384]{2,1,0:T(8,128)(2,1)S(1)} %slice.586), channel_id=1, source_target_pairs={{0,16},{4,20},{8,24},{12,28},{1,17},{5,21},{9,25},{13,29},{2,18},{... | collective-permute-start | bytes 884744 | tf_op jit(solution)/shard_map/ppermute | solution.py:23
  222.7 106.7 %all-reduce.3.cloned.1.call-start = ((), (), s32[]{:S(2)}) async-start(), calls=%async_computation | async-start | bytes 524288 | tf_op jit(solution)/shard_map/psum | solution.py:170
  228.2 57.0 %collective-permute-start.7 = (bf16[3,256,128]{2,1,0:T(8,128)(2,1)S(1)}, bf16[3,256,128]{2,1,0:T(8,128)(2,1)S(1)}, u32[]{:S(2)}, u32[]{:S(2)}) collective-permute-start(bf16[3,256,128]{2,1,0:T(8,128)(2,1)S(1)} %fusion.100), channel_id=1, source_target_pairs={{0,4},{4,8},{8,12},{12,16},{16,20},{20,24},{24,28},{1,5},{5,9},{9,... | collective-permute-start | bytes 589832 | tf_op jit(solution)/shard_map/ppermute | solution.py:23
  285.3 1.1 copy-start.3
  285.3 1.3 copy-start.5
  285.3 1.3 copy-start.7
  285.3 1.5 copy-start.9
  286.8 1.1 copy-start.10
Sparse Core Ops, SparseCore 0:
  222.8 61.3 all-reduce.4
Sparse Core Ops, SparseCore 1:
  287.9 41.5 all-reduce.2
where the time goes:
time: 343 us; the launch traced here: 340 us
  waiting for transfers between devices  137 us (40%)
  local copies, waits for them, and re-layouts  85.6 us (25%)
  other arithmetic  42.2 us (12%)
  loops' own time  38.4 us (11%)
  between operations  15.9 us (5%)
  starting transfers between devices  10.6 us (3%)
  matrix products  10 us (3%)
    dynamic_update_slice x8, local copies, waits for them, and re-layouts, visit_slot(): lax.dynamic_update_slice(local_totals, region + object_terms, (zero_index...  70.6 us
    psum x1, waiting for transfers between devices, shards(): probe_totals = lax.psum(probe_sum, 'tile')  54.7 us
    ppermute x8, waiting for transfers between devices, passed_along(): return lax.ppermute(value, axis, pairs)  41.9 us
    psum x1, waiting for transfers between devices, shards(): summed = lax.psum(combined.astype(jnp.bfloat16), 'scan').astype(jnp.float32)  40.6 us
    another operation x2, loops' own time, shards(): lax.fori_loop(0, slot_count, visit_slot, (start_totals, probe_sum))  38.4 us
    add x8, other arithmetic, visit_slot(): region + object_terms  14.3 us
    ppermute x8, starting transfers between devices, passed_along(): return lax.ppermute(value, axis, pairs)  10.5 us
    convert_element_type x8, other arithmetic, patch_terms(): resid_real = (wave_real * factor).astype(jnp.bfloat16)  8.32 us
  transfers between devices with their start and end apart: 10, of which 8 were waited for; matrix products, arithmetic and copies ran while one was open for 2% of the time, Pallas kernels for 0%

commit v1 on v0

v1 whole, which is shorter than its diff:
```python
import functools
import math

import jax
import jax.numpy as jnp
import ml_dtypes
import numpy as np
from jax import lax
from jax.experimental import pallas as pl
from jax.experimental.pallas import tpu as pltpu
from jax.sharding import PartitionSpec as P

PS = 256
TS = 256
OVER = 128
TGW = 4
SLOTS = 4
SPAN = TS + OVER
L = 128
CH = 32
META = 16

penalty = 0.5
smoothing = 0.05
probe_step = 3.0

f32 = jnp.float32
bf16 = jnp.bfloat16


def dft_tables():
    indices = np.arange(PS, dtype=np.int32)
    phase_index = indices[:, None] * indices[None, :] % PS
    angles = phase_index.astype(np.float32) * np.float32(2.0 * math.pi / PS)
    scale = np.float32(1.0 / math.sqrt(PS))
    re = (np.cos(angles) * scale).astype(ml_dtypes.bfloat16)
    im = (-np.sin(angles) * scale).astype(ml_dtypes.bfloat16)
    fwd = np.block([[re, -im], [im, re]])
    bwd = np.block([[re, im], [-im, re]])
    return jnp.asarray(fwd), jnp.asarray(bwd)


def shifted(value, rows, cols):
    n = lax.axis_size("tile")
    pairs = []
    for i in range(n):
        r, c = divmod(i, TGW)
        if 0 <= r + rows < n // TGW and 0 <= c + cols < TGW:
            pairs.append((i, i + rows * TGW + cols))
    return lax.ppermute(value, "tile", pairs)


def swapped(value, axis, bit):
    n = lax.axis_size(axis)
    return lax.ppermute(value, axis, [(i, i ^ bit) for i in range(n)])


def is_power(n):
    return n & (n - 1) == 0


def scan_sum(value):
    n = lax.axis_size("scan")
    if not is_power(n):
        return lax.psum(value, "scan").astype(f32)
    bits = [1 << k for k in range(n.bit_length() - 1)]
    half = value.shape[1] // 2
    parts = [value[:, :half], value[:, half:]]
    for k in range(len(bits)):
        for p in range(2):
            bit = bits[(k + p) % len(bits)]
            held = parts[p].astype(bf16)
            parts[p] = held.astype(f32) + swapped(held, "scan", bit).astype(f32)
    return jnp.concatenate(parts, 1)


def probe_update(total):
    return probe_step * total[0:2] / jnp.sqrt(total[2] + 1.0)


def probe_change(sums):
    n = lax.axis_size("tile")
    if not is_power(n) or n > PS // 16:
        return probe_update(lax.psum(sums, "tile"))
    index = lax.axis_index("tile")
    bits = [1 << k for k in range(n.bit_length() - 1)]
    for bit in bits:
        upper = (index // bit) % 2
        halves = sums.reshape(3, 2, sums.shape[1] // 2, PS)
        keep = lax.dynamic_index_in_dim(halves, upper, 1, keepdims=False)
        send = lax.dynamic_index_in_dim(halves, 1 - upper, 1, keepdims=False)
        sums = keep + swapped(send.astype(bf16), "tile", bit).astype(f32)
    change = probe_update(sums).astype(bf16)
    for bit in bits[::-1]:
        upper = (index // bit) % 2
        other = swapped(change, "tile", bit)
        change = jnp.where(
            upper == 1,
            jnp.concatenate([other, change], 1),
            jnp.concatenate([change, other], 1),
        )
    return change.astype(f32)


def lane_pull(blocks, c):
    lane = lax.broadcasted_iota(jnp.int32, blocks[0].shape, 1)
    keep = lane < L - c
    r = [pltpu.roll(v, (L - c) % L, 1) for v in blocks]
    return jnp.concatenate([jnp.where(keep, r[0], r[1]), jnp.where(keep, r[1], r[2])], 1)


def lane_push(blocks, c):
    lane = lax.broadcasted_iota(jnp.int32, blocks[0].shape, 1)
    past = lane >= c
    r = [pltpu.roll(v, c % L, 1) for v in blocks]
    z = jnp.zeros_like(r[0])
    return [jnp.where(past, r[0], z), jnp.where(past, r[1], r[0]), jnp.where(past, z, r[1])]


def visit_slot(s, r, c, ext, probe, amps, fwd, bwd, acc, pnum, win, X, Y, W):
    N = PS
    for k in range(0, N, CH):
        rows = slice(k, k + CH)
        w = [lane_pull([ext[ch, j, pl.ds(r + k, CH), :] for j in range(3)], c) for ch in range(2)]
        pr, pi = probe[0, rows, :], probe[1, rows, :]
        win[0, rows, :] = w[0]
        win[1, rows, :] = w[1]
        X[rows, :] = (pr * w[0] - pi * w[1]).astype(bf16)
        X[N + k : N + k + CH, :] = (pr * w[1] + pi * w[0]).astype(bf16)
        pnum[2, rows, :] += w[0] * w[0] + w[1] * w[1]
    t = jnp.dot(fwd[...], X[...], preferred_element_type=f32)
    Y[:, :N] = t[:N].astype(bf16)
    Y[:, N:] = t[N:].astype(bf16)
    W[...] = jnp.dot(Y[...], bwd[...], preferred_element_type=f32)
    for k in range(0, N, CH):
        wr, wi = W[k : k + CH, :N], W[k : k + CH, N:]
        f = amps[s, k : k + CH, :].astype(f32) * lax.rsqrt(wr * wr + wi * wi + smoothing) - 1.0
        X[k : k + CH, :] = (wr * f).astype(bf16)
        X[N + k : N + k + CH, :] = (wi * f).astype(bf16)
    t = jnp.dot(bwd[...], X[...], preferred_element_type=f32)
    Y[:, :N] = t[:N].astype(bf16)
    Y[:, N:] = t[N:].astype(bf16)
    W[...] = jnp.dot(Y[...], fwd[...], preferred_element_type=f32)
    for k in range(0, N, CH):
        rows = slice(k, k + CH)
        br, bi = W[rows, :N], W[rows, N:]
        pr, pi = probe[0, rows, :], probe[1, rows, :]
        wr, wi = win[0, rows, :], win[1, rows, :]
        pnum[0, rows, :] += wr * br + wi * bi
        pnum[1, rows, :] += wr * bi - wi * br
        for ch, v in enumerate((pr * br + pi * bi, pr * bi - pi * br)):
            for j, u in enumerate(lane_push([v[:, :L], v[:, L:]], c)):
                acc[ch, j, pl.ds(r + k, CH), :] += u


def first_pass(
    meta, own, dual, right, below, diag, probe, amps, fwd, bwd,
    acc, pnum, to_right, to_left, ext, win, X, Y, W,
):
    for j in range(2):
        cols = slice(j * L, (j + 1) * L)
        ext[:, j, :TS, :] = own[:, :, cols].astype(bf16).astype(f32)
        ext[:, j, TS:, :] = below[:, :, cols].astype(f32)
        acc[:, j, :TS, :] = -penalty * dual[:, :, cols]
        acc[:, j, TS:, :] = jnp.zeros((2, OVER, L), f32)
    ext[:, 2, :TS, :] = right[...].astype(f32)
    ext[:, 2, TS:, :] = diag[...].astype(f32)
    acc[:, 2] = jnp.zeros((2, SPAN, L), f32)
    pnum[...] = jnp.zeros_like(pnum)

    @pl.loop(0, meta[2 * SLOTS])
    def _(s):
        visit_slot(
            s, meta[2 * s], meta[2 * s + 1], ext, probe, amps, fwd, bwd, acc, pnum, win, X, Y, W
        )

    to_right[...] = acc[:, 2].astype(bf16)
    to_left[...] = acc[:, 0].astype(bf16)


def between(acc, from_left, from_right, to_below, to_above):
    for rows, out in ((slice(TS, SPAN), to_below), (slice(0, OVER), to_above)):
        out[:, 0] = (acc[:, 0, rows, :] + from_left[:, rows, :].astype(f32)).astype(bf16)
        out[:, 1] = acc[:, 1, rows, :].astype(bf16)
        out[:, 2] = (acc[:, 2, rows, :] + from_right[:, rows, :].astype(f32)).astype(bf16)


def weigh(metas, probe, weight, p2, buf):
    buf[...] = jnp.zeros_like(buf)
    for j in range(2):
        cols = slice(j * L, (j + 1) * L)
        p2[j] = probe[0, :, cols] * probe[0, :, cols] + probe[1, :, cols] * probe[1, :, cols]
    for dr in (-1, 0, 1):
        for dc in (-1, 0, 1):
            place = (dr + 1) * 3 + dc + 1
            first, rows = {-1: (OVER, OVER), 0: (0, PS), 1: (0, OVER)}[dr]
            base = {-1: 0, 0: OVER, 1: OVER + TS}[dr]

            @pl.loop(0, metas[place, 2 * SLOTS])
            def _(s, place=place, dc=dc, first=first, rows=rows, base=base):
                r, c = metas[place, 2 * s], metas[place, 2 * s + 1]
                for k in range(0, rows, 64):
                    at = pl.ds(base + r + k, 64)
                    v = [p2[j, first + k : first + k + 64, :] for j in range(2)]
                    lane = lax.broadcasted_iota(jnp.int32, v[0].shape, 1)
                    if dc == 0:
                        for j, u in enumerate(lane_push(v, c)):
                            buf[j, at, :] += u
                    elif dc < 0:
                        buf[0, at, :] += jnp.where(lane < c, pltpu.roll(v[1], c % L, 1), 0.0)
                    else:
                        buf[2, at, :] += jnp.where(lane >= c, pltpu.roll(v[0], c % L, 1), 0.0)

    weight[...] = buf[:, OVER : OVER + SPAN, :]


def second_pass(
    meta, own, dual, right, below, diag, acc1, from_left, from_right, from_above, from_below,
    weight, pnum1, probe, amps, fwd, bwd,
    partial, to_right, to_below, to_diag, pnum, ext, acc, win, X, Y, W,
):
    has_right = meta[2 * SLOTS + 1].astype(f32)
    has_below = meta[2 * SLOTS + 2].astype(f32)
    for ch in range(2):
        for j in range(3):
            cols = slice(j * L, (j + 1) * L)
            for k in range(0, SPAN, 64):
                rows = slice(k, k + 64)
                total = acc1[ch, j, rows, :]
                if j == 0:
                    total = total + from_left[ch, rows, :].astype(f32)
                if j == 2:
                    total = total + from_right[ch, rows, :].astype(f32)
                if k < OVER:
                    total = total + from_above[ch, j, rows, :].astype(f32)
                if k >= TS:
                    total = total + from_below[ch, j, k - TS : k - TS + 64, :].astype(f32)
                step = total / (weight[j, rows, :] + penalty)
                if j < 2 and k < TS:
                    est = own[ch, rows, cols] + step
                    partial[ch, rows, cols] = est
                else:
                    if k < TS:
                        est = right[ch, rows, :].astype(f32) + step
                    elif j < 2:
                        est = below[ch, k - TS : k - TS + 64, cols].astype(f32) + step
                    else:
                        est = diag[ch, k - TS : k - TS + 64, :].astype(f32) + step
                    if j == 2:
                        est = est * has_right
                    if k >= TS:
                        est = est * has_below
                ext[ch, j, rows, :] = est.astype(bf16).astype(f32)
    acc[...] = jnp.zeros_like(acc)
    pnum[...] = pnum1[...]

    @pl.loop(0, meta[2 * SLOTS])
    def _(s):
        visit_slot(
            s, meta[2 * s], meta[2 * s + 1], ext, probe, amps, fwd, bwd, acc, pnum, win, X, Y, W
        )

    for j in range(2):
        cols = slice(j * L, (j + 1) * L)
        to_below[:, :, cols] = acc[:, j, TS:, :].astype(bf16)
        for ch in range(2):
            for k in range(0, TS, 64):
                rows = slice(k, k + 64)
                est = partial[ch, rows, cols]
                pull = penalty * (own[ch, rows, cols] - dual[ch, rows, cols] - est)
                partial[ch, rows, cols] = est + (acc[ch, j, rows, :] + pull) / (
                    weight[j, rows, :] + penalty
                )
    to_right[...] = acc[:, 2, :TS, :].astype(bf16)
    to_diag[...] = acc[:, 2, TS:, :].astype(bf16)


def finish_estimate(partial, dual, weight, from_left, from_above, from_diag, combined, rounded):
    for ch in range(2):
        for j in range(2):
            cols = slice(j * L, (j + 1) * L)
            for k in range(0, TS, 64):
                rows = slice(k, k + 64)
                total = partial[ch, rows, cols] + dual[ch, rows, cols]
                came = None
                if j == 0:
                    came = from_left[ch, rows, :].astype(f32)
                if k < OVER:
                    above = from_above[ch, rows, cols].astype(f32)
                    came = above if came is None else came + above
                    if j == 0:
                        came = came + from_diag[ch, rows, :].astype(f32)
                if came is not None:
                    total = total + came / (weight[j, rows, :] + penalty)
                combined[ch, rows, cols] = total
                rounded[ch, rows, cols] = total.astype(bf16)


def settle(groups, summed, combined, settled, dual_new):
    for k in range(0, TS, CH):
        rows = slice(k, k + CH)
        re = summed[0, rows, :] * (1.0 / groups)
        im = summed[1, rows, :] * (1.0 / groups)
        over = 1.0 / jnp.maximum(jnp.sqrt(re * re + im * im), 1.0)
        re, im = re * over, im * over
        settled[0, rows, :] = re
        settled[1, rows, :] = im
        dual_new[0, rows, :] = combined[0, rows, :] - re
        dual_new[1, rows, :] = combined[1, rows, :] - im


V = pl.BlockSpec(memory_space=pltpu.VMEM)
S = pl.BlockSpec(memory_space=pltpu.SMEM)


def call(body, name, outs, scratch=(), scalars=0):
    def run(*operands):
        return pl.pallas_call(
            body,
            in_specs=[S] * scalars + [V] * (len(operands) - scalars),
            out_specs=[V] * len(outs),
            out_shape=[jax.ShapeDtypeStruct(shape, dtype) for shape, dtype in outs],
            scratch_shapes=[pltpu.VMEM(shape, dtype) for shape, dtype in scratch],
            compiler_params=pltpu.CompilerParams(vmem_limit_bytes=24 * 2**20),
            name=name,
        )(*operands)

    return run


WORK = [
    ((2, PS, PS), f32),
    ((2 * PS, PS), bf16),
    ((PS, 2 * PS), bf16),
    ((PS, 2 * PS), f32),
]
WIDE = ((2, 3, SPAN, L), f32)


def shards(consensus, duals, probes, amplitudes, offsets, counts):
    fwd, bwd = dft_tables()
    n = lax.axis_size("tile")
    index = lax.axis_index("tile")
    own = consensus[0]
    dual = duals[0, 0]
    probe = probes[0]
    amps = amplitudes[0, 0]

    rounded = own.astype(bf16)
    right = shifted(rounded[:, :, :OVER], 0, -1)
    below = shifted(rounded[:, :OVER, :], -1, 0)
    diag = shifted(rounded[:, :OVER, :OVER], -1, -1)

    edges = jnp.stack([index % TGW < TGW - 1, index // TGW < n // TGW - 1]).astype(jnp.int32)
    meta = jnp.concatenate(
        [
            offsets[0, 0].reshape(2 * SLOTS),
            counts[0],
            edges,
            jnp.zeros((META - 2 * SLOTS - 3,), jnp.int32),
        ]
    )
    beside = jnp.stack([shifted(meta, 0, 1), meta, shifted(meta, 0, -1)])
    metas = jnp.concatenate([shifted(beside, 1, 0), beside, shifted(beside, -1, 0)])
    (weight,) = call(
        weigh, "weigh", [((3, SPAN, L), f32)],
        [((2, PS, L), f32), ((3, SPAN + 2 * OVER, L), f32)], 1,
    )(metas, probe)

    acc, pnum, to_right, to_left = call(
        first_pass, "first_pass",
        [WIDE, ((3, PS, PS), f32), ((2, SPAN, L), bf16), ((2, SPAN, L), bf16)],
        [WIDE] + WORK, 1,
    )(meta, own, dual, right, below, diag, probe, amps, fwd, bwd)
    from_left = shifted(to_right, 0, 1)
    from_right = shifted(to_left, 0, -1)
    to_below, to_above = call(
        between, "between", [((2, 3, OVER, L), bf16)] * 2
    )(acc, from_left, from_right)
    from_above = shifted(to_below, 1, 0)
    from_below = shifted(to_above, -1, 0)

    partial, to_right, to_below, to_diag, pnum = call(
        second_pass, "second_pass",
        [((2, TS, TS), f32), ((2, TS, OVER), bf16), ((2, OVER, TS), bf16), ((2, OVER, OVER), bf16),
         ((3, PS, PS), f32)],
        [WIDE, WIDE] + WORK, 1,
    )(meta, own, dual, right, below, diag, acc, from_left, from_right, from_above, from_below,
      weight, pnum, probe, amps, fwd, bwd)
    from_left = shifted(to_right, 0, 1)
    from_above = shifted(to_below, 1, 0)
    from_diag = shifted(to_diag, 1, 1)
    combined, rounded = call(
        finish_estimate, "finish_estimate", [((2, TS, TS), f32), ((2, TS, TS), bf16)]
    )(partial, dual, weight, from_left, from_above, from_diag)
    summed = scan_sum(rounded)
    settled, dual_new = call(
        functools.partial(settle, lax.axis_size("scan")), "settle", [((2, TS, TS), f32)] * 2
    )(summed, combined)
    probe_new = probe + probe_change(pnum)
    return (settled[None], dual_new[None, None], probe_new[None])


def solution(mesh):
    placed = (
        P("tile", None, None, None),
        P("scan", "tile", None, None, None),
        P("scan", None, None, None),
        P("scan", "tile", None, None, None),
        P("scan", "tile", None, None),
        P("scan", "tile"),
    )
    return jax.shard_map(
        shards,
        mesh=mesh,
        in_specs=placed,
        out_specs=(
            P("tile", None, None, None),
            P("scan", "tile", None, None, None),
            P("scan", None, None, None),
        ),
        check_vma=False,
    )
```

time: 343 us -> 111 us (0.32)
  waiting for transfers between devices: 137 us -> 28.8 us
  local copies, waits for them, and re-layouts: 85.6 us -> 13.1 us
  loops' own time: 38.4 us -> 0 us
  other arithmetic: 42.2 us -> 4.37 us
  starting transfers between devices: 10.6 us -> 41.3 us
  Pallas kernels: 0 us -> 21.1 us
  between operations: 15.9 us -> 2.01 us
  matrix products: 10 us -> 0 us
    psum x2 -> x0, waiting for transfers between devices: 95.2 us -> none  [the longest x1 54.7 us: shards(): probe_totals = lax.psum(probe_sum, 'tile')]
    dynamic_update_slice x8 -> x0, local copies, waits for them, and re-layouts: 70.6 us -> none  [visit_slot(): lax.dynamic_update_slice(local_totals, region + object_terms, (zero_index...]
    another operation x2 -> x0, loops' own time: 38.4 us -> none  [shards(): lax.fori_loop(0, slot_count, visit_slot, (start_totals, probe_sum))]
    ppermute x8 -> x24, starting transfers between devices: 10.5 us -> 41.3 us  [the longest x14 35.3 us: shifted(): return lax.ppermute(value, 'tile', pairs)]
    pallas_call x0 -> x6, Pallas kernels: none -> 21.1 us  [run(): pl.pallas_call(body, in_specs=[S] * scalars + [V] * (len(operands) - scal...]
    add x21 -> x6, other arithmetic: 18.6 us -> 2.88 us  [the longest x3 1.97 us: probe_change(): sums = keep + swapped(send.astype(bf16), 'tile', bit).astype(f32)]
    ppermute x8 -> x24, waiting for transfers between devices: 41.9 us -> 28.8 us  [the longest x14 20.1 us: shifted(): return lax.ppermute(value, 'tile', pairs)]
    convert_element_type x36 -> x4, other arithmetic: 14.1 us -> 1.31 us  [the longest x1 1.15 us: shards(): rounded = own.astype(bf16)]
  transfers between devices with their start and end apart: 10 -> 24, of which waited for: 8 -> 12; matrix products, arithmetic and copies ran while one was open for 2% -> 2% of each run, Pallas kernels for 0% -> 3%
where the time goes in v1:
time: 111 us
  starting transfers between devices  41.3 us (37%)
  waiting for transfers between devices  28.8 us (26%)
  Pallas kernels  21.1 us (19%)
  local copies, waits for them, and re-layouts  13.1 us (12%)
  other arithmetic  4.37 us (4%)
  between operations  2.01 us (2%)
    ppermute x14, starting transfers between devices, shifted(): return lax.ppermute(value, 'tile', pairs)  35.3 us
    pallas_call x6, Pallas kernels, run(): pl.pallas_call(body, in_specs=[S] * scalars + [V] * (len(operands) - scal...  21.1 us
    ppermute x14, waiting for transfers between devices, shifted(): return lax.ppermute(value, 'tile', pairs)  20.1 us
    unnamed x57, local copies, waits for them, and re-layouts  12.8 us
    ppermute x10, waiting for transfers between devices, swapped(): return lax.ppermute(value, axis, [(i, i ^ bit) for i in range(n)])  8.78 us
    ppermute x10, starting transfers between devices, swapped(): return lax.ppermute(value, axis, [(i, i ^ bit) for i in range(n)])  5.96 us
  transfers between devices with their start and end apart: 24, of which 12 were waited for; matrix products, arithmetic and copies ran while one was open for 2% of the time, Pallas kernels for 3%

profile of v1, /device:TPU:0, one launch (start us, length us, event | category | flops | bytes accessed | tf_op | source)
XLA Modules:
  0.0 110.7 jit_solution(14654636175488624989)
XLA Ops:
  0.7 1.2 %bitcast_convert_fusion.1 = bf16[2,256,256]{2,1,0:T(8,128)(2,1)S(1)} fusion(f32[1,2,256,256]{3,2,1,0:T(8,128)} %param.8), kind=kLoop, calls=%fused_computation.27 | loop fusion | flops 131072 | bytes 786432 | tf_op jit(solution)/shard_map/convert_element_type | solution.py:349
  1.8 1.3 %collective-permute-start = (bf16[2,256,128]{2,1,0:T(8,128)(2,1)S(1)}, bf16[2,256,128]{2,1,0:T(8,128)(2,1)S(1)}, u32[]{:S(2)}, u32[]{:S(2)}) collective-permute-start(bf16[2,256,128]{2,1,0:T(8,128)(2,1)S(1)} %slice.28), channel_id=1, source_target_pairs={{4,0},{8,4},{12,8},{20,16},{24,20},{28,24},{5,1},{9,5},{13,9},{21,... | collective-permute-start | bytes 393224 | tf_op jit(solution)/shard_map/ppermute | solution.py:50
  3.2 1.3 %collective-permute-start.1 = (bf16[2,128,256]{2,1,0:T(8,128)(2,1)S(1)}, bf16[2,128,256]{2,1,0:T(8,128)(2,1)S(1)}, u32[]{:S(2)}, u32[]{:S(2)}) collective-permute-start(bf16[2,128,256]{2,1,0:T(8,128)(2,1)S(1)} %slice.29), channel_id=1, source_target_pairs={{16,0},{20,4},{24,8},{28,12},{17,1},{21,5},{25,9},{29,13},{18,2},{... | collective-permute-start | bytes 393224 | tf_op jit(solution)/shard_map/ppermute | solution.py:50
  4.5 1.3 %collective-permute-start.2 = (bf16[2,128,128]{2,1,0:T(8,128)(2,1)S(1)}, bf16[2,128,128]{2,1,0:T(8,128)(2,1)S(1)}, u32[]{:S(2)}, u32[]{:S(2)}) collective-permute-start(bf16[2,128,128]{2,1,0:T(8,128)(2,1)S(1)} %slice.30), channel_id=1, source_target_pairs={{20,0},{24,4},{28,8},{21,1},{25,5},{29,9},{22,2},{26,6},{30,10},{2... | collective-permute-start | bytes 196616 | tf_op jit(solution)/shard_map/ppermute | solution.py:50
  6.8 10.9 %collective-permute-done.2.diag = bf16[2,128,128]{2,1,0:T(8,128)(2,1)S(1)} collective-permute-done((bf16[2,128,128]{2,1,0:T(8,128)(2,1)S(1)}, bf16[2,128,128]{2,1,0:T(8,128)(2,1)S(1)}, u32[]{:S(2)}, u32[]{:S(2)}) %collective-permute-start.2) | collective-permute-done | bytes 65568 | tf_op jit(solution)/shard_map/ppermute | solution.py:50
  17.8 1.1 %copy-done.2 = f32[1,1,2,256,256]{4,3,2,1,0:T(8,128)S(1)} copy-done((f32[1,1,2,256,256]{4,3,2,1,0:T(8,128)S(1)}, f32[1,1,2,256,256]{4,3,2,1,0:T(8,128)}, u32[]{:S(2)}) %copy-start.2) | copy-done | bytes 524312
  21.0 1.0 copy-done.8
  22.0 8.1 %first_pass.1 = (f32[2,3,384,128]{3,2,1,0:T(8,128)S(1)}, f32[3,256,256]{2,1,0:T(8,128)S(1)}, bf16[2,384,128]{2,1,0:T(8,128)(2,1)S(1)}, bf16[2,384,128]{2,1,0:T(8,128)(2,1)S(1)}) custom-call(s32[16]{0:T(128)S(1)} %pad_add_fusion.1.meta, f32[2,256,256]{2,1,0:T(8,128)S(1)} %bitcast.40, f32[2,256,256]{2,1,0:T(8,128)S(1)} %bitcast.42, ...), custom_call_target="tpu_custom_call" | custom-call | tf_op jit(solution)/shard_map/first_pass/pallas_call | solution.py:318
  31.1 1.3 %collective-permute-start.3 = (bf16[2,384,128]{2,1,0:T(8,128)(2,1)S(1)}, bf16[2,384,128]{2,1,0:T(8,128)(2,1)S(1)}, u32[]{:S(2)}, u32[]{:S(2)}) collective-permute-start(bf16[2,384,128]{2,1,0:T(8,128)(2,1)S(1)} %get-tuple-element.19), channel_id=1, source_target_pairs={{0,4},{4,8},{8,12},{16,20},{20,24},{24,28},{1,5},{5,9},{9,13},{17,... | collective-permute-start | bytes 589832 | tf_op jit(solution)/shard_map/ppermute | solution.py:50
  32.4 1.3 %collective-permute-start.4 = (bf16[2,384,128]{2,1,0:T(8,128)(2,1)S(1)}, bf16[2,384,128]{2,1,0:T(8,128)(2,1)S(1)}, u32[]{:S(2)}, u32[]{:S(2)}) collective-permute-start(bf16[2,384,128]{2,1,0:T(8,128)(2,1)S(1)} %get-tuple-element.20), channel_id=1, source_target_pairs={{4,0},{8,4},{12,8},{20,16},{24,20},{28,24},{5,1},{9,5},{13,9},{21,... | collective-permute-start | bytes 589832 | tf_op jit(solution)/shard_map/ppermute | solution.py:50
  33.7 2.0 %collective-permute-done.4.from_right = bf16[2,384,128]{2,1,0:T(8,128)(2,1)S(1)} collective-permute-done((bf16[2,384,128]{2,1,0:T(8,128)(2,1)S(1)}, bf16[2,384,128]{2,1,0:T(8,128)(2,1)S(1)}, u32[]{:S(2)}, u32[]{:S(2)}) %collective-permute-start.4) | collective-permute-done | bytes 196640 | tf_op jit(solution)/shard_map/ppermute | solution.py:50
  36.5 2.9 %collective-permute-start.5 = (bf16[2,3,128,128]{3,2,1,0:T(8,128)(2,1)}, bf16[2,3,128,128]{3,2,1,0:T(8,128)(2,1)}, u32[]{:S(2)}, u32[]{:S(2)}) collective-permute-start(bf16[2,3,128,128]{3,2,1,0:T(8,128)(2,1)} %get-tuple-element.21), channel_id=1, source_target_pairs={{0,16},{4,20},{8,24},{12,28},{1,17},{5,21},{9,25},{13,29},{2,18},{... | collective-permute-start | bytes 589832 | tf_op jit(solution)/shard_map/ppermute | solution.py:50
  39.4 1.3 %collective-permute-start.6 = (bf16[2,3,128,128]{3,2,1,0:T(8,128)(2,1)}, bf16[2,3,128,128]{3,2,1,0:T(8,128)(2,1)}, u32[]{:S(2)}, u32[]{:S(2)}) collective-permute-start(bf16[2,3,128,128]{3,2,1,0:T(8,128)(2,1)} %get-tuple-element.22), channel_id=1, source_target_pairs={{16,0},{20,4},{24,8},{28,12},{17,1},{21,5},{25,9},{29,13},{18,2},{... | collective-permute-start | bytes 589832 | tf_op jit(solution)/shard_map/ppermute | solution.py:50
  40.7 6.8 %collective-permute-start.7 = (s32[16]{0:T(128)S(1)}, s32[16]{0:T(128)S(1)}, u32[]{:S(2)}, u32[]{:S(2)}) collective-permute-start(s32[16]{0:T(128)S(1)} %pad_add_fusion.1.meta), channel_id=1, source_target_pairs={{0,4},{4,8},{8,12},{16,20},{20,24},{24,28},{1,5},{5,9},{9,13},{17,... | collective-permute-start | bytes 200 | tf_op jit(solution)/shard_map/ppermute | solution.py:50
  47.4 1.3 %collective-permute-start.8 = (s32[16]{0:T(128)S(1)}, s32[16]{0:T(128)S(1)}, u32[]{:S(2)}, u32[]{:S(2)}) collective-permute-start(s32[16]{0:T(128)S(1)} %pad_add_fusion.1.meta), channel_id=1, source_target_pairs={{4,0},{8,4},{12,8},{20,16},{24,20},{28,24},{5,1},{9,5},{13,9},{21,... | collective-permute-start | bytes 200 | tf_op jit(solution)/shard_map/ppermute | solution.py:50
  48.8 1.7 %collective-permute-done.8 = s32[16]{0:T(128)S(1)} collective-permute-done((s32[16]{0:T(128)S(1)}, s32[16]{0:T(128)S(1)}, u32[]{:S(2)}, u32[]{:S(2)}) %collective-permute-start.8) | collective-permute-done | bytes 96 | tf_op jit(solution)/shard_map/ppermute | solution.py:50
  50.5 1.3 %collective-permute-start.10 = (s32[3,16]{1,0:T(4,128)S(1)}, s32[3,16]{1,0:T(4,128)S(1)}, u32[]{:S(2)}, u32[]{:S(2)}) collective-permute-start(s32[3,16]{1,0:T(4,128)S(1)} %pad_add_fusion), channel_id=1, source_target_pairs={{16,0},{20,4},{24,8},{28,12},{17,1},{21,5},{25,9},{29,13},{18,2},{... | collective-permute-start | bytes 584 | tf_op jit(solution)/shard_map/ppermute | solution.py:50
  51.8 5.8 %collective-permute-start.9 = (s32[3,16]{1,0:T(4,128)S(1)}, s32[3,16]{1,0:T(4,128)S(1)}, u32[]{:S(2)}, u32[]{:S(2)}) collective-permute-start(s32[3,16]{1,0:T(4,128)S(1)} %pad_add_fusion), channel_id=1, source_target_pairs={{0,16},{4,20},{8,24},{12,28},{1,17},{5,21},{9,25},{13,29},{2,18},{... | collective-permute-start | bytes 584 | tf_op jit(solution)/shard_map/ppermute | solution.py:50
  57.6 1.3 %collective-permute-done.9 = s32[3,16]{1,0:T(4,128)S(1)} collective-permute-done((s32[3,16]{1,0:T(4,128)S(1)}, s32[3,16]{1,0:T(4,128)S(1)}, u32[]{:S(2)}, u32[]{:S(2)}) %collective-permute-start.9) | collective-permute-done | bytes 224 | tf_op jit(solution)/shard_map/ppermute | solution.py:50
  59.0 2.0 %weigh.1.weight = f32[3,384,128]{2,1,0:T(8,128)S(1)} custom-call(s32[9,16]{1,0:T(8,128)S(1)} %concatenate.65.metas, f32[2,256,256]{2,1,0:T(8,128)S(1)} %bitcast.38), custom_call_target="tpu_custom_call" | custom-call | tf_op jit(solution)/shard_map/weigh/pallas_call | solution.py:318
  62.1 1.0 copy-done.7
  66.8 9.0 %second_pass.1 = (f32[2,256,256]{2,1,0:T(8,128)S(1)}, bf16[2,256,128]{2,1,0:T(8,128)(2,1)S(1)}, bf16[2,128,256]{2,1,0:T(8,128)(2,1)S(1)}, bf16[2,128,128]{2,1,0:T(8,128)(2,1)S(1)}, f32[3,256,256]{2,1,0:T(8,128)S(1)}) custom-call(s32[16]{0:T(128)S(1)} %pad_add_fusion.1.meta, f32[2,256,256]{2,1,0:T(8,128)S(1)} %bitcast.41, f32[2,256,256]{2,1,0:T(8,128)S(1)} %bitcast.43, ...), custom_call_target="tpu_custom_call" | custom-call | tf_op jit(solution)/shard_map/second_pass/pallas_call | solution.py:318
  77.7 2.5 %collective-permute-start.11 = (bf16[2,256,128]{2,1,0:T(8,128)(2,1)}, bf16[2,256,128]{2,1,0:T(8,128)(2,1)S(1)}, u32[]{:S(2)}, u32[]{:S(2)}) collective-permute-start(bf16[2,256,128]{2,1,0:T(8,128)(2,1)} %copy-done.24), channel_id=1, source_target_pairs={{0,4},{4,8},{8,12},{16,20},{20,24},{24,28},{1,5},{5,9},{9,13},{17,... | collective-permute-start | bytes 393224 | tf_op jit(solution)/shard_map/ppermute | solution.py:50
  80.2 5.8 %collective-permute-start.12 = (bf16[2,128,256]{2,1,0:T(8,128)(2,1)}, bf16[2,128,256]{2,1,0:T(8,128)(2,1)S(1)}, u32[]{:S(2)}, u32[]{:S(2)}) collective-permute-start(bf16[2,128,256]{2,1,0:T(8,128)(2,1)} %copy-done.23), channel_id=1, source_target_pairs={{0,16},{4,20},{8,24},{12,28},{1,17},{5,21},{9,25},{13,29},{2,18},{... | collective-permute-start | bytes 393224 | tf_op jit(solution)/shard_map/ppermute | solution.py:50
  87.2 1.3 %collective-permute-start.13 = (bf16[2,128,128]{2,1,0:T(8,128)(2,1)S(1)}, bf16[2,128,128]{2,1,0:T(8,128)(2,1)S(1)}, u32[]{:S(2)}, u32[]{:S(2)}) collective-permute-start(bf16[2,128,128]{2,1,0:T(8,128)(2,1)S(1)} %copy-done.26), channel_id=1, source_target_pairs={{0,20},{4,24},{8,28},{1,21},{5,25},{9,29},{2,22},{6,26},{10,30},{3... | collective-permute-start | bytes 196616 | tf_op jit(solution)/shard_map/ppermute | solution.py:50
  88.5 4.1 %collective-permute-done.13.from_diag = bf16[2,128,128]{2,1,0:T(8,128)(2,1)S(1)} collective-permute-done((bf16[2,128,128]{2,1,0:T(8,128)(2,1)S(1)}, bf16[2,128,128]{2,1,0:T(8,128)(2,1)S(1)}, u32[]{:S(2)}, u32[]{:S(2)}) %collective-permute-start.13) | collective-permute-done | bytes 65568 | tf_op jit(solution)/shard_map/ppermute | solution.py:50
  95.0 4.1 %collective-permute-done.20 = bf16[3,32,256]{2,1,0:T(8,128)(2,1)S(1)} collective-permute-done((bf16[3,32,256]{2,1,0:T(8,128)(2,1)S(1)}, bf16[3,32,256]{2,1,0:T(8,128)(2,1)S(1)}, u32[]{:S(2)}, u32[]{:S(2)}) %collective-permute-start.20) | collective-permute-done | bytes 49184 | tf_op jit(solution)/shard_map/ppermute | solution.py:55
  100.2 2.3 %collective-permute-start.17 = (bf16[2,128,256]{2,1,0:T(8,128)(2,1)S(1)}, bf16[2,128,256]{2,1,0:T(8,128)(2,1)S(1)}, u32[]{:S(2)}, u32[]{:S(2)}) collective-permute-start(bf16[2,128,256]{2,1,0:T(8,128)(2,1)S(1)} %get-tuple-element.34), channel_id=1, source_target_pairs={{0,1},{1,0},{2,3},{3,2},{4,5},{5,4},{6,7},{7,6},{8,9},{9,8},{10,11... | collective-permute-start | bytes 393224 | tf_op jit(solution)/shard_map/ppermute | solution.py:55
  102.5 1.5 %collective-permute-done.21 = bf16[2,32,256]{2,1,0:T(8,128)(2,1)S(1)} collective-permute-done((bf16[2,32,256]{2,1,0:T(8,128)(2,1)S(1)}, bf16[2,32,256]{2,1,0:T(8,128)(2,1)S(1)}, u32[]{:S(2)}, u32[]{:S(2)}) %collective-permute-start.21) | collective-permute-done | bytes 32800 | tf_op jit(solution)/shard_map/ppermute | solution.py:55
  104.1 1.5 %collective-permute-start.22 = (bf16[2,64,256]{2,1,0:T(8,128)(2,1)S(1)}, bf16[2,64,256]{2,1,0:T(8,128)(2,1)S(1)}, u32[]{:S(2)}, u32[]{:S(2)}) collective-permute-start(bf16[2,64,256]{2,1,0:T(8,128)(2,1)S(1)} %maximum_select_fusion.2), channel_id=1, source_target_pairs={{0,8},{4,12},{8,0},{12,4},{16,24},{20,28},{24,16},{28,20},{1,9},{5... | collective-permute-start | bytes 196616 | tf_op jit(solution)/shard_map/ppermute | solution.py:55
  106.5 1.9 %collective-permute-done.22 = bf16[2,64,256]{2,1,0:T(8,128)(2,1)S(1)} collective-permute-done((bf16[2,64,256]{2,1,0:T(8,128)(2,1)S(1)}, bf16[2,64,256]{2,1,0:T(8,128)(2,1)S(1)}, u32[]{:S(2)}, u32[]{:S(2)}) %collective-permute-start.22) | collective-permute-done | bytes 65568 | tf_op jit(solution)/shard_map/ppermute | solution.py:55
  108.6 1.1 %settle.1 = (f32[2,256,256]{2,1,0:T(8,128)}, f32[2,256,256]{2,1,0:T(8,128)}) custom-call(f32[2,256,256]{2,1,0:T(8,128)S(1)} %pad_maximum_fusion.summed, f32[2,256,256]{2,1,0:T(8,128)S(1)} %get-tuple-element.29.combined), custom_call_target="tpu_custom_call" | custom-call | tf_op jit(solution)/shard_map/settle/pallas_call | solution.py:318
  (105 shorter events, 17.5 us)
Async XLA Ops:
  0.6 17.1 %copy-start.1 = (f32[1,2,256,256]{3,2,1,0:T(8,128)S(1)}, f32[1,2,256,256]{3,2,1,0:T(8,128)}, u32[]{:S(2)}) copy-start(f32[1,2,256,256]{3,2,1,0:T(8,128)} %param.8) | copy-start | bytes 1572868
  0.7 17.1 %copy-start = (f32[1,2,256,256]{3,2,1,0:T(8,128)S(1)}, f32[1,2,256,256]{3,2,1,0:T(8,128)}, u32[]{:S(2)}) copy-start(f32[1,2,256,256]{3,2,1,0:T(8,128)} %param.10) | copy-start | bytes 1572868
  1.8 15.9 %collective-permute-start = (bf16[2,256,128]{2,1,0:T(8,128)(2,1)S(1)}, bf16[2,256,128]{2,1,0:T(8,128)(2,1)S(1)}, u32[]{:S(2)}, u32[]{:S(2)}) collective-permute-start(bf16[2,256,128]{2,1,0:T(8,128)(2,1)S(1)} %slice.28), channel_id=1, source_target_pairs={{4,0},{8,4},{12,8},{20,16},{24,20},{28,24},{5,1},{9,5},{13,9},{21,... | collective-permute-start | bytes 393224 | tf_op jit(solution)/shard_map/ppermute | solution.py:50
  3.2 14.6 %collective-permute-start.1 = (bf16[2,128,256]{2,1,0:T(8,128)(2,1)S(1)}, bf16[2,128,256]{2,1,0:T(8,128)(2,1)S(1)}, u32[]{:S(2)}, u32[]{:S(2)}) collective-permute-start(bf16[2,128,256]{2,1,0:T(8,128)(2,1)S(1)} %slice.29), channel_id=1, source_target_pairs={{16,0},{20,4},{24,8},{28,12},{17,1},{21,5},{25,9},{29,13},{18,2},{... | collective-permute-start | bytes 393224 | tf_op jit(solution)/shard_map/ppermute | solution.py:50
  4.5 13.3 %collective-permute-start.2 = (bf16[2,128,128]{2,1,0:T(8,128)(2,1)S(1)}, bf16[2,128,128]{2,1,0:T(8,128)(2,1)S(1)}, u32[]{:S(2)}, u32[]{:S(2)}) collective-permute-start(bf16[2,128,128]{2,1,0:T(8,128)(2,1)S(1)} %slice.30), channel_id=1, source_target_pairs={{20,0},{24,4},{28,8},{21,1},{25,5},{29,9},{22,2},{26,6},{30,10},{2... | collective-permute-start | bytes 196616 | tf_op jit(solution)/shard_map/ppermute | solution.py:50
  17.7 12.4 %copy-start.21 = (bf16[2,128,128]{2,1,0:T(8,128)(2,1)}, bf16[2,128,128]{2,1,0:T(8,128)(2,1)S(1)}, u32[]{:S(2)}) copy-start(bf16[2,128,128]{2,1,0:T(8,128)(2,1)S(1)} %collective-permute-done.2.diag) | copy-start | bytes 196612
  17.7 12.4 %copy-start.14 = (bf16[2,256,128]{2,1,0:T(8,128)(2,1)}, bf16[2,256,128]{2,1,0:T(8,128)(2,1)S(1)}, u32[]{:S(2)}) copy-start(bf16[2,256,128]{2,1,0:T(8,128)(2,1)S(1)} %collective-permute-done.right) | copy-start | bytes 393220
  17.7 12.4 %copy-start.16 = (bf16[2,128,256]{2,1,0:T(8,128)(2,1)}, bf16[2,128,256]{2,1,0:T(8,128)(2,1)S(1)}, u32[]{:S(2)}) copy-start(bf16[2,128,256]{2,1,0:T(8,128)(2,1)S(1)} %collective-permute-done.1.below) | copy-start | bytes 393220
  31.1 2.6 %collective-permute-start.3 = (bf16[2,384,128]{2,1,0:T(8,128)(2,1)S(1)}, bf16[2,384,128]{2,1,0:T(8,128)(2,1)S(1)}, u32[]{:S(2)}, u32[]{:S(2)}) collective-permute-start(bf16[2,384,128]{2,1,0:T(8,128)(2,1)S(1)} %get-tuple-element.19), channel_id=1, source_target_pairs={{0,4},{4,8},{8,12},{16,20},{20,24},{24,28},{1,5},{5,9},{9,13},{17,... | collective-permute-start | bytes 589832 | tf_op jit(solution)/shard_map/ppermute | solution.py:50
  32.4 3.3 %collective-permute-start.4 = (bf16[2,384,128]{2,1,0:T(8,128)(2,1)S(1)}, bf16[2,384,128]{2,1,0:T(8,128)(2,1)S(1)}, u32[]{:S(2)}, u32[]{:S(2)}) collective-permute-start(bf16[2,384,128]{2,1,0:T(8,128)(2,1)S(1)} %get-tuple-element.20), channel_id=1, source_target_pairs={{4,0},{8,4},{12,8},{20,16},{24,20},{28,24},{5,1},{9,5},{13,9},{21,... | collective-permute-start | bytes 589832 | tf_op jit(solution)/shard_map/ppermute | solution.py:50
  35.7 23.2 %copy-start.10 = (bf16[2,384,128]{2,1,0:T(8,128)(2,1)}, bf16[2,384,128]{2,1,0:T(8,128)(2,1)S(1)}, u32[]{:S(2)}) copy-start(bf16[2,384,128]{2,1,0:T(8,128)(2,1)S(1)} %collective-permute-done.4.from_right) | copy-start | bytes 589828
  35.7 25.3 %copy-start.3 = (f32[1,1,2,256,256]{4,3,2,1,0:T(8,128)S(1)}, f32[1,1,2,256,256]{4,3,2,1,0:T(8,128)}, u32[]{:S(2)}) copy-start(f32[1,1,2,256,256]{4,3,2,1,0:T(8,128)} %param.9) | copy-start | bytes 1572868
  36.5 24.5 %collective-permute-start.5 = (bf16[2,3,128,128]{3,2,1,0:T(8,128)(2,1)}, bf16[2,3,128,128]{3,2,1,0:T(8,128)(2,1)}, u32[]{:S(2)}, u32[]{:S(2)}) collective-permute-start(bf16[2,3,128,128]{3,2,1,0:T(8,128)(2,1)} %get-tuple-element.21), channel_id=1, source_target_pairs={{0,16},{4,20},{8,24},{12,28},{1,17},{5,21},{9,25},{13,29},{2,18},{... | collective-permute-start | bytes 589832 | tf_op jit(solution)/shard_map/ppermute | solution.py:50
  39.4 21.7 %collective-permute-start.6 = (bf16[2,3,128,128]{3,2,1,0:T(8,128)(2,1)}, bf16[2,3,128,128]{3,2,1,0:T(8,128)(2,1)}, u32[]{:S(2)}, u32[]{:S(2)}) collective-permute-start(bf16[2,3,128,128]{3,2,1,0:T(8,128)(2,1)} %get-tuple-element.22), channel_id=1, source_target_pairs={{16,0},{20,4},{24,8},{28,12},{17,1},{21,5},{25,9},{29,13},{18,2},{... | collective-permute-start | bytes 589832 | tf_op jit(solution)/shard_map/ppermute | solution.py:50
  40.7 8.1 %collective-permute-start.7 = (s32[16]{0:T(128)S(1)}, s32[16]{0:T(128)S(1)}, u32[]{:S(2)}, u32[]{:S(2)}) collective-permute-start(s32[16]{0:T(128)S(1)} %pad_add_fusion.1.meta), channel_id=1, source_target_pairs={{0,4},{4,8},{8,12},{16,20},{20,24},{24,28},{1,5},{5,9},{9,13},{17,... | collective-permute-start | bytes 200 | tf_op jit(solution)/shard_map/ppermute | solution.py:50
  47.4 3.0 %collective-permute-start.8 = (s32[16]{0:T(128)S(1)}, s32[16]{0:T(128)S(1)}, u32[]{:S(2)}, u32[]{:S(2)}) collective-permute-start(s32[16]{0:T(128)S(1)} %pad_add_fusion.1.meta), channel_id=1, source_target_pairs={{4,0},{8,4},{12,8},{20,16},{24,20},{28,24},{5,1},{9,5},{13,9},{21,... | collective-permute-start | bytes 200 | tf_op jit(solution)/shard_map/ppermute | solution.py:50
  50.5 7.1 %collective-permute-start.10 = (s32[3,16]{1,0:T(4,128)S(1)}, s32[3,16]{1,0:T(4,128)S(1)}, u32[]{:S(2)}, u32[]{:S(2)}) collective-permute-start(s32[3,16]{1,0:T(4,128)S(1)} %pad_add_fusion), channel_id=1, source_target_pairs={{16,0},{20,4},{24,8},{28,12},{17,1},{21,5},{25,9},{29,13},{18,2},{... | collective-permute-start | bytes 584 | tf_op jit(solution)/shard_map/ppermute | solution.py:50
  51.8 7.1 %collective-permute-start.9 = (s32[3,16]{1,0:T(4,128)S(1)}, s32[3,16]{1,0:T(4,128)S(1)}, u32[]{:S(2)}, u32[]{:S(2)}) collective-permute-start(s32[3,16]{1,0:T(4,128)S(1)} %pad_add_fusion), channel_id=1, source_target_pairs={{0,16},{4,20},{8,24},{12,28},{1,17},{5,21},{9,25},{13,29},{2,18},{... | collective-permute-start | bytes 584 | tf_op jit(solution)/shard_map/ppermute | solution.py:50
  76.6 16.0 %copy-start.19 = (f32[2,256,256]{2,1,0:T(8,128)S(1)}, f32[2,256,256]{2,1,0:T(8,128)}, u32[]{:S(2)}) copy-start(f32[2,256,256]{2,1,0:T(8,128)} %copy-done.18) | copy-start | bytes 1572868
  77.6 8.4 %collective-permute-start.18 = (bf16[3,128,256]{2,1,0:T(8,128)(2,1)S(1)}, bf16[3,128,256]{2,1,0:T(8,128)(2,1)S(1)}, u32[]{:S(2)}, u32[]{:S(2)}) collective-permute-start(bf16[3,128,256]{2,1,0:T(8,128)(2,1)S(1)} %fusion), channel_id=1, source_target_pairs={{0,4},{4,0},{8,12},{12,8},{16,20},{20,16},{24,28},{28,24},{1,5},{5... | collective-permute-start | bytes 589832 | tf_op jit(solution)/shard_map/ppermute | solution.py:55
  77.7 14.9 %collective-permute-start.11 = (bf16[2,256,128]{2,1,0:T(8,128)(2,1)}, bf16[2,256,128]{2,1,0:T(8,128)(2,1)S(1)}, u32[]{:S(2)}, u32[]{:S(2)}) collective-permute-start(bf16[2,256,128]{2,1,0:T(8,128)(2,1)} %copy-done.24), channel_id=1, source_target_pairs={{0,4},{4,8},{8,12},{16,20},{20,24},{24,28},{1,5},{5,9},{9,13},{17,... | collective-permute-start | bytes 393224 | tf_op jit(solution)/shard_map/ppermute | solution.py:50
  80.2 12.5 %collective-permute-start.12 = (bf16[2,128,256]{2,1,0:T(8,128)(2,1)}, bf16[2,128,256]{2,1,0:T(8,128)(2,1)S(1)}, u32[]{:S(2)}, u32[]{:S(2)}) collective-permute-start(bf16[2,128,256]{2,1,0:T(8,128)(2,1)} %copy-done.23), channel_id=1, source_target_pairs={{0,16},{4,20},{8,24},{12,28},{1,17},{5,21},{9,25},{13,29},{2,18},{... | collective-permute-start | bytes 393224 | tf_op jit(solution)/shard_map/ppermute | solution.py:50
  87.1 5.7 %collective-permute-start.19 = (bf16[3,64,256]{2,1,0:T(8,128)(2,1)S(1)}, bf16[3,64,256]{2,1,0:T(8,128)(2,1)}, u32[]{:S(2)}, u32[]{:S(2)}) collective-permute-start(bf16[3,64,256]{2,1,0:T(8,128)(2,1)S(1)} %fusion.1), channel_id=1, source_target_pairs={{0,8},{4,12},{8,0},{12,4},{16,24},{20,28},{24,16},{28,20},{1,9},{5... | collective-permute-start | bytes 294920 | tf_op jit(solution)/shard_map/ppermute | solution.py:55
  87.2 5.5 %collective-permute-start.13 = (bf16[2,128,128]{2,1,0:T(8,128)(2,1)S(1)}, bf16[2,128,128]{2,1,0:T(8,128)(2,1)S(1)}, u32[]{:S(2)}, u32[]{:S(2)}) collective-permute-start(bf16[2,128,128]{2,1,0:T(8,128)(2,1)S(1)} %copy-done.26), channel_id=1, source_target_pairs={{0,20},{4,24},{8,28},{1,21},{5,25},{9,29},{2,22},{6,26},{10,30},{3... | collective-permute-start | bytes 196616 | tf_op jit(solution)/shard_map/ppermute | solution.py:50
  93.8 5.4 %collective-permute-start.20 = (bf16[3,32,256]{2,1,0:T(8,128)(2,1)S(1)}, bf16[3,32,256]{2,1,0:T(8,128)(2,1)S(1)}, u32[]{:S(2)}, u32[]{:S(2)}) collective-permute-start(bf16[3,32,256]{2,1,0:T(8,128)(2,1)S(1)} %fusion.4), channel_id=1, source_target_pairs={{0,16},{4,20},{8,24},{12,28},{16,0},{20,4},{24,8},{28,12},{1,17},{... | collective-permute-start | bytes 147464 | tf_op jit(solution)/shard_map/ppermute | solution.py:55
  94.7 5.3 %collective-permute-start.14 = (bf16[2,128,256]{2,1,0:T(8,128)(2,1)S(1)}, bf16[2,128,256]{2,1,0:T(8,128)(2,1)S(1)}, u32[]{:S(2)}, u32[]{:S(2)}) collective-permute-start(bf16[2,128,256]{2,1,0:T(8,128)(2,1)S(1)} %get-tuple-element.35), channel_id=1, source_target_pairs={{0,1},{1,0},{2,3},{3,2},{4,5},{5,4},{6,7},{7,6},{8,9},{9,8},{10,11... | collective-permute-start | bytes 393224 | tf_op jit(solution)/shard_map/ppermute | solution.py:55
  94.7 5.3 %collective-permute-start.16 = (bf16[2,128,256]{2,1,0:T(8,128)(2,1)S(1)}, bf16[2,128,256]{2,1,0:T(8,128)(2,1)S(1)}, u32[]{:S(2)}, u32[]{:S(2)}) collective-permute-start(bf16[2,128,256]{2,1,0:T(8,128)(2,1)S(1)} %get-tuple-element.36), channel_id=1, source_target_pairs={{0,2},{1,3},{2,0},{3,1},{4,6},{5,7},{6,4},{7,5},{8,10},{9,11},{10,... | collective-permute-start | bytes 393224 | tf_op jit(solution)/shard_map/ppermute | solution.py:55
  99.2 4.9 %collective-permute-start.21 = (bf16[2,32,256]{2,1,0:T(8,128)(2,1)S(1)}, bf16[2,32,256]{2,1,0:T(8,128)(2,1)S(1)}, u32[]{:S(2)}, u32[]{:S(2)}) collective-permute-start(bf16[2,32,256]{2,1,0:T(8,128)(2,1)S(1)} %fusion.3), channel_id=1, source_target_pairs={{0,16},{4,20},{8,24},{12,28},{16,0},{20,4},{24,8},{28,12},{1,17},{... | collective-permute-start | bytes 98312 | tf_op jit(solution)/shard_map/ppermute | solution.py:55
  100.1 6.4 %collective-permute-start.15 = (bf16[2,128,256]{2,1,0:T(8,128)(2,1)S(1)}, bf16[2,128,256]{2,1,0:T(8,128)(2,1)S(1)}, u32[]{:S(2)}, u32[]{:S(2)}) collective-permute-start(bf16[2,128,256]{2,1,0:T(8,128)(2,1)S(1)} %get-tuple-element.33), channel_id=1, source_target_pairs={{0,2},{1,3},{2,0},{3,1},{4,6},{5,7},{6,4},{7,5},{8,10},{9,11},{10,... | collective-permute-start | bytes 393224 | tf_op jit(solution)/shard_map/ppermute | solution.py:55
  100.2 8.3 %collective-permute-start.17 = (bf16[2,128,256]{2,1,0:T(8,128)(2,1)S(1)}, bf16[2,128,256]{2,1,0:T(8,128)(2,1)S(1)}, u32[]{:S(2)}, u32[]{:S(2)}) collective-permute-start(bf16[2,128,256]{2,1,0:T(8,128)(2,1)S(1)} %get-tuple-element.34), channel_id=1, source_target_pairs={{0,1},{1,0},{2,3},{3,2},{4,5},{5,4},{6,7},{7,6},{8,9},{9,8},{10,11... | collective-permute-start | bytes 393224 | tf_op jit(solution)/shard_map/ppermute | solution.py:55
  104.1 4.3 %collective-permute-start.22 = (bf16[2,64,256]{2,1,0:T(8,128)(2,1)S(1)}, bf16[2,64,256]{2,1,0:T(8,128)(2,1)S(1)}, u32[]{:S(2)}, u32[]{:S(2)}) collective-permute-start(bf16[2,64,256]{2,1,0:T(8,128)(2,1)S(1)} %maximum_select_fusion.2), channel_id=1, source_target_pairs={{0,8},{4,12},{8,0},{12,4},{16,24},{20,28},{24,16},{28,20},{1,9},{5... | collective-permute-start | bytes 196616 | tf_op jit(solution)/shard_map/ppermute | solution.py:55
  108.4 1.4 %collective-permute-start.23 = (bf16[2,128,256]{2,1,0:T(8,128)(2,1)S(1)}, bf16[2,128,256]{2,1,0:T(8,128)(2,1)S(1)}, u32[]{:S(2)}, u32[]{:S(2)}) collective-permute-start(bf16[2,128,256]{2,1,0:T(8,128)(2,1)S(1)} %maximum_select_fusion.1), channel_id=1, source_target_pairs={{0,4},{4,0},{8,12},{12,8},{16,20},{20,16},{24,28},{28,24},{1,5},{5... | collective-permute-start | bytes 393224 | tf_op jit(solution)/shard_map/ppermute | solution.py:55
  (20 other events, 34.4 us)

commit v2 on v1

v2 whole, which is shorter than its diff:
```python
import functools
import math

import jax
import jax.numpy as jnp
import ml_dtypes
import numpy as np
from jax import lax
from jax.experimental import pallas as pl
from jax.experimental.pallas import tpu as pltpu
from jax.sharding import PartitionSpec as P

PS = 256
TS = 256
OVER = 128
TGW = 4
SLOTS = 4
SPAN = TS + OVER
L = 128
CH = 32
META = 16
COUNT = 2 * SLOTS
HAS_LEFT, HAS_RIGHT, HAS_ABOVE, HAS_BELOW, ODD, BIT1 = range(6)

penalty = 0.5
smoothing = 0.05
probe_step = 3.0

f32 = jnp.float32
bf16 = jnp.bfloat16


def dft_tables():
    indices = np.arange(PS, dtype=np.int32)
    phase_index = indices[:, None] * indices[None, :] % PS
    angles = phase_index.astype(np.float32) * np.float32(2.0 * math.pi / PS)
    scale = np.float32(1.0 / math.sqrt(PS))
    re = (np.cos(angles) * scale).astype(ml_dtypes.bfloat16)
    im = (-np.sin(angles) * scale).astype(ml_dtypes.bfloat16)
    fwd = np.block([[re, -im], [im, re]])
    bwd = np.block([[re, im], [-im, re]])
    return jnp.asarray(fwd), jnp.asarray(bwd)


def shifted(value, rows, cols):
    height = lax.axis_size("tile") // TGW
    pairs = []
    for i in range(height * TGW):
        r, c = divmod(i, TGW)
        pairs.append((i, (r + rows) % height * TGW + (c + cols) % TGW))
    return lax.ppermute(value, "tile", pairs)


def swapped(value, axis, bit):
    n = lax.axis_size(axis)
    return lax.ppermute(value, axis, [(i, i ^ bit) for i in range(n)])


def is_power(n):
    return n & (n - 1) == 0


def inner_swapped(value):
    n = lax.axis_size("tile")
    return lax.ppermute(value, "tile", [(i, i ^ 3 if i % TGW in (1, 2) else i) for i in range(n)])


def scan_sums(parts, sums):
    n = lax.axis_size("scan")
    change = None
    if not is_power(n):
        return [v for part in parts for v in (lax.psum(part, "scan"), jnp.zeros_like(part))], change
    bits = [1 << k for k in range(n.bit_length() - 1)]
    for k in range(len(bits)):
        came = [swapped(parts[p], "scan", bits[(k + p) % len(bits)]) for p in range(2)]
        pairs = [parts[0], came[0], parts[1], came[1]]
        if k < len(bits) - 1:
            outs = [(parts[0].shape, bf16)] * 2
            if sums is not None and k == 0:
                last = swapped(sums, "tile", 4)
                outs = outs + [((2,) + sums.shape[1:], bf16)]
                *parts, change = call(mix_and_update, "mix_and_update", outs)(*pairs, sums, last)
            else:
                parts = call(mix, f"mix{k}", outs)(*pairs)
    return pairs, change


def doubled(index, change, bit):
    other = swapped(change, "tile", bit)
    return jnp.where(
        (index // bit) % 2 == 1,
        jnp.concatenate([other, change], 1),
        jnp.concatenate([change, other], 1),
    )


def lane_pull(blocks, c):
    lane = lax.broadcasted_iota(jnp.int32, blocks[0].shape, 1)
    keep = lane < L - c
    r = [pltpu.roll(v, (L - c) % L, 1) for v in blocks]
    return jnp.concatenate([jnp.where(keep, r[0], r[1]), jnp.where(keep, r[1], r[2])], 1)


def lane_push(blocks, c):
    lane = lax.broadcasted_iota(jnp.int32, blocks[0].shape, 1)
    past = lane >= c
    r = [pltpu.roll(v, c % L, 1) for v in blocks]
    z = jnp.zeros_like(r[0])
    return [jnp.where(past, r[0], z), jnp.where(past, r[1], r[0]), jnp.where(past, z, r[1])]


def visit_pair(p, meta, ext, probe, amps, fwd, bwd, acc, pnum, win, X, Y, W):
    N = PS
    used = jnp.where(2 * p + 1 < meta[COUNT], 1.0, 0.0).astype(f32)
    corners = [(meta[4 * p + 2 * i], meta[4 * p + 2 * i + 1]) for i in range(2)]

    def leave(i):
        r, c = corners[i]
        for k in range(0, N, CH):
            rows = slice(k, k + CH)
            w = [
                lane_pull([ext[ch, j, pl.ds(r + k, CH), :] for j in range(3)], c) for ch in range(2)
            ]
            if i == 1:
                w = [v * used for v in w]
            pr, pi = probe[0, rows, :], probe[1, rows, :]
            win[i, 0, rows, :] = w[0]
            win[i, 1, rows, :] = w[1]
            X[i, rows, :] = (pr * w[0] - pi * w[1]).astype(bf16)
            X[i, N + k : N + k + CH, :] = (pr * w[1] + pi * w[0]).astype(bf16)
            pnum[2, rows, :] += w[0] * w[0] + w[1] * w[1]

    def columns(i, table):
        t = jnp.dot(table[...], X[i], preferred_element_type=f32)
        Y[i, :, :N] = t[:N].astype(bf16)
        Y[i, :, N:] = t[N:].astype(bf16)

    def rows_of(i, table):
        W[i] = jnp.dot(Y[i], table[...], preferred_element_type=f32)

    def compare(i):
        for k in range(0, N, CH):
            wr, wi = W[i, k : k + CH, :N], W[i, k : k + CH, N:]
            a = amps[2 * p + i, k : k + CH, :].astype(f32)
            f = a * lax.rsqrt(wr * wr + wi * wi + smoothing) - 1.0
            X[i, k : k + CH, :] = (wr * f).astype(bf16)
            X[i, N + k : N + k + CH, :] = (wi * f).astype(bf16)

    def gather(i):
        r, c = corners[i]
        for k in range(0, N, CH):
            rows = slice(k, k + CH)
            br, bi = W[i, rows, :N], W[i, rows, N:]
            pr, pi = probe[0, rows, :], probe[1, rows, :]
            wr, wi = win[i, 0, rows, :], win[i, 1, rows, :]
            pnum[0, rows, :] += wr * br + wi * bi
            pnum[1, rows, :] += wr * bi - wi * br
            for ch, v in enumerate((pr * br + pi * bi, pr * bi - pi * br)):
                for j, u in enumerate(lane_push([v[:, :L], v[:, L:]], c)):
                    acc[ch, j, pl.ds(r + k, CH), :] += u

    leave(0)
    columns(0, fwd)
    leave(1)
    rows_of(0, bwd)
    columns(1, fwd)
    compare(0)
    rows_of(1, bwd)
    columns(0, bwd)
    compare(1)
    rows_of(0, fwd)
    columns(1, bwd)
    gather(0)
    rows_of(1, fwd)
    gather(1)


def fetch(pairs, sems):
    copies = [pltpu.make_async_copy(src, dst, sems.at[i]) for i, (src, dst) in enumerate(pairs)]
    for copy in copies:
        copy.start()
    return copies


def stage(own_h, dual_h, probe_h, ext, acc, probe, sems, own, dual):
    copies = fetch([(own_h, own), (dual_h, dual), (probe_h, probe)], sems)
    acc[:, 2] = jnp.zeros((2, SPAN, L), f32)
    copies[0].wait()
    for j in range(2):
        cols = slice(j * L, (j + 1) * L)
        acc[:, j, TS:, :] = jnp.zeros((2, OVER, L), f32)
        ext[:, j, :TS, :] = own[:, :, cols].astype(bf16).astype(f32)
    copies[1].wait()
    for j in range(2):
        cols = slice(j * L, (j + 1) * L)
        acc[:, j, :TS, :] = -penalty * dual[:, :, cols]
    copies[2].wait()


def first_pass(
    two, meta, flags, right, below, diag, ext0, acc0, probe, fwd_h, bwd_h, amps_h, *rest,
):
    ext, acc, pnum, side, inner, *mids, fwd, bwd, amps, sems, win, X, Y, W = rest[3:]
    copies = fetch([(fwd_h, fwd), (bwd_h, bwd), (amps_h, amps)], sems)
    has_right = flags[HAS_RIGHT : HAS_RIGHT + 1, :]
    has_below = flags[HAS_BELOW : HAS_BELOW + 1, :]
    ext[:, 2, :TS, :] = right[...].astype(f32) * has_right
    ext[:, 2, TS:, :] = diag[...].astype(f32) * (has_right * has_below)
    for j in range(2):
        cols = slice(j * L, (j + 1) * L)
        ext[:, j, TS:, :] = below[:, :, cols].astype(f32) * has_below
    pnum[...] = jnp.zeros_like(pnum)
    for copy in copies:
        copy.wait()

    @pl.loop(0, (meta[COUNT] + 1) // 2)
    def _(p):
        visit_pair(p, meta, ext, probe, amps, fwd, bwd, acc, pnum, win, X, Y, W)

    odd = flags[ODD : ODD + 1, :] > 0.0
    for ch in range(2):
        side[ch] = jnp.where(odd, acc[ch, 0], acc[ch, 2]).astype(bf16)
        inner[ch] = jnp.where(odd, acc[ch, 2], acc[ch, 0]).astype(bf16)
        for rim, mid in zip(rims_of(two, flags, lambda rows: acc[ch, 1, rows, :]), mids):
            mid[ch] = rim.astype(bf16)


def rims_of(two, flags, get):
    down, up = get(slice(TS, SPAN)), get(slice(0, OVER))
    return [jnp.where(flags[HAS_BELOW : HAS_BELOW + 1, :] > 0.0, down, up)] if two else [down, up]


def from_sides(flags, side, inner):
    odd = flags[ODD : ODD + 1, :] > 0.0
    valid = flags[HAS_LEFT : HAS_LEFT + 1, :] * flags[HAS_RIGHT : HAS_RIGHT + 1, :]
    side, inner = side.astype(f32), inner.astype(f32) * valid
    return jnp.where(odd, side, inner), jnp.where(odd, inner, side)


def between(two, flags, acc, side, inner, *rest):
    outs = rest[-1:] if two else rest[-2:]
    for ch in range(2):
        for at in range(2):

            def total(rows):
                came = from_sides(flags, side[ch, rows, :], inner[ch, rows, :])[at]
                return acc[ch, 2 * at, rows, :] + came

            for rim, out in zip(rims_of(two, flags, total), outs):
                out[ch, at] = rim.astype(bf16)


def weigh(two, *rest):
    metas = rest[:3]
    flags, *sources = rest[-18:-11]
    weight, *targets, sems, p2, buf, there = rest[-11:]
    copies = fetch([(flags, there)] + list(zip(sources, targets)), sems)
    probe = targets[2]
    buf[...] = jnp.zeros_like(buf)
    copies[3].wait()
    for j in range(2):
        cols = slice(j * L, (j + 1) * L)
        p2[j] = probe[0, :, cols] * probe[0, :, cols] + probe[1, :, cols] * probe[1, :, cols]
    copies[0].wait()
    for dr in (-1, 0, 1):
        for dc in (-1, 0, 1):
            meta, at_row = metas[{0: 0, -1: 1, 1: 2}[dc]], {0: 0, -1: 1, 1: 1 if two else 2}[dr]
            first, rows = {-1: (OVER, OVER), 0: (0, PS), 1: (0, OVER)}[dr]
            base = {-1: 0, 0: OVER, 1: OVER + TS}[dr]
            count = meta[at_row, COUNT]
            for flag, at, step in (
                (HAS_ABOVE, -1, dr), (HAS_BELOW, 1, dr), (HAS_LEFT, -1, dc), (HAS_RIGHT, 1, dc)
            ):
                if step == at:
                    count = jnp.where(there[flag, 0] > 0.0, count, 0)

            @pl.loop(0, count)
            def _(s, meta=meta, at_row=at_row, dc=dc, first=first, rows=rows, base=base):
                r, c = meta[at_row, 2 * s], meta[at_row, 2 * s + 1]
                for k in range(0, rows, 64):
                    at = pl.ds(base + r + k, 64)
                    v = [p2[j, first + k : first + k + 64, :] for j in range(2)]
                    lane = lax.broadcasted_iota(jnp.int32, v[0].shape, 1)
                    if dc == 0:
                        for j, u in enumerate(lane_push(v, c)):
                            buf[j, at, :] += u
                    elif dc < 0:
                        buf[0, at, :] += jnp.where(lane < c, pltpu.roll(v[1], c % L, 1), 0.0)
                    else:
                        buf[2, at, :] += jnp.where(lane >= c, pltpu.roll(v[0], c % L, 1), 0.0)

    weight[...] = buf[:, OVER : OVER + SPAN, :]
    for k, copy in enumerate(copies):
        if k not in (0, 3):
            copy.wait()


def second_pass(
    meta, flags, right, below, diag, acc1, side, inner, mid_above, mid_below, from_above, from_below,
    weight, pnum1, own, dual, probe, amps, fwd, bwd,
    base, shrink, to_right, to_below, to_diag, pnum, to_swap,
    partial, ext, acc, win, X, Y, W,
):
    has_right = flags[HAS_RIGHT : HAS_RIGHT + 1, :]
    has_below = flags[HAS_BELOW : HAS_BELOW + 1, :]
    has_above = flags[HAS_ABOVE : HAS_ABOVE + 1, :]
    acc[...] = jnp.zeros_like(acc)
    pnum[...] = pnum1[...]
    for ch in range(2):
        for j in range(3):
            cols = slice(j * L, (j + 1) * L)
            for k in range(0, SPAN, 64):
                rows = slice(k, k + 64)
                total = acc1[ch, j, rows, :]
                if j != 1:
                    total = total + from_sides(flags, side[ch, rows, :], inner[ch, rows, :])[j // 2]
                if k < OVER:
                    came = mid_above[ch, rows, :] if j == 1 else from_above[ch, j // 2, rows, :]
                    total = total + came.astype(f32) * has_above
                if k >= TS:
                    rim = slice(k - TS, k - TS + 64)
                    came = mid_below[ch, rim, :] if j == 1 else from_below[ch, j // 2, rim, :]
                    total = total + came.astype(f32)
                step = total / (weight[j, rows, :] + penalty)
                if j < 2 and k < TS:
                    est = own[ch, rows, cols] + step
                    partial[ch, rows, cols] = est
                else:
                    if k < TS:
                        est = right[ch, rows, :].astype(f32) + step
                    elif j < 2:
                        est = below[ch, k - TS : k - TS + 64, cols].astype(f32) + step
                    else:
                        est = diag[ch, k - TS : k - TS + 64, :].astype(f32) + step
                    if j == 2:
                        est = est * has_right
                    if k >= TS:
                        est = est * has_below
                ext[ch, j, rows, :] = est.astype(bf16).astype(f32)

    @pl.loop(0, (meta[COUNT] + 1) // 2)
    def _(p):
        visit_pair(p, meta, ext, probe, amps, fwd, bwd, acc, pnum, win, X, Y, W)

    to_diag[...] = acc[:, 2, TS:, :].astype(bf16)
    to_right[...] = acc[:, 2, :TS, :].astype(bf16)
    odd = flags[ODD : ODD + 1, :1] > 0.0
    for ch in range(3):
        lo, hi = pnum[ch, : PS // 2, :], pnum[ch, PS // 2 :, :]
        to_swap[ch] = jnp.where(odd, lo, hi).astype(bf16)
    for j in range(2):
        cols = slice(j * L, (j + 1) * L)
        to_below[:, :, cols] = acc[:, j, TS:, :].astype(bf16)
        for k in range(0, TS, 64):
            rows = slice(k, k + 64)
            over = 1.0 / (weight[j, rows, :] + penalty)
            shrink[j, rows, :] = over
            for ch in range(2):
                est = partial[ch, rows, cols]
                held = dual[ch, rows, cols]
                pull = penalty * (own[ch, rows, cols] - held - est)
                base[ch, rows, cols] = est + held + (acc[ch, j, rows, :] + pull) * over


def halve(k, flags, sums, came, *rest):
    outs = rest[-1:] if k == 1 else rest[-2:]
    total = []
    for ch in range(3):
        kept = sums[ch]
        if k == 0:
            lo, hi = kept[: PS // 2], kept[PS // 2 :]
            kept = jnp.where(flags[ODD : ODD + 1, :1] > 0.0, hi, lo)
        total.append(kept + came[ch].astype(f32))
    if k == 1:
        for ch in range(3):
            outs[0][ch] = total[ch].astype(bf16)
        return
    up = flags[BIT1 : BIT1 + 1, :1] > 0.0
    half = came.shape[1] // 2
    for ch in range(3):
        lo, hi = total[ch][:half], total[ch][half:]
        outs[0][ch] = jnp.where(up, hi, lo)
        outs[1][ch] = jnp.where(up, lo, hi).astype(bf16)


def finish_estimate(flags, base, shrink, from_left, from_above, from_diag, *rest):
    combined, parts = rest[-3], rest[-2:]
    has_left = flags[HAS_LEFT : HAS_LEFT + 1, :]
    has_above = flags[HAS_ABOVE : HAS_ABOVE + 1, :]
    for ch in range(2):
        for j in range(2):
            cols = slice(j * L, (j + 1) * L)
            for k in range(0, TS, 64):
                rows = slice(k, k + 64)
                total = base[ch, rows, cols]
                came = None
                if j == 0:
                    came = from_left[ch, rows, :].astype(f32) * has_left
                if k < OVER:
                    above = from_above[ch, rows, cols].astype(f32) * has_above
                    came = above if came is None else came + above
                    if j == 0:
                        came = came + from_diag[ch, rows, :].astype(f32) * (has_left * has_above)
                if came is not None:
                    total = total + came * shrink[j, rows, :]
                combined[ch, rows, cols] = total
                part = slice(k % (TS // 2), k % (TS // 2) + 64)
                parts[k // (TS // 2)][ch, part, cols] = total.astype(bf16)


def mixed(first, first_came, second, second_came, outs):
    for out, part, came in ((outs[0], first, first_came), (outs[1], second, second_came)):
        for ch in range(2):
            out[ch] = (part[ch].astype(f32) + came[ch].astype(f32)).astype(bf16)


def mix(*refs):
    mixed(*refs[:4], refs[-2:])


def mix_and_update(first, first_came, second, second_came, held, came, *outs):
    mixed(first, first_came, second, second_came, outs)
    total = [held[ch].astype(f32) + came[ch].astype(f32) for ch in range(3)]
    over = probe_step * lax.rsqrt(total[2] + 1.0)
    for ch in range(2):
        outs[2][ch] = (total[ch] * over).astype(bf16)


def settle(groups, first, first_came, second, second_came, combined, *rest):
    settled, dual_new = rest[-2:]
    for k in range(0, TS, CH):
        rows = slice(k, k + CH)
        part, came = (first, first_came) if k < TS // 2 else (second, second_came)
        at = slice(k % (TS // 2), k % (TS // 2) + CH)
        re, im = [
            (part[ch, at, :].astype(f32) + came[ch, at, :].astype(f32)) * (1.0 / groups)
            for ch in range(2)
        ]
        over = 1.0 / jnp.maximum(jnp.sqrt(re * re + im * im), 1.0)
        re, im = re * over, im * over
        settled[0, rows, :] = re
        settled[1, rows, :] = im
        dual_new[0, rows, :] = combined[0, rows, :] - re
        dual_new[1, rows, :] = combined[1, rows, :] - im


V = pl.BlockSpec(memory_space=pltpu.VMEM)
S = pl.BlockSpec(memory_space=pltpu.SMEM)
H = pl.BlockSpec(memory_space=pltpu.HBM)


def pinned(value):
    return pltpu.with_memory_space_constraint(value, pltpu.VMEM)


def call(body, name, outs, scratch=(), scalars=0, far=0, copies=0, aliases=None, held=False, flops=0):
    def run(*operands):
        near = len(operands) - scalars - far
        spaces = [None] * (scalars + near) + [pltpu.HBM] * far
        operands = [
            v if space is None else pltpu.with_memory_space_constraint(v, space)
            for v, space in zip(operands, spaces)
        ]
        return pl.pallas_call(
            body,
            in_specs=[S] * scalars + [V] * near + [H] * far,
            out_specs=[V] * len(outs),
            out_shape=[
                pltpu.VMEM(shape, dtype) if held else jax.ShapeDtypeStruct(shape, dtype)
                for shape, dtype in outs
            ],
            scratch_shapes=[
                pltpu.SemaphoreType.DMA((copies,)) if one is None else pltpu.VMEM(*one)
                if isinstance(one, tuple) else one
                for one in scratch
            ],
            input_output_aliases=aliases or {},
            cost_estimate=pl.CostEstimate(
                flops=flops or sum(math.prod(shape) for shape, _ in outs),
                bytes_accessed=sum(v.size * v.dtype.itemsize for v in operands[scalars + near :]),
                transcendentals=0,
            ),
            compiler_params=pltpu.CompilerParams(vmem_limit_bytes=24 * 2**20),
            name=name,
        )(*operands)

    return run


PLANES = ((2, PS, PS), f32)
PASS = SLOTS * 4 * 8 * PS**3
WORK = [
    ((2, 2, PS, PS), f32),
    ((2, 2 * PS, PS), bf16),
    ((2, PS, 2 * PS), bf16),
    ((2, PS, 2 * PS), f32),
]
TABLE = ((2 * PS, 2 * PS), bf16)
WIDE = ((2, 3, SPAN, L), f32)
SUMS = ((3, PS, PS), f32)


def shards(consensus, duals, probes, amplitudes, offsets, counts):
    fwd, bwd = dft_tables()
    n = lax.axis_size("tile")
    index = lax.axis_index("tile")
    own = consensus[0]
    dual = duals[0, 0]
    probe = probes[0]
    amps = amplitudes[0, 0]
    measured = ((SLOTS, PS, PS), bf16)

    rounded = own.astype(bf16)
    below = shifted(rounded[:, :OVER, :], -1, 0)
    diag = shifted(rounded[:, :OVER, :OVER], -1, -1)
    right = shifted(rounded[:, :, :OVER], 0, -1)

    height = n // TGW
    two = height == 2
    row, col = index // TGW, index % TGW
    flags = [col > 0, col < TGW - 1, row > 0, row < height - 1]
    flags = flags + [(index // bit) % 2 == 1 for bit in (1, 2)] + [col < 0] * 2
    flags = jnp.broadcast_to(jnp.stack(flags).astype(f32)[:, None], (8, L))
    meta = jnp.concatenate(
        [offsets[0, 0].reshape(COUNT), counts[0], jnp.zeros((META - COUNT - 1,), jnp.int32)]
    )
    column = [meta, shifted(meta, 1, 0)] if two else [meta, shifted(meta, 1, 0), shifted(meta, -1, 0)]
    column = jnp.stack(column)
    metas = [column, shifted(column, 0, 1), shifted(column, 0, -1)]

    inputs = (own, dual, probe, amps, fwd, bwd)
    staged = call(
        stage, "stage", [WIDE, WIDE, PLANES], [None, PLANES, PLANES], 0, 3, 3, held=True
    )(own, dual, probe)
    staged = [pinned(v) for v in staged]
    rim = ((2, OVER, L), bf16)
    ext, acc, pnum, side, inner, *mids = call(
        functools.partial(first_pass, two), "first_pass",
        [WIDE, WIDE, SUMS, ((2, SPAN, L), bf16), ((2, SPAN, L), bf16)] + [rim] * (1 if two else 2),
        [TABLE, TABLE, measured, None] + WORK, 1, 6, 3, aliases={5: 0, 6: 1}, flops=PASS,
    )(meta, flags, right, below, diag, *staged, fwd, bwd, amps, *metas)
    side = swapped(side, "tile", 1)
    inner = inner_swapped(inner)

    def down_and_up(rims):
        down = shifted(rims[0], 1, 0)
        return down, down if two else shifted(rims[1], -1, 0)

    mid_above, mid_below = down_and_up(mids)
    rims = call(
        functools.partial(between, two), "between", [((2, 2, OVER, L), bf16)] * (1 if two else 2)
    )(flags, acc, side, inner, pnum, right, below, diag, mid_above, mid_below)
    from_above, from_below = down_and_up(rims)
    weight, *inputs = call(
        functools.partial(weigh, two), "weigh",
        [((3, SPAN, L), f32), PLANES, PLANES, PLANES, measured, TABLE, TABLE],
        [None, ((2, PS, L), f32), ((3, SPAN + 2 * OVER, L), f32), pltpu.SMEM((8, L), f32)],
        len(metas), 7, 7, held=True,
    )(*metas, rims[0], acc, side, inner, pnum, right, below, diag, mid_above, mid_below, flags, *inputs)
    weight, *inputs = [pinned(v) for v in (weight, *inputs)]

    base, shrink, to_right, to_below, to_diag, pnum, to_swap = call(
        second_pass, "second_pass",
        [PLANES, ((2, TS, L), f32), ((2, TS, OVER), bf16), ((2, OVER, TS), bf16),
         ((2, OVER, OVER), bf16), SUMS, ((3, PS // 2, PS), bf16)],
        [PLANES, WIDE, WIDE] + WORK, 1, flops=PASS,
    )(meta, flags, right, below, diag, acc, side, inner, mid_above, mid_below, from_above,
      from_below, weight, pnum, *inputs)
    from_above = shifted(to_below, 1, 0)
    from_diag = shifted(to_diag, 1, 1)
    from_left = shifted(to_right, 0, 1)

    def halved(k, sums, send, *after):
        came = swapped(send, "tile", 1 << k)
        rows = came.shape[1]
        outs = [((3, rows // 2, PS), f32), ((3, rows // 2, PS), bf16)]
        if k == 1:
            outs = [((3, rows, PS), bf16)]
        return call(functools.partial(halve, k), f"halve{k}", outs)(flags, sums, came, *after)

    eight = n == 8 and lax.axis_size("scan") in (4, 8)
    first = halved(0, pnum, to_swap, base, shrink) if eight else []
    combined, *parts = call(
        finish_estimate, "finish_estimate", [PLANES] + [((2, TS // 2, TS), bf16)] * 2
    )(flags, base, shrink, from_left, from_above, from_diag, *first)
    sums = halved(1, *first, parts[0])[0] if eight else None
    pairs, change = scan_sums(parts, sums)
    settled, dual_new = call(
        functools.partial(settle, lax.axis_size("scan")), "settle", [PLANES] * 2
    )(*pairs, combined)
    if eight:
        change = doubled(index, doubled(index, change, 2), 1).astype(f32)
    else:
        total = lax.psum(pnum, "tile")
        change = probe_step * total[0:2] / jnp.sqrt(total[2] + 1.0)
    probe_new = probe + change
    return (settled[None], dual_new[None, None], probe_new[None])


def solution(mesh):
    placed = (
        P("tile", None, None, None),
        P("scan", "tile", None, None, None),
        P("scan", None, None, None),
        P("scan", "tile", None, None, None),
        P("scan", "tile", None, None),
        P("scan", "tile"),
    )
    return jax.shard_map(
        shards,
        mesh=mesh,
        in_specs=placed,
        out_specs=(
            P("tile", None, None, None),
            P("scan", "tile", None, None, None),
            P("scan", None, None, None),
        ),
        check_vma=False,
    )
```

time: 111 us -> 76.3 us (0.69)
  starting transfers between devices: 41.3 us -> 19 us
  local copies, waits for them, and re-layouts: 13.1 us -> 1.57 us
  waiting for transfers between devices: 28.8 us -> 31.9 us
  other arithmetic: 4.37 us -> 2.12 us
  Pallas kernels: 21.1 us -> 19.5 us
    ppermute x14 -> x11, starting transfers between devices: 35.3 us -> 11.9 us  [shifted(): return lax.ppermute(value, 'tile', pairs)]
    unnamed x57 -> x19, local copies, waits for them, and re-layouts: 12.8 us -> 1.28 us
    ppermute x14 -> x11, waiting for transfers between devices: 20.1 us -> 22.3 us  [shifted(): return lax.ppermute(value, 'tile', pairs)]
    add x6 -> x1, other arithmetic: 2.88 us -> 0.86 us  [shards(): probe_new = probe + change]
    pallas_call x6 -> x10, Pallas kernels: 21.1 us -> 19.5 us  [run(): pl.pallas_call(body, in_specs=[S] * scalars + [V] * near + [H] * far, out...]
  transfers between devices with their start and end apart: 24 -> 22, of which waited for: 12 -> 13; matrix products, arithmetic and copies ran while one was open for 2% -> 2% of each run, Pallas kernels for 3% -> 8%
where the time goes in v2:
time: 76.3 us; the launch traced here: 75.6 us
  waiting for transfers between devices  31.9 us (42%)
  Pallas kernels  19.5 us (26%)
  starting transfers between devices  19 us (25%)
  other arithmetic  2.12 us (3%)
  local copies, waits for them, and re-layouts  1.57 us (2%)
  between operations  1.52 us (2%)
    ppermute x11, waiting for transfers between devices, shifted(): return lax.ppermute(value, 'tile', pairs)  22.3 us
    pallas_call x10, Pallas kernels, run(): pl.pallas_call(body, in_specs=[S] * scalars + [V] * near + [H] * far, out...  19.5 us
    ppermute x11, starting transfers between devices, shifted(): return lax.ppermute(value, 'tile', pairs)  11.9 us
    ppermute x10, waiting for transfers between devices, swapped(): return lax.ppermute(value, axis, [(i, i ^ bit) for i in range(n)])  9.59 us
    ppermute x10, starting transfers between devices, swapped(): return lax.ppermute(value, axis, [(i, i ^ bit) for i in range(n)])  6.41 us
  transfers between devices with their start and end apart: 22, of which 13 were waited for; matrix products, arithmetic and copies ran while one was open for 2% of the time, Pallas kernels for 8%

profile of v2, /device:TPU:0, one launch (start us, length us, event | category | flops | bytes accessed | tf_op | source)
XLA Modules:
  0.0 75.6 jit_solution(14979400288391475027)
XLA Ops:
  1.3 0.8 %copy.14 = s32[1,1,4,2]{3,2,1,0:T(4,128)S(1)} copy(s32[1,1,4,2]{2,3,1,0:T(2,128)} %param.12) | data formatting | bytes 64 | tf_op args[4]
  2.2 4.0 %collective-permute-start.3 = (s32[16]{0:T(128)S(1)}, s32[16]{0:T(128)S(1)}, u32[]{:S(2)}, u32[]{:S(2)}) collective-permute-start(s32[16]{0:T(128)S(1)} %pad_add_fusion.1.meta), channel_id=1, source_target_pairs={{0,16},{4,20},{8,24},{12,28},{16,0},{20,4},{24,8},{28,12},{1,17},{... | collective-permute-start | bytes 200 | tf_op jit(solution)/shard_map/ppermute | solution.py:51
  6.2 1.1 %bitcast_convert_fusion = bf16[2,256,256]{2,1,0:T(8,128)(2,1)S(1)} fusion(f32[1,2,256,256]{3,2,1,0:T(8,128)} %param.8), kind=kLoop, calls=%fused_computation.5 | loop fusion | flops 131072 | bytes 786432 | tf_op jit(solution)/shard_map/convert_element_type | solution.py:513
  7.3 0.6 collective-permute-start.2
  7.9 1.2 %collective-permute-start = (bf16[2,256,128]{2,1,0:T(8,128)(2,1)S(1)}, bf16[2,256,128]{2,1,0:T(8,128)(2,1)S(1)}, u32[]{:S(2)}, u32[]{:S(2)}) collective-permute-start(bf16[2,256,128]{2,1,0:T(8,128)(2,1)S(1)} %slice.12), channel_id=1, source_target_pairs={{0,12},{4,0},{8,4},{12,8},{16,28},{20,16},{24,20},{28,24},{1,13},{... | collective-permute-start | bytes 393224 | tf_op jit(solution)/shard_map/ppermute | solution.py:51
  9.1 2.7 %collective-permute-start.1 = (bf16[2,128,256]{2,1,0:T(8,128)(2,1)S(1)}, bf16[2,128,256]{2,1,0:T(8,128)(2,1)S(1)}, u32[]{:S(2)}, u32[]{:S(2)}) collective-permute-start(bf16[2,128,256]{2,1,0:T(8,128)(2,1)S(1)} %slice.13), channel_id=1, source_target_pairs={{0,16},{4,20},{8,24},{12,28},{16,0},{20,4},{24,8},{28,12},{1,17},{... | collective-permute-start | bytes 393224 | tf_op jit(solution)/shard_map/ppermute | solution.py:51
  11.8 1.4 %stage.1 = (f32[2,3,384,128]{3,2,1,0:T(8,128)S(1)}, f32[2,3,384,128]{3,2,1,0:T(8,128)S(1)}, f32[2,256,256]{2,1,0:T(8,128)S(1)}) custom-call(f32[2,256,256]{2,1,0:T(8,128)} %bitcast.24, f32[2,256,256]{2,1,0:T(8,128)} %bitcast.26, f32[2,256,256]{2,1,0:T(8,128)} %bitcast.22), custom_call_target="tpu_custom_call" | custom-call | flops 720896 | bytes 1572864 | tf_op jit(solution)/shard_map/stage/pallas_call | solution.py:464
  13.4 0.5 collective-permute-start.4
  13.9 0.8 %collective-permute-done.5.rest_2_ = s32[2,16]{1,0:T(2,128)S(1)} collective-permute-done((s32[2,16]{1,0:T(2,128)S(1)}, s32[2,16]{1,0:T(2,128)S(1)}, u32[]{:S(2)}, u32[]{:S(2)}) %collective-permute-start.5) | collective-permute-done | bytes 160 | tf_op jit(solution)/shard_map/ppermute | solution.py:51
  14.7 1.8 %collective-permute-done.4.rest_1_ = s32[2,16]{1,0:T(2,128)S(1)} collective-permute-done((s32[2,16]{1,0:T(2,128)S(1)}, s32[2,16]{1,0:T(2,128)S(1)}, u32[]{:S(2)}, u32[]{:S(2)}) %collective-permute-start.4) | collective-permute-done | bytes 160 | tf_op jit(solution)/shard_map/ppermute | solution.py:51
  16.5 2.9 %collective-permute-done.1.below.rest_2_.rest_9_ = bf16[2,128,256]{2,1,0:T(8,128)(2,1)S(1)} collective-permute-done((bf16[2,128,256]{2,1,0:T(8,128)(2,1)S(1)}, bf16[2,128,256]{2,1,0:T(8,128)(2,1)S(1)}, u32[]{:S(2)}, u32[]{:S(2)}) %collective-permute-start.1) | collective-permute-done | bytes 131104 | tf_op jit(solution)/shard_map/ppermute | solution.py:51
  19.5 6.8 %first_pass.1 = (f32[2,3,384,128]{3,2,1,0:T(8,128)S(1)}, f32[2,3,384,128]{3,2,1,0:T(8,128)S(1)}, f32[3,256,256]{2,1,0:T(8,128)S(1)}, bf16[2,384,128]{2,1,0:T(8,1...) custom-call(s32[16]{0:T(128)S(1)} %pad_add_fusion.1.meta, ...), custom_call_target="tpu_custom_call", output_to_operand_aliasing={{0}: (5, {}), {1}: (6, {})} | custom-call | flops 2147483648 | bytes 1573248 | tf_op jit(solution)/shard_map/first_pass/pallas_call | solution.py:464
  26.4 0.7 collective-permute-start.7
  27.2 6.6 %collective-permute-done.8.rest_4_.rest_5_.rest_11_.rest_12_.mid_above.mid_below = bf16[2,128,128]{2,1,0:T(8,128)(2,1)S(1)} collective-permute-done((bf16[2,128,128]{2,1,0:T(8,128)(2,1)S(1)}, bf16[2,128,128]{2,1,0:T(8,128)(2,1)S(1)}, u32[]{:S(2)}, u32[]{:S(2)}) %collective-permute-start.8) | collective-permute-done | bytes 65568 | tf_op jit(solution)/shard_map/ppermute | solution.py:51
  34.4 3.3 %weigh.1 = (f32[3,384,128]{2,1,0:T(8,128)S(1)}, f32[2,256,256]{2,1,0:T(8,128)S(1)}, f32[2,256,256]{2,1,0:T(8,128)S(1)}, f32[2,256,256]{2,1,0:T(8,128)S(1)}, bf16...) custom-call(s32[2,16]{1,0:T(2,128)S(1)} %copy-done.3, ...), custom_call_target="tpu_custom_call" | custom-call | flops 1327104 | bytes 3149824 | tf_op jit(solution)/shard_map/weigh/pallas_call | solution.py:464
  37.8 4.6 %collective-permute-done.9.from_above.from_below = bf16[2,2,128,128]{3,2,1,0:T(8,128)(2,1)S(1)} collective-permute-done((bf16[2,2,128,128]{3,2,1,0:T(8,128)(2,1)S(1)}, bf16[2,2,128,128]{3,2,1,0:T(8,128)(2,1)S(1)}, u32[]{:S(2)}, u32[]{:S(2)}) %collective-permute-start.9) | collective-permute-done | bytes 131104 | tf_op jit(solution)/shard_map/ppermute | solution.py:51
  42.3 6.4 %second_pass.1 = (f32[2,256,256]{2,1,0:T(8,128)S(1)}, f32[2,256,128]{2,1,0:T(8,128)S(1)}, bf16[2,256,128]{2,1,0:T(8,128)(2,1)S(1)}, bf16[2,128,256]{2,1,0:T(8,12...) custom-call(s32[16]{0:T(128)S(1)} %pad_add_fusion.1.meta, ...), custom_call_target="tpu_custom_call" | custom-call | flops 2147483648 | tf_op jit(solution)/shard_map/second_pass/pallas_call | solution.py:464
  48.8 0.5 collective-permute-start.10
  49.3 2.2 %collective-permute-start.12 = (bf16[2,128,128]{2,1,0:T(8,128)(2,1)S(1)}, bf16[2,128,128]{2,1,0:T(8,128)(2,1)S(1)}, u32[]{:S(2)}, u32[]{:S(2)}) collective-permute-start(bf16[2,128,128]{2,1,0:T(8,128)(2,1)S(1)} %get-tuple-element.54), channel_id=1, source_target_pairs={{0,20},{4,24},{8,28},{12,16},{16,4},{20,8},{24,12},{28,0},{1,21},{... | collective-permute-start | bytes 196616 | tf_op jit(solution)/shard_map/ppermute | solution.py:51
  51.6 1.8 %collective-permute-start.16 = (bf16[3,64,256]{2,1,0:T(8,128)(2,1)S(1)}, bf16[3,64,256]{2,1,0:T(8,128)(2,1)S(1)}, u32[]{:S(2)}, u32[]{:S(2)}) collective-permute-start(bf16[3,64,256]{2,1,0:T(8,128)(2,1)S(1)} %get-tuple-element.58.rest_1_), channel_id=1, source_target_pairs={{0,8},{4,12},{8,0},{12,4},{16,24},{20,28},{24,16},{28,20},{1,9},{5... | collective-permute-start | bytes 294920 | tf_op jit(solution)/shard_map/ppermute | solution.py:56
  53.4 4.2 %collective-permute-done.12.from_diag = bf16[2,128,128]{2,1,0:T(8,128)(2,1)S(1)} collective-permute-done((bf16[2,128,128]{2,1,0:T(8,128)(2,1)S(1)}, bf16[2,128,128]{2,1,0:T(8,128)(2,1)S(1)}, u32[]{:S(2)}, u32[]{:S(2)}) %collective-permute-start.12) | collective-permute-done | bytes 65568 | tf_op jit(solution)/shard_map/ppermute | solution.py:51
  57.6 1.5 %collective-permute-done.11.from_above = bf16[2,128,256]{2,1,0:T(8,128)(2,1)S(1)} collective-permute-done((bf16[2,128,256]{2,1,0:T(8,128)(2,1)S(1)}, bf16[2,128,256]{2,1,0:T(8,128)(2,1)S(1)}, u32[]{:S(2)}, u32[]{:S(2)}) %collective-permute-start.11) | collective-permute-done | bytes 131104 | tf_op jit(solution)/shard_map/ppermute | solution.py:51
  59.5 1.2 %collective-permute-start.17 = (bf16[3,64,256]{2,1,0:T(8,128)(2,1)S(1)}, bf16[3,64,256]{2,1,0:T(8,128)(2,1)S(1)}, u32[]{:S(2)}, u32[]{:S(2)}) collective-permute-start(bf16[3,64,256]{2,1,0:T(8,128)(2,1)S(1)} %halve1.1.held), channel_id=1, source_target_pairs={{0,16},{4,20},{8,24},{12,28},{16,0},{20,4},{24,8},{28,12},{1,17},{... | collective-permute-start | bytes 294920 | tf_op jit(solution)/shard_map/ppermute | solution.py:56
  60.7 4.5 %collective-permute-done.15.second_came = bf16[2,128,256]{2,1,0:T(8,128)(2,1)S(1)} collective-permute-done((bf16[2,128,256]{2,1,0:T(8,128)(2,1)S(1)}, bf16[2,128,256]{2,1,0:T(8,128)(2,1)S(1)}, u32[]{:S(2)}, u32[]{:S(2)}) %collective-permute-start.15) | collective-permute-done | bytes 131104 | tf_op jit(solution)/shard_map/ppermute | solution.py:56
  65.4 1.8 %collective-permute-done.17.came = bf16[3,64,256]{2,1,0:T(8,128)(2,1)S(1)} collective-permute-done((bf16[3,64,256]{2,1,0:T(8,128)(2,1)S(1)}, bf16[3,64,256]{2,1,0:T(8,128)(2,1)S(1)}, u32[]{:S(2)}, u32[]{:S(2)}) %collective-permute-start.17) | collective-permute-done | bytes 98336 | tf_op jit(solution)/shard_map/ppermute | solution.py:56
  67.4 1.2 %collective-permute-start.18 = (bf16[2,128,256]{2,1,0:T(8,128)(2,1)S(1)}, bf16[2,128,256]{2,1,0:T(8,128)(2,1)S(1)}, u32[]{:S(2)}, u32[]{:S(2)}) collective-permute-start(bf16[2,128,256]{2,1,0:T(8,128)(2,1)S(1)} %get-tuple-element.61.first), channel_id=1, source_target_pairs={{0,2},{1,3},{2,0},{3,1},{4,6},{5,7},{6,4},{7,5},{8,10},{9,11},{10,... | collective-permute-start | bytes 393224 | tf_op jit(solution)/shard_map/ppermute | solution.py:56
  68.6 1.7 %collective-permute-start.19 = (bf16[2,128,256]{2,1,0:T(8,128)(2,1)S(1)}, bf16[2,128,256]{2,1,0:T(8,128)(2,1)S(1)}, u32[]{:S(2)}, u32[]{:S(2)}) collective-permute-start(bf16[2,128,256]{2,1,0:T(8,128)(2,1)S(1)} %get-tuple-element.62.second), channel_id=1, source_target_pairs={{0,1},{1,0},{2,3},{3,2},{4,5},{5,4},{6,7},{7,6},{8,9},{9,8},{10,11... | collective-permute-start | bytes 393224 | tf_op jit(solution)/shard_map/ppermute | solution.py:56
  70.4 1.3 %collective-permute-done.20 = bf16[2,64,256]{2,1,0:T(8,128)(2,1)S(1)} collective-permute-done((bf16[2,64,256]{2,1,0:T(8,128)(2,1)S(1)}, bf16[2,64,256]{2,1,0:T(8,128)(2,1)S(1)}, u32[]{:S(2)}, u32[]{:S(2)}) %collective-permute-start.20) | collective-permute-done | bytes 65568 | tf_op jit(solution)/shard_map/ppermute | solution.py:56
  71.7 1.2 %collective-permute-done.18.first_came = bf16[2,128,256]{2,1,0:T(8,128)(2,1)S(1)} collective-permute-done((bf16[2,128,256]{2,1,0:T(8,128)(2,1)S(1)}, bf16[2,128,256]{2,1,0:T(8,128)(2,1)S(1)}, u32[]{:S(2)}, u32[]{:S(2)}) %collective-permute-start.18) | collective-permute-done | bytes 131104 | tf_op jit(solution)/shard_map/ppermute | solution.py:56
  72.9 0.7 collective-permute-done.19.second_came
  73.6 1.2 %settle.1 = (f32[2,256,256]{2,1,0:T(8,128)}, f32[2,256,256]{2,1,0:T(8,128)}) custom-call(bf16[2,128,256]{2,1,0:T(8,128)(2,1)S(1)} %get-tuple-element.61.first, bf16[2,128,256]{2,1,0:T(8,128)(2,1)S(1)} %collective-permute-done.18.first_came, bf16[2,128,256]{2,1,0:T(8,128)(2,1)S(1)} %get-tuple-element.62.second, ...), custom_call_target="tpu_custom_call" | custom-call | flops 262144 | tf_op jit(solution)/shard_map/settle/pallas_call | solution.py:464
  74.8 0.9 %convert_add_fusion = f32[1,2,256,256]{3,2,1,0:T(8,128)} fusion(f32[1,2,256,256]{3,2,1,0:T(8,128)S(1)} %copy-done.8, bf16[1,2,128,256]{3,2,1,0:T(8,128)(2,1)S(1)} %bitcast.28, bf16[1,2,128,256]{3,2,1,0:T(8,128)(2,1)S(1)} %bitcast.31, pred[]{:T(512)} %eq.14), kind=kLoop, calls=%fused_computation | loop fusion | flops 1441792 | bytes 1310721 | tf_op jit(solution)/shard_map/add | solution.py:596
  (55 shorter events, 2.2 us)
Async XLA Ops:
  2.2 11.1 %collective-permute-start.3 = (s32[16]{0:T(128)S(1)}, s32[16]{0:T(128)S(1)}, u32[]{:S(2)}, u32[]{:S(2)}) collective-permute-start(s32[16]{0:T(128)S(1)} %pad_add_fusion.1.meta), channel_id=1, source_target_pairs={{0,16},{4,20},{8,24},{12,28},{16,0},{20,4},{24,8},{28,12},{1,17},{... | collective-permute-start | bytes 200 | tf_op jit(solution)/shard_map/ppermute | solution.py:51
  7.3 9.1 %collective-permute-start.2 = (bf16[2,128,128]{2,1,0:T(8,128)(2,1)S(1)}, bf16[2,128,128]{2,1,0:T(8,128)(2,1)S(1)}, u32[]{:S(2)}, u32[]{:S(2)}) collective-permute-start(bf16[2,128,128]{2,1,0:T(8,128)(2,1)S(1)} %slice.14), channel_id=1, source_target_pairs={{0,28},{4,16},{8,20},{12,24},{16,12},{20,0},{24,4},{28,8},{1,29},{... | collective-permute-start | bytes 196616 | tf_op jit(solution)/shard_map/ppermute | solution.py:51
  7.9 8.6 %collective-permute-start = (bf16[2,256,128]{2,1,0:T(8,128)(2,1)S(1)}, bf16[2,256,128]{2,1,0:T(8,128)(2,1)S(1)}, u32[]{:S(2)}, u32[]{:S(2)}) collective-permute-start(bf16[2,256,128]{2,1,0:T(8,128)(2,1)S(1)} %slice.12), channel_id=1, source_target_pairs={{0,12},{4,0},{8,4},{12,8},{16,28},{20,16},{24,20},{28,24},{1,13},{... | collective-permute-start | bytes 393224 | tf_op jit(solution)/shard_map/ppermute | solution.py:51
  9.1 10.3 %collective-permute-start.1 = (bf16[2,128,256]{2,1,0:T(8,128)(2,1)S(1)}, bf16[2,128,256]{2,1,0:T(8,128)(2,1)S(1)}, u32[]{:S(2)}, u32[]{:S(2)}) collective-permute-start(bf16[2,128,256]{2,1,0:T(8,128)(2,1)S(1)} %slice.13), channel_id=1, source_target_pairs={{0,16},{4,20},{8,24},{12,28},{16,0},{20,4},{24,8},{28,12},{1,17},{... | collective-permute-start | bytes 393224 | tf_op jit(solution)/shard_map/ppermute | solution.py:51
  13.3 6.1 %copy-start.2 = (s32[2,16]{1,0:T(2,128)}, s32[2,16]{1,0:T(2,128)S(1)}, u32[]{:S(2)}) copy-start(s32[2,16]{1,0:T(2,128)S(1)} %pad_add_fusion.rest_0_) | copy-start | bytes 388
  13.4 1.4 %collective-permute-start.5 = (s32[2,16]{1,0:T(2,128)S(1)}, s32[2,16]{1,0:T(2,128)S(1)}, u32[]{:S(2)}, u32[]{:S(2)}) collective-permute-start(s32[2,16]{1,0:T(2,128)S(1)} %pad_add_fusion.rest_0_), channel_id=1, source_target_pairs={{0,12},{4,0},{8,4},{12,8},{16,28},{20,16},{24,20},{28,24},{1,13},{... | collective-permute-start | bytes 392 | tf_op jit(solution)/shard_map/ppermute | solution.py:51
  13.4 3.1 %collective-permute-start.4 = (s32[2,16]{1,0:T(2,128)S(1)}, s32[2,16]{1,0:T(2,128)S(1)}, u32[]{:S(2)}, u32[]{:S(2)}) collective-permute-start(s32[2,16]{1,0:T(2,128)S(1)} %pad_add_fusion.rest_0_), channel_id=1, source_target_pairs={{0,4},{4,8},{8,12},{12,0},{16,20},{20,24},{24,28},{28,16},{1,5},{5... | collective-permute-start | bytes 392 | tf_op jit(solution)/shard_map/ppermute | solution.py:51
  14.7 4.8 %copy-start.4 = (s32[2,16]{1,0:T(2,128)}, s32[2,16]{1,0:T(2,128)S(1)}, u32[]{:S(2)}) copy-start(s32[2,16]{1,0:T(2,128)S(1)} %collective-permute-done.5.rest_2_) | copy-start | bytes 388
  16.5 3.0 %copy-start.6 = (s32[2,16]{1,0:T(2,128)}, s32[2,16]{1,0:T(2,128)S(1)}, u32[]{:S(2)}) copy-start(s32[2,16]{1,0:T(2,128)S(1)} %collective-permute-done.4.rest_1_) | copy-start | bytes 388
  19.5 14.3 %copy-start = (f32[8,128]{1,0:T(8,128)}, f32[8,128]{1,0:T(8,128)S(1)}, u32[]{:S(2)}) copy-start(f32[8,128]{1,0:T(8,128)S(1)} %broadcast_in_dim.6.flags.rest_13_) | copy-start | bytes 12292
  26.3 7.4 %collective-permute-start.6 = (bf16[2,384,128]{2,1,0:T(8,128)(2,1)S(1)}, bf16[2,384,128]{2,1,0:T(8,128)(2,1)S(1)}, u32[]{:S(2)}, u32[]{:S(2)}) collective-permute-start(bf16[2,384,128]{2,1,0:T(8,128)(2,1)S(1)} %get-tuple-element.39), channel_id=1, source_target_pairs={{0,4},{4,0},{8,12},{12,8},{16,20},{20,16},{24,28},{28,24},{1,5},{5... | collective-permute-start | bytes 589832 | tf_op jit(solution)/shard_map/ppermute | solution.py:56
  26.4 7.3 %collective-permute-start.7 = (bf16[2,384,128]{2,1,0:T(8,128)(2,1)S(1)}, bf16[2,384,128]{2,1,0:T(8,128)(2,1)S(1)}, u32[]{:S(2)}, u32[]{:S(2)}) collective-permute-start(bf16[2,384,128]{2,1,0:T(8,128)(2,1)S(1)} %get-tuple-element.40), channel_id=1, source_target_pairs={{0,0},{4,8},{8,4},{12,12},{16,16},{20,24},{24,20},{28,28},{1,1},{5... | collective-permute-start | bytes 589832 | tf_op jit(solution)/shard_map/ppermute | solution.py:65
  27.1 6.6 %collective-permute-start.8 = (bf16[2,128,128]{2,1,0:T(8,128)(2,1)S(1)}, bf16[2,128,128]{2,1,0:T(8,128)(2,1)S(1)}, u32[]{:S(2)}, u32[]{:S(2)}) collective-permute-start(bf16[2,128,128]{2,1,0:T(8,128)(2,1)S(1)} %get-tuple-element.41), channel_id=1, source_target_pairs={{0,16},{4,20},{8,24},{12,28},{16,0},{20,4},{24,8},{28,12},{1,17},{... | collective-permute-start | bytes 196616 | tf_op jit(solution)/shard_map/ppermute | solution.py:51
  33.7 0.7 copy-start.3
  33.7 0.7 copy-start.5
  33.8 0.7 copy-start.7
  33.9 8.4 %copy-start.1 = (f32[8,128]{1,0:T(8,128)S(1)}, f32[8,128]{1,0:T(8,128)}, u32[]{:S(2)}) copy-start(f32[8,128]{1,0:T(8,128)} %copy-done) | copy-start | bytes 12292
  33.9 8.4 %collective-permute-start.9 = (bf16[2,2,128,128]{3,2,1,0:T(8,128)(2,1)S(1)}, bf16[2,2,128,128]{3,2,1,0:T(8,128)(2,1)S(1)}, u32[]{:S(2)}, u32[]{:S(2)}) collective-permute-start(bf16[2,2,128,128]{3,2,1,0:T(8,128)(2,1)S(1)} %between.1.rest_3_), channel_id=1, source_target_pairs={{0,16},{4,20},{8,24},{12,28},{16,0},{20,4},{24,8},{28,12},{1,17},{... | collective-permute-start | bytes 393224 | tf_op jit(solution)/shard_map/ppermute | solution.py:51
  48.7 2.8 %collective-permute-start.13 = (bf16[3,128,256]{2,1,0:T(8,128)(2,1)S(1)}, bf16[3,128,256]{2,1,0:T(8,128)(2,1)S(1)}, u32[]{:S(2)}, u32[]{:S(2)}) collective-permute-start(bf16[3,128,256]{2,1,0:T(8,128)(2,1)S(1)} %get-tuple-element.56), channel_id=1, source_target_pairs={{0,4},{4,0},{8,12},{12,8},{16,20},{20,16},{24,28},{28,24},{1,5},{5... | collective-permute-start | bytes 589832 | tf_op jit(solution)/shard_map/ppermute | solution.py:56
  48.8 8.9 %collective-permute-start.10 = (bf16[2,256,128]{2,1,0:T(8,128)(2,1)S(1)}, bf16[2,256,128]{2,1,0:T(8,128)(2,1)S(1)}, u32[]{:S(2)}, u32[]{:S(2)}) collective-permute-start(bf16[2,256,128]{2,1,0:T(8,128)(2,1)S(1)} %get-tuple-element.52), channel_id=1, source_target_pairs={{0,4},{4,8},{8,12},{12,0},{16,20},{20,24},{24,28},{28,16},{1,5},{5... | collective-permute-start | bytes 393224 | tf_op jit(solution)/shard_map/ppermute | solution.py:51
  49.3 9.9 %collective-permute-start.11 = (bf16[2,128,256]{2,1,0:T(8,128)(2,1)S(1)}, bf16[2,128,256]{2,1,0:T(8,128)(2,1)S(1)}, u32[]{:S(2)}, u32[]{:S(2)}) collective-permute-start(bf16[2,128,256]{2,1,0:T(8,128)(2,1)S(1)} %get-tuple-element.53), channel_id=1, source_target_pairs={{0,16},{4,20},{8,24},{12,28},{16,0},{20,4},{24,8},{28,12},{1,17},{... | collective-permute-start | bytes 393224 | tf_op jit(solution)/shard_map/ppermute | solution.py:51
  49.3 8.4 %collective-permute-start.12 = (bf16[2,128,128]{2,1,0:T(8,128)(2,1)S(1)}, bf16[2,128,128]{2,1,0:T(8,128)(2,1)S(1)}, u32[]{:S(2)}, u32[]{:S(2)}) collective-permute-start(bf16[2,128,128]{2,1,0:T(8,128)(2,1)S(1)} %get-tuple-element.54), channel_id=1, source_target_pairs={{0,20},{4,24},{8,28},{12,16},{16,4},{20,8},{24,12},{28,0},{1,21},{... | collective-permute-start | bytes 196616 | tf_op jit(solution)/shard_map/ppermute | solution.py:51
  51.6 7.8 %collective-permute-start.16 = (bf16[3,64,256]{2,1,0:T(8,128)(2,1)S(1)}, bf16[3,64,256]{2,1,0:T(8,128)(2,1)S(1)}, u32[]{:S(2)}, u32[]{:S(2)}) collective-permute-start(bf16[3,64,256]{2,1,0:T(8,128)(2,1)S(1)} %get-tuple-element.58.rest_1_), channel_id=1, source_target_pairs={{0,8},{4,12},{8,0},{12,4},{16,24},{20,28},{24,16},{28,20},{1,9},{5... | collective-permute-start | bytes 294920 | tf_op jit(solution)/shard_map/ppermute | solution.py:56
  59.3 6.0 %collective-permute-start.15 = (bf16[2,128,256]{2,1,0:T(8,128)(2,1)S(1)}, bf16[2,128,256]{2,1,0:T(8,128)(2,1)S(1)}, u32[]{:S(2)}, u32[]{:S(2)}) collective-permute-start(bf16[2,128,256]{2,1,0:T(8,128)(2,1)S(1)} %get-tuple-element.60.second), channel_id=1, source_target_pairs={{0,2},{1,3},{2,0},{3,1},{4,6},{5,7},{6,4},{7,5},{8,10},{9,11},{10,... | collective-permute-start | bytes 393224 | tf_op jit(solution)/shard_map/ppermute | solution.py:56
  59.4 15.4 %copy-start.8 = (f32[1,2,256,256]{3,2,1,0:T(8,128)S(1)}, f32[1,2,256,256]{3,2,1,0:T(8,128)}, u32[]{:S(2)}) copy-start(f32[1,2,256,256]{3,2,1,0:T(8,128)} %param.10) | copy-start | bytes 1572868
  59.4 6.0 %collective-permute-start.14 = (bf16[2,128,256]{2,1,0:T(8,128)(2,1)S(1)}, bf16[2,128,256]{2,1,0:T(8,128)(2,1)S(1)}, u32[]{:S(2)}, u32[]{:S(2)}) collective-permute-start(bf16[2,128,256]{2,1,0:T(8,128)(2,1)S(1)} %get-tuple-element.59.rest_0_.first), channel_id=1, source_target_pairs={{0,1},{1,0},{2,3},{3,2},{4,5},{5,4},{6,7},{7,6},{8,9},{9,8},{10,11... | collective-permute-start | bytes 393224 | tf_op jit(solution)/shard_map/ppermute | solution.py:56
  59.5 7.7 %collective-permute-start.17 = (bf16[3,64,256]{2,1,0:T(8,128)(2,1)S(1)}, bf16[3,64,256]{2,1,0:T(8,128)(2,1)S(1)}, u32[]{:S(2)}, u32[]{:S(2)}) collective-permute-start(bf16[3,64,256]{2,1,0:T(8,128)(2,1)S(1)} %halve1.1.held), channel_id=1, source_target_pairs={{0,16},{4,20},{8,24},{12,28},{16,0},{20,4},{24,8},{28,12},{1,17},{... | collective-permute-start | bytes 294920 | tf_op jit(solution)/shard_map/ppermute | solution.py:56
  67.3 4.3 %collective-permute-start.20 = (bf16[2,64,256]{2,1,0:T(8,128)(2,1)S(1)}, bf16[2,64,256]{2,1,0:T(8,128)(2,1)S(1)}, u32[]{:S(2)}, u32[]{:S(2)}) collective-permute-start(bf16[2,64,256]{2,1,0:T(8,128)(2,1)S(1)} %get-tuple-element.66), channel_id=1, source_target_pairs={{0,8},{4,12},{8,0},{12,4},{16,24},{20,28},{24,16},{28,20},{1,9},{5... | collective-permute-start | bytes 196616 | tf_op jit(solution)/shard_map/ppermute | solution.py:56
  67.4 5.5 %collective-permute-start.18 = (bf16[2,128,256]{2,1,0:T(8,128)(2,1)S(1)}, bf16[2,128,256]{2,1,0:T(8,128)(2,1)S(1)}, u32[]{:S(2)}, u32[]{:S(2)}) collective-permute-start(bf16[2,128,256]{2,1,0:T(8,128)(2,1)S(1)} %get-tuple-element.61.first), channel_id=1, source_target_pairs={{0,2},{1,3},{2,0},{3,1},{4,6},{5,7},{6,4},{7,5},{8,10},{9,11},{10,... | collective-permute-start | bytes 393224 | tf_op jit(solution)/shard_map/ppermute | solution.py:56
  68.6 5.0 %collective-permute-start.19 = (bf16[2,128,256]{2,1,0:T(8,128)(2,1)S(1)}, bf16[2,128,256]{2,1,0:T(8,128)(2,1)S(1)}, u32[]{:S(2)}, u32[]{:S(2)}) collective-permute-start(bf16[2,128,256]{2,1,0:T(8,128)(2,1)S(1)} %get-tuple-element.62.second), channel_id=1, source_target_pairs={{0,1},{1,0},{2,3},{3,2},{4,5},{5,4},{6,7},{7,6},{8,9},{9,8},{10,11... | collective-permute-start | bytes 393224 | tf_op jit(solution)/shard_map/ppermute | solution.py:56
  71.7 3.1 %collective-permute-start.21 = (bf16[2,128,256]{2,1,0:T(8,128)(2,1)S(1)}, bf16[2,128,256]{2,1,0:T(8,128)(2,1)S(1)}, u32[]{:S(2)}, u32[]{:S(2)}) collective-permute-start(bf16[2,128,256]{2,1,0:T(8,128)(2,1)S(1)} %maximum_select_fusion.1), channel_id=1, source_target_pairs={{0,4},{4,0},{8,12},{12,8},{16,20},{20,16},{24,28},{28,24},{1,5},{5... | collective-permute-start | bytes 393224 | tf_op jit(solution)/shard_map/ppermute | solution.py:56

commit v3 on v2

--- a/solution.py
+++ b/solution.py
@@ -20,7 +20,7 @@
 CH = 32
 META = 16
 COUNT = 2 * SLOTS
-HAS_LEFT, HAS_RIGHT, HAS_ABOVE, HAS_BELOW, ODD, BIT1 = range(6)
+HAS_LEFT, HAS_RIGHT, HAS_ABOVE, HAS_BELOW, ODD = range(5)
 
 penalty = 0.5
 smoothing = 0.05
@@ -65,24 +65,18 @@
     return lax.ppermute(value, "tile", [(i, i ^ 3 if i % TGW in (1, 2) else i) for i in range(n)])
 
 
-def scan_sums(parts, sums):
+def scan_sums(parts):
     n = lax.axis_size("scan")
-    change = None
     if not is_power(n):
-        return [v for part in parts for v in (lax.psum(part, "scan"), jnp.zeros_like(part))], change
+        return [v for part in parts for v in (lax.psum(part, "scan"), jnp.zeros_like(part))]
     bits = [1 << k for k in range(n.bit_length() - 1)]
     for k in range(len(bits)):
         came = [swapped(parts[p], "scan", bits[(k + p) % len(bits)]) for p in range(2)]
         pairs = [parts[0], came[0], parts[1], came[1]]
         if k < len(bits) - 1:
             outs = [(parts[0].shape, bf16)] * 2
-            if sums is not None and k == 0:
-                last = swapped(sums, "tile", 4)
-                outs = outs + [((2,) + sums.shape[1:], bf16)]
-                *parts, change = call(mix_and_update, "mix_and_update", outs)(*pairs, sums, last)
-            else:
-                parts = call(mix, f"mix{k}", outs)(*pairs)
-    return pairs, change
+            parts = call(mix, f"mix{k}", outs)(*pairs)
+    return pairs
 
 
 def doubled(index, change, bit):
@@ -198,7 +192,7 @@
 
 
 def first_pass(
-    two, meta, flags, right, below, diag, ext0, acc0, probe, fwd_h, bwd_h, amps_h, *rest,
+    two, meta, flags, right, below0, below1, diag, ext0, acc0, probe, fwd_h, bwd_h, amps_h, *rest,
 ):
     ext, acc, pnum, side, inner, *mids, fwd, bwd, amps, sems, win, X, Y, W = rest[3:]
     copies = fetch([(fwd_h, fwd), (bwd_h, bwd), (amps_h, amps)], sems)
@@ -207,8 +201,7 @@
     ext[:, 2, :TS, :] = right[...].astype(f32) * has_right
     ext[:, 2, TS:, :] = diag[...].astype(f32) * (has_right * has_below)
     for j in range(2):
-        cols = slice(j * L, (j + 1) * L)
-        ext[:, j, TS:, :] = below[:, :, cols].astype(f32) * has_below
+        ext[:, j, TS:, :] = (below0, below1)[j][...].astype(f32) * has_below
     pnum[...] = jnp.zeros_like(pnum)
     for copy in copies:
         copy.wait()
@@ -296,9 +289,9 @@
 
 
 def second_pass(
-    meta, flags, right, below, diag, acc1, side, inner, mid_above, mid_below, from_above, from_below,
+    meta, flags, right, below0, below1, diag, acc1, side, inner, mid_above, mid_below, from_above, from_below,
     weight, pnum1, own, dual, probe, amps, fwd, bwd,
-    base, shrink, to_right, to_below, to_diag, pnum, to_swap,
+    base, shrink, to_right, lower, to_below, pnum, to_swap,
     partial, ext, acc, win, X, Y, W,
 ):
     has_right = flags[HAS_RIGHT : HAS_RIGHT + 1, :]
@@ -329,7 +322,7 @@
                     if k < TS:
                         est = right[ch, rows, :].astype(f32) + step
                     elif j < 2:
-                        est = below[ch, k - TS : k - TS + 64, cols].astype(f32) + step
+                        est = (below0, below1)[j][ch, k - TS : k - TS + 64, :].astype(f32) + step
                     else:
                         est = diag[ch, k - TS : k - TS + 64, :].astype(f32) + step
                     if j == 2:
@@ -342,15 +335,15 @@
     def _(p):
         visit_pair(p, meta, ext, probe, amps, fwd, bwd, acc, pnum, win, X, Y, W)
 
-    to_diag[...] = acc[:, 2, TS:, :].astype(bf16)
-    to_right[...] = acc[:, 2, :TS, :].astype(bf16)
+    to_right[...] = acc[:, 2].astype(bf16)
+    to_below[...] = acc[:, 1, TS:, :].astype(bf16)
+    lower[...] = acc[:, 0, TS:, :]
     odd = flags[ODD : ODD + 1, :1] > 0.0
     for ch in range(3):
         lo, hi = pnum[ch, : PS // 2, :], pnum[ch, PS // 2 :, :]
         to_swap[ch] = jnp.where(odd, lo, hi).astype(bf16)
     for j in range(2):
         cols = slice(j * L, (j + 1) * L)
-        to_below[:, :, cols] = acc[:, j, TS:, :].astype(bf16)
         for k in range(0, TS, 64):
             rows = slice(k, k + 64)
             over = 1.0 / (weight[j, rows, :] + penalty)
@@ -362,28 +355,25 @@
                 base[ch, rows, cols] = est + held + (acc[ch, j, rows, :] + pull) * over
 
 
-def halve(k, flags, sums, came, *rest):
-    outs = rest[-1:] if k == 1 else rest[-2:]
-    total = []
+def halve(flags, sums, came, *rest):
+    odd = flags[ODD : ODD + 1, :1] > 0.0
     for ch in range(3):
-        kept = sums[ch]
-        if k == 0:
-            lo, hi = kept[: PS // 2], kept[PS // 2 :]
-            kept = jnp.where(flags[ODD : ODD + 1, :1] > 0.0, hi, lo)
-        total.append(kept + came[ch].astype(f32))
-    if k == 1:
-        for ch in range(3):
-            outs[0][ch] = total[ch].astype(bf16)
-        return
-    up = flags[BIT1 : BIT1 + 1, :1] > 0.0
-    half = came.shape[1] // 2
+        lo, hi = sums[ch, : PS // 2, :], sums[ch, PS // 2 :, :]
+        rest[-1][ch] = (jnp.where(odd, hi, lo) + came[ch].astype(f32)).astype(bf16)
+
+
+def add(held, came, *rest):
     for ch in range(3):
-        lo, hi = total[ch][:half], total[ch][half:]
-        outs[0][ch] = jnp.where(up, hi, lo)
-        outs[1][ch] = jnp.where(up, lo, hi).astype(bf16)
-
-
-def finish_estimate(flags, base, shrink, from_left, from_above, from_diag, *rest):
+        rest[-1][ch] = (held[ch].astype(f32) + came[ch].astype(f32)).astype(bf16)
+
+
+def add_rim(flags, rim, from_left, *rest):
+    has_left = flags[HAS_LEFT : HAS_LEFT + 1, :]
+    for ch in range(2):
+        rest[-1][ch] = (rim[ch] + from_left[ch, TS:, :].astype(f32) * has_left).astype(bf16)
+
+
+def finish_estimate(flags, base, shrink, from_left, above0, above1, *rest):
     combined, parts = rest[-3], rest[-2:]
     has_left = flags[HAS_LEFT : HAS_LEFT + 1, :]
     has_above = flags[HAS_ABOVE : HAS_ABOVE + 1, :]
@@ -397,10 +387,8 @@
                 if j == 0:
                     came = from_left[ch, rows, :].astype(f32) * has_left
                 if k < OVER:
-                    above = from_above[ch, rows, cols].astype(f32) * has_above
+                    above = (above0, above1)[j][ch, rows, :].astype(f32) * has_above
                     came = above if came is None else came + above
-                    if j == 0:
-                        came = came + from_diag[ch, rows, :].astype(f32) * (has_left * has_above)
                 if came is not None:
                     total = total + came * shrink[j, rows, :]
                 combined[ch, rows, cols] = total
@@ -418,12 +406,11 @@
     mixed(*refs[:4], refs[-2:])
 
 
-def mix_and_update(first, first_came, second, second_came, held, came, *outs):
-    mixed(first, first_came, second, second_came, outs)
+def update(held, came, *rest):
     total = [held[ch].astype(f32) + came[ch].astype(f32) for ch in range(3)]
     over = probe_step * lax.rsqrt(total[2] + 1.0)
     for ch in range(2):
-        outs[2][ch] = (total[ch] * over).astype(bf16)
+        rest[-1][ch] = (total[ch] * over).astype(bf16)
 
 
 def settle(groups, first, first_came, second, second_came, combined, *rest):
@@ -511,20 +498,21 @@
     measured = ((SLOTS, PS, PS), bf16)
 
     rounded = own.astype(bf16)
-    below = shifted(rounded[:, :OVER, :], -1, 0)
-    diag = shifted(rounded[:, :OVER, :OVER], -1, -1)
+    below = [shifted(rounded[:, :OVER, j * L : (j + 1) * L], -1, 0) for j in range(2)]
     right = shifted(rounded[:, :, :OVER], 0, -1)
+    below.append(shifted(below[0], 0, -1))
 
     height = n // TGW
     two = height == 2
     row, col = index // TGW, index % TGW
     flags = [col > 0, col < TGW - 1, row > 0, row < height - 1]
-    flags = flags + [(index // bit) % 2 == 1 for bit in (1, 2)] + [col < 0] * 2
+    flags = flags + [index % 2 == 1] + [col < 0] * 3
     flags = jnp.broadcast_to(jnp.stack(flags).astype(f32)[:, None], (8, L))
     meta = jnp.concatenate(
         [offsets[0, 0].reshape(COUNT), counts[0], jnp.zeros((META - COUNT - 1,), jnp.int32)]
     )
-    column = [meta, shifted(meta, 1, 0)] if two else [meta, shifted(meta, 1, 0), shifted(meta, -1, 0)]
+    _, meta = lax.optimization_barrier((rounded, meta))
+    column = [meta, shifted(meta, 1, 0)] + ([] if two else [shifted(meta, -1, 0)])
     column = jnp.stack(column)
     metas = [column, shifted(column, 0, 1), shifted(column, 0, -1)]
 
@@ -537,8 +525,8 @@
     ext, acc, pnum, side, inner, *mids = call(
         functools.partial(first_pass, two), "first_pass",
         [WIDE, WIDE, SUMS, ((2, SPAN, L), bf16), ((2, SPAN, L), bf16)] + [rim] * (1 if two else 2),
-        [TABLE, TABLE, measured, None] + WORK, 1, 6, 3, aliases={5: 0, 6: 1}, flops=PASS,
-    )(meta, flags, right, below, diag, *staged, fwd, bwd, amps, *metas)
+        [TABLE, TABLE, measured, None] + WORK, 1, 6, 3, aliases={6: 0, 7: 1}, flops=PASS,
+    )(meta, flags, right, *below, *staged, fwd, bwd, amps, *metas)
     side = swapped(side, "tile", 1)
     inner = inner_swapped(inner)
 
@@ -549,47 +537,47 @@
     mid_above, mid_below = down_and_up(mids)
     rims = call(
         functools.partial(between, two), "between", [((2, 2, OVER, L), bf16)] * (1 if two else 2)
-    )(flags, acc, side, inner, pnum, right, below, diag, mid_above, mid_below)
+    )(flags, acc, side, inner, pnum, right, *below, mid_above, mid_below)
     from_above, from_below = down_and_up(rims)
     weight, *inputs = call(
         functools.partial(weigh, two), "weigh",
         [((3, SPAN, L), f32), PLANES, PLANES, PLANES, measured, TABLE, TABLE],
         [None, ((2, PS, L), f32), ((3, SPAN + 2 * OVER, L), f32), pltpu.SMEM((8, L), f32)],
         len(metas), 7, 7, held=True,
-    )(*metas, rims[0], acc, side, inner, pnum, right, below, diag, mid_above, mid_below, flags, *inputs)
+    )(*metas, rims[0], acc, side, inner, pnum, right, *below, mid_above, mid_below, flags, *inputs)
     weight, *inputs = [pinned(v) for v in (weight, *inputs)]
 
-    base, shrink, to_right, to_below, to_diag, pnum, to_swap = call(
+    base, shrink, to_right, rim, to_below, pnum, to_swap = call(
         second_pass, "second_pass",
-        [PLANES, ((2, TS, L), f32), ((2, TS, OVER), bf16), ((2, OVER, TS), bf16),
-         ((2, OVER, OVER), bf16), SUMS, ((3, PS // 2, PS), bf16)],
+        [PLANES, ((2, TS, L), f32), ((2, SPAN, L), bf16), ((2, OVER, L), f32), ((2, OVER, L), bf16),
+         SUMS, ((3, PS // 2, PS), bf16)],
         [PLANES, WIDE, WIDE] + WORK, 1, flops=PASS,
-    )(meta, flags, right, below, diag, acc, side, inner, mid_above, mid_below, from_above,
+    )(meta, flags, right, *below, acc, side, inner, mid_above, mid_below, from_above,
       from_below, weight, pnum, *inputs)
-    from_above = shifted(to_below, 1, 0)
-    from_diag = shifted(to_diag, 1, 1)
     from_left = shifted(to_right, 0, 1)
-
-    def halved(k, sums, send, *after):
-        came = swapped(send, "tile", 1 << k)
-        rows = came.shape[1]
-        outs = [((3, rows // 2, PS), f32), ((3, rows // 2, PS), bf16)]
-        if k == 1:
-            outs = [((3, rows, PS), bf16)]
-        return call(functools.partial(halve, k), f"halve{k}", outs)(flags, sums, came, *after)
-
-    eight = n == 8 and lax.axis_size("scan") in (4, 8)
-    first = halved(0, pnum, to_swap, base, shrink) if eight else []
+    above1 = shifted(to_below, 1, 0)
+    (to_below,) = call(add_rim, "add_rim", [((2, OVER, L), bf16)])(flags, rim, from_left, base, shrink)
+    above0 = shifted(to_below, 1, 0)
+
+    eight = n == 8
+    half = [((3, PS // 2, PS), bf16)]
+    if eight:
+        (sums,) = call(halve, "halve", half)(flags, pnum, swapped(to_swap, "tile", 1), base, shrink)
+        came = swapped(sums, "tile", 2)
     combined, *parts = call(
         finish_estimate, "finish_estimate", [PLANES] + [((2, TS // 2, TS), bf16)] * 2
-    )(flags, base, shrink, from_left, from_above, from_diag, *first)
-    sums = halved(1, *first, parts[0])[0] if eight else None
-    pairs, change = scan_sums(parts, sums)
+    )(flags, base, shrink, from_left, above0, above1, *([sums] if eight else []))
+    if eight:
+        (sums,) = call(add, "add", half)(sums, came, parts[0])
+        came = swapped(sums, "tile", 4)
+    pairs = scan_sums(parts)
+    if eight:
+        (change,) = call(update, "update", [((2, PS // 2, PS), bf16)])(sums, came, pairs[1])
     settled, dual_new = call(
         functools.partial(settle, lax.axis_size("scan")), "settle", [PLANES] * 2
     )(*pairs, combined)
     if eight:
-        change = doubled(index, doubled(index, change, 2), 1).astype(f32)
+        change = doubled(index, change, 1).astype(f32)
     else:
         total = lax.psum(pnum, "tile")
         change = probe_step * total[0:2] / jnp.sqrt(total[2] + 1.0)

time: 76.3 us -> 72.2 us (0.946)
  starting transfers between devices: 19 us -> 14.9 us
  waiting for transfers between devices: 31.9 us -> 32.8 us
    ppermute x11 -> x12, starting transfers between devices: 11.9 us -> 9.6 us  [shifted(): return lax.ppermute(value, 'tile', pairs)]
    ppermute x10 -> x9, starting transfers between devices: 6.41 us -> 4.59 us  [swapped(): return lax.ppermute(value, axis, [(i, i ^ bit) for i in range(n)])]
    ppermute x11 -> x12, waiting for transfers between devices: 22.3 us -> 23.1 us  [shifted(): return lax.ppermute(value, 'tile', pairs)]
    pallas_call x10 -> x12, Pallas kernels: 19.5 us -> 19.3 us  [run(): pl.pallas_call(body, in_specs=[S] * scalars + [V] * near + [H] * far, out...]
    ppermute x10 -> x9, waiting for transfers between devices: 9.59 us -> 9.66 us  [swapped(): return lax.ppermute(value, axis, [(i, i ^ bit) for i in range(n)])]
  transfers between devices with their start and end apart: 22 -> 22, of which waited for: 13 -> 13; matrix products, arithmetic and copies ran while one was open for 2% -> 1% of each run, Pallas kernels for 8% -> 8%
where the time goes in v3:
time: 72.2 us; the launch traced here: 71.8 us
  waiting for transfers between devices  32.8 us (45%)
  Pallas kernels  19.3 us (27%)
  starting transfers between devices  14.9 us (21%)
  other arithmetic  2.03 us (3%)
  between operations  1.53 us (2%)
  local copies, waits for them, and re-layouts  1.37 us (2%)
    ppermute x12, waiting for transfers between devices, shifted(): return lax.ppermute(value, 'tile', pairs)  23.1 us
    pallas_call x12, Pallas kernels, run(): pl.pallas_call(body, in_specs=[S] * scalars + [V] * near + [H] * far, out...  19.3 us
    ppermute x9, waiting for transfers between devices, swapped(): return lax.ppermute(value, axis, [(i, i ^ bit) for i in range(n)])  9.66 us
    ppermute x12, starting transfers between devices, shifted(): return lax.ppermute(value, 'tile', pairs)  9.6 us
    ppermute x9, starting transfers between devices, swapped(): return lax.ppermute(value, axis, [(i, i ^ bit) for i in range(n)])  4.59 us
  transfers between devices with their start and end apart: 22, of which 13 were waited for; matrix products, arithmetic and copies ran while one was open for 1% of the time, Pallas kernels for 8%

profile of v3, /device:TPU:0, one launch (start us, length us, event | category | flops | bytes accessed | tf_op | source)
XLA Modules:
  0.0 71.8 jit_solution(3126207442910242982)
XLA Ops:
  0.6 1.1 %bitcast_convert_fusion = bf16[2,256,256]{2,1,0:T(8,128)(2,1)S(1)} fusion(f32[1,2,256,256]{3,2,1,0:T(8,128)} %param.8), kind=kLoop, calls=%fused_computation.4 | loop fusion | flops 131072 | bytes 786432 | tf_op jit(solution)/shard_map/convert_element_type | solution.py:500
  1.8 4.1 %collective-permute-start.1 = (bf16[2,128,128]{2,1,0:T(8,128)(2,1)S(1)}, bf16[2,128,128]{2,1,0:T(8,128)(2,1)S(1)}, u32[]{:S(2)}, u32[]{:S(2)}) collective-permute-start(bf16[2,128,128]{2,1,0:T(8,128)(2,1)S(1)} %get-tuple-element.64), channel_id=1, source_target_pairs={{0,16},{4,20},{8,24},{12,28},{16,0},{20,4},{24,8},{28,12},{1,17},{... | collective-permute-start | bytes 196616 | tf_op jit(solution)/shard_map/ppermute | solution.py:51
  5.9 0.8 %collective-permute-start = (bf16[2,256,128]{2,1,0:T(8,128)(2,1)S(1)}, bf16[2,256,128]{2,1,0:T(8,128)(2,1)S(1)}, u32[]{:S(2)}, u32[]{:S(2)}) collective-permute-start(bf16[2,256,128]{2,1,0:T(8,128)(2,1)S(1)} %slice.12), channel_id=1, source_target_pairs={{0,12},{4,0},{8,4},{12,8},{16,28},{20,16},{24,20},{28,24},{1,13},{... | collective-permute-start | bytes 393224 | tf_op jit(solution)/shard_map/ppermute | solution.py:51
  7.6 0.3 collective-permute-start.4
  7.9 2.6 %collective-permute-start.2 = (bf16[2,128,128]{2,1,0:T(8,128)(2,1)S(1)}, bf16[2,128,128]{2,1,0:T(8,128)(2,1)S(1)}, u32[]{:S(2)}, u32[]{:S(2)}) collective-permute-start(bf16[2,128,128]{2,1,0:T(8,128)(2,1)S(1)} %get-tuple-element.63), channel_id=1, source_target_pairs={{0,16},{4,20},{8,24},{12,28},{16,0},{20,4},{24,8},{28,12},{1,17},{... | collective-permute-start | bytes 196616 | tf_op jit(solution)/shard_map/ppermute | solution.py:51
  10.6 1.4 %stage.1 = (f32[2,3,384,128]{3,2,1,0:T(8,128)S(1)}, f32[2,3,384,128]{3,2,1,0:T(8,128)S(1)}, f32[2,256,256]{2,1,0:T(8,128)S(1)}) custom-call(f32[2,256,256]{2,1,0:T(8,128)} %bitcast.23, f32[2,256,256]{2,1,0:T(8,128)} %bitcast.25, f32[2,256,256]{2,1,0:T(8,128)} %bitcast.21), custom_call_target="tpu_custom_call" | custom-call | flops 720896 | bytes 1572864 | tf_op jit(solution)/shard_map/stage/pallas_call | solution.py:451
  12.0 0.4 collective-permute-start.3
  12.5 0.6 collective-permute-start.6
  13.1 1.3 %collective-permute-done.6.rest_2_ = s32[2,16]{1,0:T(2,128)S(1)} collective-permute-done((s32[2,16]{1,0:T(2,128)S(1)}, s32[2,16]{1,0:T(2,128)S(1)}, u32[]{:S(2)}, u32[]{:S(2)}) %collective-permute-start.6) | collective-permute-done | bytes 160 | tf_op jit(solution)/shard_map/ppermute | solution.py:51
  14.4 1.7 %collective-permute-done.5.rest_1_ = s32[2,16]{1,0:T(2,128)S(1)} collective-permute-done((s32[2,16]{1,0:T(2,128)S(1)}, s32[2,16]{1,0:T(2,128)S(1)}, u32[]{:S(2)}, u32[]{:S(2)}) %collective-permute-start.5) | collective-permute-done | bytes 160 | tf_op jit(solution)/shard_map/ppermute | solution.py:51
  16.2 0.5 copy-done.6
  16.7 6.8 %first_pass.1 = (f32[2,3,384,128]{3,2,1,0:T(8,128)S(1)}, f32[2,3,384,128]{3,2,1,0:T(8,128)S(1)}, f32[3,256,256]{2,1,0:T(8,128)S(1)}, bf16[2,384,128]{2,1,0:T(8,1...) custom-call(s32[16]{0:T(128)S(1)} %pad_add_fusion.1.meta, ...), custom_call_target="tpu_custom_call", output_to_operand_aliasing={{0}: (6, {}), {1}: (7, {})} | custom-call | flops 2147483648 | bytes 1573248 | tf_op jit(solution)/shard_map/first_pass/pallas_call | solution.py:451
  23.5 0.7 collective-permute-start.8
  24.3 5.7 %collective-permute-done.9.rest_5_.rest_6_.rest_12_.rest_13_.mid_above.mid_below = bf16[2,128,128]{2,1,0:T(8,128)(2,1)S(1)} collective-permute-done((bf16[2,128,128]{2,1,0:T(8,128)(2,1)S(1)}, bf16[2,128,128]{2,1,0:T(8,128)(2,1)S(1)}, u32[]{:S(2)}, u32[]{:S(2)}) %collective-permute-start.9) | collective-permute-done | bytes 65568 | tf_op jit(solution)/shard_map/ppermute | solution.py:51
  30.2 0.5 copy-done.3
  30.7 3.0 %weigh.1 = (f32[3,384,128]{2,1,0:T(8,128)S(1)}, f32[2,256,256]{2,1,0:T(8,128)S(1)}, f32[2,256,256]{2,1,0:T(8,128)S(1)}, f32[2,256,256]{2,1,0:T(8,128)S(1)}, bf16...) custom-call(s32[2,16]{1,0:T(2,128)S(1)} %copy-done.3, ...), custom_call_target="tpu_custom_call" | custom-call | flops 1327104 | bytes 3149824 | tf_op jit(solution)/shard_map/weigh/pallas_call | solution.py:451
  33.8 5.0 %collective-permute-done.10.from_above.from_below = bf16[2,2,128,128]{3,2,1,0:T(8,128)(2,1)S(1)} collective-permute-done((bf16[2,2,128,128]{3,2,1,0:T(8,128)(2,1)S(1)}, bf16[2,2,128,128]{3,2,1,0:T(8,128)(2,1)S(1)}, u32[]{:S(2)}, u32[]{:S(2)}) %collective-permute-start.10) | collective-permute-done | bytes 131104 | tf_op jit(solution)/shard_map/ppermute | solution.py:51
  38.7 6.4 %second_pass.1 = (f32[2,256,256]{2,1,0:T(8,128)S(1)}, f32[2,256,128]{2,1,0:T(8,128)S(1)}, bf16[2,384,128]{2,1,0:T(8,128)(2,1)S(1)}, f32[2,128,128]{2,1,0:T(8,128...) custom-call(s32[16]{0:T(128)S(1)} %pad_add_fusion.1.meta, ...), custom_call_target="tpu_custom_call" | custom-call | flops 2147483648 | tf_op jit(solution)/shard_map/second_pass/pallas_call | solution.py:451
  45.2 0.5 collective-permute-start.11
  45.7 0.9 %collective-permute-done.14.came = bf16[3,128,256]{2,1,0:T(8,128)(2,1)S(1)} collective-permute-done((bf16[3,128,256]{2,1,0:T(8,128)(2,1)S(1)}, bf16[3,128,256]{2,1,0:T(8,128)(2,1)S(1)}, u32[]{:S(2)}, u32[]{:S(2)}) %collective-permute-start.14) | collective-permute-done | bytes 196640 | tf_op jit(solution)/shard_map/ppermute | solution.py:56
  47.0 3.3 %collective-permute-done.11.from_left = bf16[2,384,128]{2,1,0:T(8,128)(2,1)S(1)} collective-permute-done((bf16[2,384,128]{2,1,0:T(8,128)(2,1)S(1)}, bf16[2,384,128]{2,1,0:T(8,128)(2,1)S(1)}, u32[]{:S(2)}, u32[]{:S(2)}) %collective-permute-start.11) | collective-permute-done | bytes 196640 | tf_op jit(solution)/shard_map/ppermute | solution.py:51
  50.5 4.4 %collective-permute-done.13.above1 = bf16[2,128,128]{2,1,0:T(8,128)(2,1)S(1)} collective-permute-done((bf16[2,128,128]{2,1,0:T(8,128)(2,1)S(1)}, bf16[2,128,128]{2,1,0:T(8,128)(2,1)S(1)}, u32[]{:S(2)}, u32[]{:S(2)}) %collective-permute-start.13) | collective-permute-done | bytes 65568 | tf_op jit(solution)/shard_map/ppermute | solution.py:51
  54.8 1.7 %collective-permute-done.12.above0 = bf16[2,128,128]{2,1,0:T(8,128)(2,1)S(1)} collective-permute-done((bf16[2,128,128]{2,1,0:T(8,128)(2,1)S(1)}, bf16[2,128,128]{2,1,0:T(8,128)(2,1)S(1)}, u32[]{:S(2)}, u32[]{:S(2)}) %collective-permute-start.12) | collective-permute-done | bytes 65568 | tf_op jit(solution)/shard_map/ppermute | solution.py:51
  56.6 1.7 %collective-permute-start.16 = (bf16[2,128,256]{2,1,0:T(8,128)(2,1)S(1)}, bf16[2,128,256]{2,1,0:T(8,128)(2,1)S(1)}, u32[]{:S(2)}, u32[]{:S(2)}) collective-permute-start(bf16[2,128,256]{2,1,0:T(8,128)(2,1)S(1)} %get-tuple-element.57.refs_2_), channel_id=1, source_target_pairs={{0,2},{1,3},{2,0},{3,1},{4,6},{5,7},{6,4},{7,5},{8,10},{9,11},{10,... | collective-permute-start | bytes 393224 | tf_op jit(solution)/shard_map/ppermute | solution.py:56
  58.4 1.9 %collective-permute-start.20 = (bf16[3,128,256]{2,1,0:T(8,128)(2,1)S(1)}, bf16[3,128,256]{2,1,0:T(8,128)(2,1)S(1)}, u32[]{:S(2)}, u32[]{:S(2)}) collective-permute-start(bf16[3,128,256]{2,1,0:T(8,128)(2,1)S(1)} %add.25.held), channel_id=1, source_target_pairs={{0,16},{4,20},{8,24},{12,28},{16,0},{20,4},{24,8},{28,12},{1,17},{... | collective-permute-start | bytes 589832 | tf_op jit(solution)/shard_map/ppermute | solution.py:56
  60.3 1.3 %collective-permute-done.16.refs_3_ = bf16[2,128,256]{2,1,0:T(8,128)(2,1)S(1)} collective-permute-done((bf16[2,128,256]{2,1,0:T(8,128)(2,1)S(1)}, bf16[2,128,256]{2,1,0:T(8,128)(2,1)S(1)}, u32[]{:S(2)}, u32[]{:S(2)}) %collective-permute-start.16) | collective-permute-done | bytes 131104 | tf_op jit(solution)/shard_map/ppermute | solution.py:56
  61.7 1.6 %collective-permute-done.15.refs_1_ = bf16[2,128,256]{2,1,0:T(8,128)(2,1)S(1)} collective-permute-done((bf16[2,128,256]{2,1,0:T(8,128)(2,1)S(1)}, bf16[2,128,256]{2,1,0:T(8,128)(2,1)S(1)}, u32[]{:S(2)}, u32[]{:S(2)}) %collective-permute-start.15) | collective-permute-done | bytes 131104 | tf_op jit(solution)/shard_map/ppermute | solution.py:56
  63.4 0.5 collective-permute-start.17
  63.8 4.6 %collective-permute-done.17.first_came.rest_0_ = bf16[2,128,256]{2,1,0:T(8,128)(2,1)S(1)} collective-permute-done((bf16[2,128,256]{2,1,0:T(8,128)(2,1)S(1)}, bf16[2,128,256]{2,1,0:T(8,128)(2,1)S(1)}, u32[]{:S(2)}, u32[]{:S(2)}) %collective-permute-start.17) | collective-permute-done | bytes 131104 | tf_op jit(solution)/shard_map/ppermute | solution.py:56
  68.4 1.1 %collective-permute-done.20.came = bf16[3,128,256]{2,1,0:T(8,128)(2,1)S(1)} collective-permute-done((bf16[3,128,256]{2,1,0:T(8,128)(2,1)S(1)}, bf16[3,128,256]{2,1,0:T(8,128)(2,1)S(1)}, u32[]{:S(2)}, u32[]{:S(2)}) %collective-permute-start.20) | collective-permute-done | bytes 196640 | tf_op jit(solution)/shard_map/ppermute | solution.py:56
  69.6 1.2 %settle.1 = (f32[2,256,256]{2,1,0:T(8,128)}, f32[2,256,256]{2,1,0:T(8,128)}) custom-call(bf16[2,128,256]{2,1,0:T(8,128)(2,1)S(1)} %get-tuple-element.58.first, bf16[2,128,256]{2,1,0:T(8,128)(2,1)S(1)} %collective-permute-done.17.first_came.rest_0_, bf16[2,128,256]{2,1,0:T(8,128)(2,1)S(1)} %get-tuple-element.59.second, ...), custom_call_target="tpu_custom_call" | custom-call | flops 262144 | tf_op jit(solution)/shard_map/settle/pallas_call | solution.py:451
  71.0 0.9 %convert_add_fusion = f32[1,2,256,256]{3,2,1,0:T(8,128)} fusion(f32[1,2,256,256]{3,2,1,0:T(8,128)S(1)} %copy-done.8, bf16[1,2,128,256]{3,2,1,0:T(8,128)(2,1)S(1)} %bitcast.19, bf16[1,2,128,256]{3,2,1,0:T(8,128)(2,1)S(1)} %bitcast.29, pred[]{:T(512)} %eq.8), kind=kLoop, calls=%fused_computation | loop fusion | flops 1441792 | bytes 1310721 | tf_op jit(solution)/shard_map/add | solution.py:584
  (56 shorter events, 1.9 us)
Async XLA Ops:
  0.6 6.7 %copy-start.9 = (s32[1,1,4,2]{2,3,1,0:T(2,128)S(1)}, s32[1,1,4,2]{2,3,1,0:T(2,128)}, u32[]{:S(2)}) copy-start(s32[1,1,4,2]{2,3,1,0:T(2,128)} %param.12) | copy-start | bytes 100
  1.8 10.3 %collective-permute-start.1 = (bf16[2,128,128]{2,1,0:T(8,128)(2,1)S(1)}, bf16[2,128,128]{2,1,0:T(8,128)(2,1)S(1)}, u32[]{:S(2)}, u32[]{:S(2)}) collective-permute-start(bf16[2,128,128]{2,1,0:T(8,128)(2,1)S(1)} %get-tuple-element.64), channel_id=1, source_target_pairs={{0,16},{4,20},{8,24},{12,28},{16,0},{20,4},{24,8},{28,12},{1,17},{... | collective-permute-start | bytes 196616 | tf_op jit(solution)/shard_map/ppermute | solution.py:51
  5.9 10.3 %collective-permute-start = (bf16[2,256,128]{2,1,0:T(8,128)(2,1)S(1)}, bf16[2,256,128]{2,1,0:T(8,128)(2,1)S(1)}, u32[]{:S(2)}, u32[]{:S(2)}) collective-permute-start(bf16[2,256,128]{2,1,0:T(8,128)(2,1)S(1)} %slice.12), channel_id=1, source_target_pairs={{0,12},{4,0},{8,4},{12,8},{16,28},{20,16},{24,20},{28,24},{1,13},{... | collective-permute-start | bytes 393224 | tf_op jit(solution)/shard_map/ppermute | solution.py:51
  7.6 4.9 %collective-permute-start.4 = (s32[16]{0:T(128)S(1)}, s32[16]{0:T(128)S(1)}, u32[]{:S(2)}, u32[]{:S(2)}) collective-permute-start(s32[16]{0:T(128)S(1)} %pad_add_fusion.1.meta), channel_id=1, source_target_pairs={{0,16},{4,20},{8,24},{12,28},{16,0},{20,4},{24,8},{28,12},{1,17},{... | collective-permute-start | bytes 200 | tf_op jit(solution)/shard_map/ppermute | solution.py:51
  7.9 8.2 %collective-permute-start.2 = (bf16[2,128,128]{2,1,0:T(8,128)(2,1)S(1)}, bf16[2,128,128]{2,1,0:T(8,128)(2,1)S(1)}, u32[]{:S(2)}, u32[]{:S(2)}) collective-permute-start(bf16[2,128,128]{2,1,0:T(8,128)(2,1)S(1)} %get-tuple-element.63), channel_id=1, source_target_pairs={{0,16},{4,20},{8,24},{12,28},{16,0},{20,4},{24,8},{28,12},{1,17},{... | collective-permute-start | bytes 196616 | tf_op jit(solution)/shard_map/ppermute | solution.py:51
  12.0 4.1 %collective-permute-start.3 = (bf16[2,128,128]{2,1,0:T(8,128)(2,1)S(1)}, bf16[2,128,128]{2,1,0:T(8,128)(2,1)S(1)}, u32[]{:S(2)}, u32[]{:S(2)}) collective-permute-start(bf16[2,128,128]{2,1,0:T(8,128)(2,1)S(1)} %collective-permute-done.1.below0.rest_2_.rest_9_), channel_id=1, source_target_pairs={{0,12},{4,0},{8,4},{12,8},{16,28},{20,16},{24,20},{28,24},{1,13},{... | collective-permute-start | bytes 196616 | tf_op jit(solution)/shard_map/ppermute | solution.py:51
  12.5 3.7 %copy-start.2 = (s32[2,16]{1,0:T(2,128)}, s32[2,16]{1,0:T(2,128)S(1)}, u32[]{:S(2)}) copy-start(s32[2,16]{1,0:T(2,128)S(1)} %pad_add_fusion.rest_0_) | copy-start | bytes 388
  12.5 1.9 %collective-permute-start.6 = (s32[2,16]{1,0:T(2,128)S(1)}, s32[2,16]{1,0:T(2,128)S(1)}, u32[]{:S(2)}, u32[]{:S(2)}) collective-permute-start(s32[2,16]{1,0:T(2,128)S(1)} %pad_add_fusion.rest_0_), channel_id=1, source_target_pairs={{0,12},{4,0},{8,4},{12,8},{16,28},{20,16},{24,20},{28,24},{1,13},{... | collective-permute-start | bytes 392 | tf_op jit(solution)/shard_map/ppermute | solution.py:51
  13.1 3.0 %collective-permute-start.5 = (s32[2,16]{1,0:T(2,128)S(1)}, s32[2,16]{1,0:T(2,128)S(1)}, u32[]{:S(2)}, u32[]{:S(2)}) collective-permute-start(s32[2,16]{1,0:T(2,128)S(1)} %pad_add_fusion.rest_0_), channel_id=1, source_target_pairs={{0,4},{4,8},{8,12},{12,0},{16,20},{20,24},{24,28},{28,16},{1,5},{5... | collective-permute-start | bytes 392 | tf_op jit(solution)/shard_map/ppermute | solution.py:51
  14.4 1.8 %copy-start.4 = (s32[2,16]{1,0:T(2,128)}, s32[2,16]{1,0:T(2,128)S(1)}, u32[]{:S(2)}) copy-start(s32[2,16]{1,0:T(2,128)S(1)} %collective-permute-done.6.rest_2_) | copy-start | bytes 388
  16.1 0.6 copy-start.6
  16.2 13.8 %copy-start = (f32[8,128]{1,0:T(8,128)}, f32[8,128]{1,0:T(8,128)S(1)}, u32[]{:S(2)}) copy-start(f32[8,128]{1,0:T(8,128)S(1)} %broadcast_in_dim.6.flags.rest_14_) | copy-start | bytes 12292
  23.4 6.6 %collective-permute-start.7 = (bf16[2,384,128]{2,1,0:T(8,128)(2,1)S(1)}, bf16[2,384,128]{2,1,0:T(8,128)(2,1)S(1)}, u32[]{:S(2)}, u32[]{:S(2)}) collective-permute-start(bf16[2,384,128]{2,1,0:T(8,128)(2,1)S(1)} %get-tuple-element.38), channel_id=1, source_target_pairs={{0,4},{4,0},{8,12},{12,8},{16,20},{20,16},{24,28},{28,24},{1,5},{5... | collective-permute-start | bytes 589832 | tf_op jit(solution)/shard_map/ppermute | solution.py:56
  23.5 6.5 %collective-permute-start.8 = (bf16[2,384,128]{2,1,0:T(8,128)(2,1)S(1)}, bf16[2,384,128]{2,1,0:T(8,128)(2,1)S(1)}, u32[]{:S(2)}, u32[]{:S(2)}) collective-permute-start(bf16[2,384,128]{2,1,0:T(8,128)(2,1)S(1)} %get-tuple-element.39), channel_id=1, source_target_pairs={{0,0},{4,8},{8,4},{12,12},{16,16},{20,24},{24,20},{28,28},{1,1},{5... | collective-permute-start | bytes 589832 | tf_op jit(solution)/shard_map/ppermute | solution.py:65
  24.2 5.8 %collective-permute-start.9 = (bf16[2,128,128]{2,1,0:T(8,128)(2,1)S(1)}, bf16[2,128,128]{2,1,0:T(8,128)(2,1)S(1)}, u32[]{:S(2)}, u32[]{:S(2)}) collective-permute-start(bf16[2,128,128]{2,1,0:T(8,128)(2,1)S(1)} %get-tuple-element.40), channel_id=1, source_target_pairs={{0,16},{4,20},{8,24},{12,28},{16,0},{20,4},{24,8},{28,12},{1,17},{... | collective-permute-start | bytes 196616 | tf_op jit(solution)/shard_map/ppermute | solution.py:51
  30.0 0.7 copy-start.3
  30.0 0.7 copy-start.5
  30.0 0.7 copy-start.7
  30.2 8.6 %copy-start.1 = (f32[8,128]{1,0:T(8,128)S(1)}, f32[8,128]{1,0:T(8,128)}, u32[]{:S(2)}) copy-start(f32[8,128]{1,0:T(8,128)} %copy-done) | copy-start | bytes 12292
  30.2 8.6 %collective-permute-start.10 = (bf16[2,2,128,128]{3,2,1,0:T(8,128)(2,1)S(1)}, bf16[2,2,128,128]{3,2,1,0:T(8,128)(2,1)S(1)}, u32[]{:S(2)}, u32[]{:S(2)}) collective-permute-start(bf16[2,2,128,128]{3,2,1,0:T(8,128)(2,1)S(1)} %between.1.rest_3_), channel_id=1, source_target_pairs={{0,16},{4,20},{8,24},{12,28},{16,0},{20,4},{24,8},{28,12},{1,17},{... | collective-permute-start | bytes 393224 | tf_op jit(solution)/shard_map/ppermute | solution.py:51
  45.1 1.5 %collective-permute-start.14 = (bf16[3,128,256]{2,1,0:T(8,128)(2,1)S(1)}, bf16[3,128,256]{2,1,0:T(8,128)(2,1)S(1)}, u32[]{:S(2)}, u32[]{:S(2)}) collective-permute-start(bf16[3,128,256]{2,1,0:T(8,128)(2,1)S(1)} %get-tuple-element.55), channel_id=1, source_target_pairs={{0,4},{4,0},{8,12},{12,8},{16,20},{20,16},{24,28},{28,24},{1,5},{5... | collective-permute-start | bytes 589832 | tf_op jit(solution)/shard_map/ppermute | solution.py:56
  45.2 5.1 %collective-permute-start.11 = (bf16[2,384,128]{2,1,0:T(8,128)(2,1)S(1)}, bf16[2,384,128]{2,1,0:T(8,128)(2,1)S(1)}, u32[]{:S(2)}, u32[]{:S(2)}) collective-permute-start(bf16[2,384,128]{2,1,0:T(8,128)(2,1)S(1)} %get-tuple-element.51), channel_id=1, source_target_pairs={{0,4},{4,8},{8,12},{12,0},{16,20},{20,24},{24,28},{28,16},{1,5},{5... | collective-permute-start | bytes 589832 | tf_op jit(solution)/shard_map/ppermute | solution.py:51
  46.7 11.6 %collective-permute-start.19 = (bf16[3,128,256]{2,1,0:T(8,128)(2,1)S(1)}, bf16[3,128,256]{2,1,0:T(8,128)(2,1)S(1)}, u32[]{:S(2)}, u32[]{:S(2)}) collective-permute-start(bf16[3,128,256]{2,1,0:T(8,128)(2,1)S(1)} %halve.1.rest_0_.held), channel_id=1, source_target_pairs={{0,8},{4,12},{8,0},{12,4},{16,24},{20,28},{24,16},{28,20},{1,9},{5... | collective-permute-start | bytes 589832 | tf_op jit(solution)/shard_map/ppermute | solution.py:56
  47.0 7.8 %collective-permute-start.13 = (bf16[2,128,128]{2,1,0:T(8,128)(2,1)S(1)}, bf16[2,128,128]{2,1,0:T(8,128)(2,1)S(1)}, u32[]{:S(2)}, u32[]{:S(2)}) collective-permute-start(bf16[2,128,128]{2,1,0:T(8,128)(2,1)S(1)} %get-tuple-element.53), channel_id=1, source_target_pairs={{0,16},{4,20},{8,24},{12,28},{16,0},{20,4},{24,8},{28,12},{1,17},{... | collective-permute-start | bytes 196616 | tf_op jit(solution)/shard_map/ppermute | solution.py:51
  50.4 6.2 %collective-permute-start.12 = (bf16[2,128,128]{2,1,0:T(8,128)(2,1)S(1)}, bf16[2,128,128]{2,1,0:T(8,128)(2,1)S(1)}, u32[]{:S(2)}, u32[]{:S(2)}) collective-permute-start(bf16[2,128,128]{2,1,0:T(8,128)(2,1)S(1)} %add_rim.1), channel_id=1, source_target_pairs={{0,16},{4,20},{8,24},{12,28},{16,0},{20,4},{24,8},{28,12},{1,17},{... | collective-permute-start | bytes 196616 | tf_op jit(solution)/shard_map/ppermute | solution.py:51
  56.6 5.0 %collective-permute-start.16 = (bf16[2,128,256]{2,1,0:T(8,128)(2,1)S(1)}, bf16[2,128,256]{2,1,0:T(8,128)(2,1)S(1)}, u32[]{:S(2)}, u32[]{:S(2)}) collective-permute-start(bf16[2,128,256]{2,1,0:T(8,128)(2,1)S(1)} %get-tuple-element.57.refs_2_), channel_id=1, source_target_pairs={{0,2},{1,3},{2,0},{3,1},{4,6},{5,7},{6,4},{7,5},{8,10},{9,11},{10,... | collective-permute-start | bytes 393224 | tf_op jit(solution)/shard_map/ppermute | solution.py:56
  58.3 5.0 %collective-permute-start.15 = (bf16[2,128,256]{2,1,0:T(8,128)(2,1)S(1)}, bf16[2,128,256]{2,1,0:T(8,128)(2,1)S(1)}, u32[]{:S(2)}, u32[]{:S(2)}) collective-permute-start(bf16[2,128,256]{2,1,0:T(8,128)(2,1)S(1)} %get-tuple-element.56.refs_0_.rest_0_), channel_id=1, source_target_pairs={{0,1},{1,0},{2,3},{3,2},{4,5},{5,4},{6,7},{7,6},{8,9},{9,8},{10,11... | collective-permute-start | bytes 393224 | tf_op jit(solution)/shard_map/ppermute | solution.py:56
  58.4 12.6 %copy-start.8 = (f32[1,2,256,256]{3,2,1,0:T(8,128)S(1)}, f32[1,2,256,256]{3,2,1,0:T(8,128)}, u32[]{:S(2)}) copy-start(f32[1,2,256,256]{3,2,1,0:T(8,128)} %param.10) | copy-start | bytes 1572868
  58.4 11.1 %collective-permute-start.20 = (bf16[3,128,256]{2,1,0:T(8,128)(2,1)S(1)}, bf16[3,128,256]{2,1,0:T(8,128)(2,1)S(1)}, u32[]{:S(2)}, u32[]{:S(2)}) collective-permute-start(bf16[3,128,256]{2,1,0:T(8,128)(2,1)S(1)} %add.25.held), channel_id=1, source_target_pairs={{0,16},{4,20},{8,24},{12,28},{16,0},{20,4},{24,8},{28,12},{1,17},{... | collective-permute-start | bytes 589832 | tf_op jit(solution)/shard_map/ppermute | solution.py:56
  63.4 5.0 %collective-permute-start.17 = (bf16[2,128,256]{2,1,0:T(8,128)(2,1)S(1)}, bf16[2,128,256]{2,1,0:T(8,128)(2,1)S(1)}, u32[]{:S(2)}, u32[]{:S(2)}) collective-permute-start(bf16[2,128,256]{2,1,0:T(8,128)(2,1)S(1)} %get-tuple-element.58.first), channel_id=1, source_target_pairs={{0,2},{1,3},{2,0},{3,1},{4,6},{5,7},{6,4},{7,5},{8,10},{9,11},{10,... | collective-permute-start | bytes 393224 | tf_op jit(solution)/shard_map/ppermute | solution.py:56
  63.8 5.8 %collective-permute-start.18 = (bf16[2,128,256]{2,1,0:T(8,128)(2,1)S(1)}, bf16[2,128,256]{2,1,0:T(8,128)(2,1)S(1)}, u32[]{:S(2)}, u32[]{:S(2)}) collective-permute-start(bf16[2,128,256]{2,1,0:T(8,128)(2,1)S(1)} %get-tuple-element.59.second), channel_id=1, source_target_pairs={{0,1},{1,0},{2,3},{3,2},{4,5},{5,4},{6,7},{7,6},{8,9},{9,8},{10,11... | collective-permute-start | bytes 393224 | tf_op jit(solution)/shard_map/ppermute | solution.py:56
  69.5 1.4 %collective-permute-start.21 = (bf16[2,128,256]{2,1,0:T(8,128)(2,1)S(1)}, bf16[2,128,256]{2,1,0:T(8,128)(2,1)S(1)}, u32[]{:S(2)}, u32[]{:S(2)}) collective-permute-start(bf16[2,128,256]{2,1,0:T(8,128)(2,1)S(1)} %update.1), channel_id=1, source_target_pairs={{0,4},{4,0},{8,12},{12,8},{16,20},{20,16},{24,28},{28,24},{1,5},{5... | collective-permute-start | bytes 393224 | tf_op jit(solution)/shard_map/ppermute | solution.py:56

commit v4 on v3

--- a/solution.py
+++ b/solution.py
@@ -18,8 +18,8 @@
 SPAN = TS + OVER
 L = 128
 CH = 32
-META = 16
 COUNT = 2 * SLOTS
+CARD = 16
 HAS_LEFT, HAS_RIGHT, HAS_ABOVE, HAS_BELOW, ODD = range(5)
 
 penalty = 0.5
@@ -192,16 +192,19 @@
 
 
 def first_pass(
-    two, meta, flags, right, below0, below1, diag, ext0, acc0, probe, fwd_h, bwd_h, amps_h, *rest,
+    two, meta, flags, right, below0, below1, diag, ext0, acc0, probe, *rest,
 ):
-    ext, acc, pnum, side, inner, *mids, fwd, bwd, amps, sems, win, X, Y, W = rest[3:]
+    *cards, fwd_h, bwd_h, amps_h = rest[: 4 if two else 5]
+    ext, acc, pnum, side, inner, *mids, fwd, bwd, amps, sems, win, X, Y, W = rest[4 if two else 5 :]
     copies = fetch([(fwd_h, fwd), (bwd_h, bwd), (amps_h, amps)], sems)
     has_right = flags[HAS_RIGHT : HAS_RIGHT + 1, :]
     has_below = flags[HAS_BELOW : HAS_BELOW + 1, :]
     ext[:, 2, :TS, :] = right[...].astype(f32) * has_right
-    ext[:, 2, TS:, :] = diag[...].astype(f32) * (has_right * has_below)
+    for ch in range(2):
+        ext[ch, 2, TS:, :] = diag[plane(ch, OVER), :].astype(f32) * (has_right * has_below)
     for j in range(2):
-        ext[:, j, TS:, :] = (below0, below1)[j][...].astype(f32) * has_below
+        for ch in range(2):
+            ext[ch, j, TS:, :] = (below0, below1)[j][plane(ch, OVER), :].astype(f32) * has_below
     pnum[...] = jnp.zeros_like(pnum)
     for copy in copies:
         copy.wait()
@@ -211,11 +214,18 @@
         visit_pair(p, meta, ext, probe, amps, fwd, bwd, acc, pnum, win, X, Y, W)
 
     odd = flags[ODD : ODD + 1, :] > 0.0
+    column = [card[...] for card in cards] + [below1[2 * OVER :, :]]
+    side[2 * SPAN :, :] = jnp.concatenate(column, 0)
+    inner[2 * SPAN :, :] = jnp.concatenate(column, 0)
     for ch in range(2):
-        side[ch] = jnp.where(odd, acc[ch, 0], acc[ch, 2]).astype(bf16)
-        inner[ch] = jnp.where(odd, acc[ch, 2], acc[ch, 0]).astype(bf16)
+        side[plane(ch, SPAN), :] = jnp.where(odd, acc[ch, 0], acc[ch, 2]).astype(bf16)
+        inner[plane(ch, SPAN), :] = jnp.where(odd, acc[ch, 2], acc[ch, 0]).astype(bf16)
         for rim, mid in zip(rims_of(two, flags, lambda rows: acc[ch, 1, rows, :]), mids):
             mid[ch] = rim.astype(bf16)
+
+
+def plane(ch, rows, start=0, count=None):
+    return slice(ch * rows + start, ch * rows + start + (rows if count is None else count))
 
 
 def rims_of(two, flags, get):
@@ -236,7 +246,8 @@
         for at in range(2):
 
             def total(rows):
-                came = from_sides(flags, side[ch, rows, :], inner[ch, rows, :])[at]
+                where = plane(ch, SPAN, rows.start, OVER)
+                came = from_sides(flags, side[where, :], inner[where, :])[at]
                 return acc[ch, 2 * at, rows, :] + came
 
             for rim, out in zip(rims_of(two, flags, total), outs):
@@ -244,32 +255,44 @@
 
 
 def weigh(two, *rest):
-    metas = rest[:3]
-    flags, *sources = rest[-18:-11]
-    weight, *targets, sems, p2, buf, there = rest[-11:]
-    copies = fetch([(flags, there)] + list(zip(sources, targets)), sems)
+    *cards, flags, side, inner = rest[: 4 if two else 5]
+    below1, *sources = rest[-19:-12]
+    weight, *targets, sems, p2, buf, held, table = rest[-12:]
+    copies = fetch(list(zip(sources, targets)), sems)
     probe = targets[2]
+    last = 2 * OVER
+    blocks = [card[...].astype(f32) for card in cards] + [below1[last:, :].astype(f32)]
+    for k, block in enumerate(blocks):
+        held[k : k + 1, :] = block[:1]
+        at = 2 * SPAN + k * CARD
+        odd = flags[ODD : ODD + 1, :] > 0.0
+        by_side, by_inner = [v[at : at + CARD, :].astype(f32)[:1] for v in (side, inner)]
+        held[4 + k : 5 + k, :] = jnp.where(odd, by_side, by_inner)
+        held[8 + k : 9 + k, :] = jnp.where(odd, by_inner, by_side)
+    held[16:24, :] = flags[...]
+    moved = pltpu.make_async_copy(held, table, sems.at[6])
+    moved.start()
     buf[...] = jnp.zeros_like(buf)
-    copies[3].wait()
+    copies[2].wait()
     for j in range(2):
         cols = slice(j * L, (j + 1) * L)
         p2[j] = probe[0, :, cols] * probe[0, :, cols] + probe[1, :, cols] * probe[1, :, cols]
-    copies[0].wait()
+    moved.wait()
     for dr in (-1, 0, 1):
         for dc in (-1, 0, 1):
-            meta, at_row = metas[{0: 0, -1: 1, 1: 2}[dc]], {0: 0, -1: 1, 1: 1 if two else 2}[dr]
+            at_row = {0: 0, -1: 4, 1: 8}[dc] + {0: 0, -1: 1, 1: 1 if two else 2}[dr]
             first, rows = {-1: (OVER, OVER), 0: (0, PS), 1: (0, OVER)}[dr]
             base = {-1: 0, 0: OVER, 1: OVER + TS}[dr]
-            count = meta[at_row, COUNT]
+            count = table[at_row, COUNT].astype(jnp.int32)
             for flag, at, step in (
                 (HAS_ABOVE, -1, dr), (HAS_BELOW, 1, dr), (HAS_LEFT, -1, dc), (HAS_RIGHT, 1, dc)
             ):
                 if step == at:
-                    count = jnp.where(there[flag, 0] > 0.0, count, 0)
+                    count = jnp.where(table[16 + flag, 0] > 0.0, count, 0)
 
             @pl.loop(0, count)
-            def _(s, meta=meta, at_row=at_row, dc=dc, first=first, rows=rows, base=base):
-                r, c = meta[at_row, 2 * s], meta[at_row, 2 * s + 1]
+            def _(s, at_row=at_row, dc=dc, first=first, rows=rows, base=base):
+                r, c = [table[at_row, 2 * s + i].astype(jnp.int32) for i in range(2)]
                 for k in range(0, rows, 64):
                     at = pl.ds(base + r + k, 64)
                     v = [p2[j, first + k : first + k + 64, :] for j in range(2)]
@@ -284,7 +307,7 @@
 
     weight[...] = buf[:, OVER : OVER + SPAN, :]
     for k, copy in enumerate(copies):
-        if k not in (0, 3):
+        if k != 2:
             copy.wait()
 
 
@@ -306,7 +329,8 @@
                 rows = slice(k, k + 64)
                 total = acc1[ch, j, rows, :]
                 if j != 1:
-                    total = total + from_sides(flags, side[ch, rows, :], inner[ch, rows, :])[j // 2]
+                    at = plane(ch, SPAN, k, 64)
+                    total = total + from_sides(flags, side[at, :], inner[at, :])[j // 2]
                 if k < OVER:
                     came = mid_above[ch, rows, :] if j == 1 else from_above[ch, j // 2, rows, :]
                     total = total + came.astype(f32) * has_above
@@ -322,9 +346,9 @@
                     if k < TS:
                         est = right[ch, rows, :].astype(f32) + step
                     elif j < 2:
-                        est = (below0, below1)[j][ch, k - TS : k - TS + 64, :].astype(f32) + step
+                        est = (below0, below1)[j][plane(ch, OVER, k - TS, 64), :].astype(f32) + step
                     else:
-                        est = diag[ch, k - TS : k - TS + 64, :].astype(f32) + step
+                        est = diag[plane(ch, OVER, k - TS, 64), :].astype(f32) + step
                     if j == 2:
                         est = est * has_right
                     if k >= TS:
@@ -498,23 +522,20 @@
     measured = ((SLOTS, PS, PS), bf16)
 
     rounded = own.astype(bf16)
-    below = [shifted(rounded[:, :OVER, j * L : (j + 1) * L], -1, 0) for j in range(2)]
-    right = shifted(rounded[:, :, :OVER], 0, -1)
-    below.append(shifted(below[0], 0, -1))
-
     height = n // TGW
     two = height == 2
     row, col = index // TGW, index % TGW
     flags = [col > 0, col < TGW - 1, row > 0, row < height - 1]
     flags = flags + [index % 2 == 1] + [col < 0] * 3
     flags = jnp.broadcast_to(jnp.stack(flags).astype(f32)[:, None], (8, L))
-    meta = jnp.concatenate(
-        [offsets[0, 0].reshape(COUNT), counts[0], jnp.zeros((META - COUNT - 1,), jnp.int32)]
-    )
-    _, meta = lax.optimization_barrier((rounded, meta))
-    column = [meta, shifted(meta, 1, 0)] + ([] if two else [shifted(meta, -1, 0)])
-    column = jnp.stack(column)
-    metas = [column, shifted(column, 0, 1), shifted(column, 0, -1)]
+    meta = jnp.concatenate([offsets[0, 0].reshape(COUNT), counts[0]])
+    card = jnp.pad(meta.astype(bf16)[None], ((0, CARD - 1), (0, L - COUNT - 1)))
+
+    sent = [rounded[:, :OVER, j * L : (j + 1) * L].reshape(2 * OVER, L) for j in range(2)]
+    below = [shifted(sent[0], -1, 0), shifted(jnp.concatenate([sent[1], card]), -1, 0)]
+    right = shifted(rounded[:, :, :OVER], 0, -1)
+    below.append(shifted(below[0], 0, -1))
+    cards = [card] if two else [card, shifted(card, 1, 0)]
 
     inputs = (own, dual, probe, amps, fwd, bwd)
     staged = call(
@@ -524,9 +545,10 @@
     rim = ((2, OVER, L), bf16)
     ext, acc, pnum, side, inner, *mids = call(
         functools.partial(first_pass, two), "first_pass",
-        [WIDE, WIDE, SUMS, ((2, SPAN, L), bf16), ((2, SPAN, L), bf16)] + [rim] * (1 if two else 2),
-        [TABLE, TABLE, measured, None] + WORK, 1, 6, 3, aliases={6: 0, 7: 1}, flops=PASS,
-    )(meta, flags, right, *below, *staged, fwd, bwd, amps, *metas)
+        [WIDE, WIDE, SUMS] + [((2 * SPAN + (len(cards) + 1) * CARD, L), bf16)] * 2
+        + [rim] * (1 if two else 2),
+        [TABLE, TABLE, measured, None] + WORK, 1, 3, 3, aliases={6: 0, 7: 1}, flops=PASS,
+    )(meta, flags, right, *below, *staged, *cards, fwd, bwd, amps)
     side = swapped(side, "tile", 1)
     inner = inner_swapped(inner)
 
@@ -542,9 +564,11 @@
     weight, *inputs = call(
         functools.partial(weigh, two), "weigh",
         [((3, SPAN, L), f32), PLANES, PLANES, PLANES, measured, TABLE, TABLE],
-        [None, ((2, PS, L), f32), ((3, SPAN + 2 * OVER, L), f32), pltpu.SMEM((8, L), f32)],
-        len(metas), 7, 7, held=True,
-    )(*metas, rims[0], acc, side, inner, pnum, right, *below, mid_above, mid_below, flags, *inputs)
+        [None, ((2, PS, L), f32), ((3, SPAN + 2 * OVER, L), f32), ((24, L), f32),
+         pltpu.SMEM((24, L), f32)],
+        0, 6, 7, held=True,
+    )(*cards, flags, side, inner, rims[0], acc, pnum, right, below[0], below[2], mid_above, mid_below,
+      below[1], *inputs)
     weight, *inputs = [pinned(v) for v in (weight, *inputs)]
 
     base, shrink, to_right, rim, to_below, pnum, to_swap = call(
@@ -569,7 +593,7 @@
     )(flags, base, shrink, from_left, above0, above1, *([sums] if eight else []))
     if eight:
         (sums,) = call(add, "add", half)(sums, came, parts[0])
-        came = swapped(sums, "tile", 4)
+        came = swapped(sums, "tile", 6)
     pairs = scan_sums(parts)
     if eight:
         (change,) = call(update, "update", [((2, PS // 2, PS), bf16)])(sums, came, pairs[1])

time: 72.2 us -> 70.2 us (0.972)
  waiting for transfers between devices: 32.8 us -> 26.8 us
  starting transfers between devices: 14.9 us -> 20.4 us
  local copies, waits for them, and re-layouts: 1.37 us -> 0.59 us
    ppermute x9, starting transfers between devices: 4.59 us -> 10.7 us  [swapped(): return lax.ppermute(value, axis, [(i, i ^ bit) for i in range(n)])]
    ppermute x12 -> x9, waiting for transfers between devices: 23.1 us -> 20 us  [shifted(): return lax.ppermute(value, 'tile', pairs)]
    ppermute x9, waiting for transfers between devices: 9.66 us -> 6.74 us  [swapped(): return lax.ppermute(value, axis, [(i, i ^ bit) for i in range(n)])]
    unnamed x21 -> x5, local copies, waits for them, and re-layouts: 1.07 us -> 0.1 us
    ppermute x12 -> x9, starting transfers between devices: 9.6 us -> 9.03 us  [shifted(): return lax.ppermute(value, 'tile', pairs)]
  transfers between devices with their start and end apart: 22 -> 19, of which waited for: 13 -> 10; matrix products, arithmetic and copies ran while one was open for 1% -> 1% of each run, Pallas kernels for 8% -> 8%
where the time goes in v4:
time: 70.2 us; the launch traced here: 70.1 us
  waiting for transfers between devices  26.8 us (38%)
  starting transfers between devices  20.4 us (29%)
  Pallas kernels  18.8 us (27%)
  other arithmetic  2.11 us (3%)
  between operations  1.49 us (2%)
    ppermute x9, waiting for transfers between devices, shifted(): return lax.ppermute(value, 'tile', pairs)  20 us
    pallas_call x12, Pallas kernels, run(): pl.pallas_call(body, in_specs=[S] * scalars + [V] * near + [H] * far, out...  18.8 us
    ppermute x9, starting transfers between devices, swapped(): return lax.ppermute(value, axis, [(i, i ^ bit) for i in range(n)])  10.7 us
    ppermute x9, starting transfers between devices, shifted(): return lax.ppermute(value, 'tile', pairs)  9.03 us
    ppermute x9, waiting for transfers between devices, swapped(): return lax.ppermute(value, axis, [(i, i ^ bit) for i in range(n)])  6.74 us
  transfers between devices with their start and end apart: 19, of which 10 were waited for; matrix products, arithmetic and copies ran while one was open for 1% of the time, Pallas kernels for 8%

profile of v4, /device:TPU:0, one launch (start us, length us, event | category | flops | bytes accessed | tf_op | source)
XLA Modules:
  0.0 70.1 jit_solution(11460134495746507288)
XLA Ops:
  0.6 1.1 %bitcast_convert_fusion = bf16[2,256,256]{2,1,0:T(8,128)(2,1)S(1)} fusion(f32[1,2,256,256]{3,2,1,0:T(8,128)} %param.8), kind=kLoop, calls=%fused_computation.12 | loop fusion | flops 131072 | bytes 786432 | tf_op jit(solution)/shard_map/convert_element_type | solution.py:524
  1.8 4.1 %collective-permute-start.1 = (bf16[256,128]{1,0:T(8,128)(2,1)S(1)}, bf16[256,128]{1,0:T(8,128)(2,1)S(1)}, u32[]{:S(2)}, u32[]{:S(2)}) collective-permute-start(bf16[256,128]{1,0:T(8,128)(2,1)S(1)} %bitcast.30), channel_id=1, source_target_pairs={{0,16},{4,20},{8,24},{12,28},{16,0},{20,4},{24,8},{28,12},{1,17},{... | collective-permute-start | bytes 196616 | tf_op jit(solution)/shard_map/ppermute | solution.py:51
  5.9 0.8 %collective-permute-start = (bf16[2,256,128]{2,1,0:T(8,128)(2,1)S(1)}, bf16[2,256,128]{2,1,0:T(8,128)(2,1)S(1)}, u32[]{:S(2)}, u32[]{:S(2)}) collective-permute-start(bf16[2,256,128]{2,1,0:T(8,128)(2,1)S(1)} %slice.12), channel_id=1, source_target_pairs={{0,12},{4,0},{8,4},{12,8},{16,28},{20,16},{24,20},{28,24},{1,13},{... | collective-permute-start | bytes 393224 | tf_op jit(solution)/shard_map/ppermute | solution.py:51
  7.3 0.1 copy.16
  7.6 0.4 collective-permute-start.2
  8.1 0.1 stack.29
  8.3 1.4 %stage.1 = (f32[2,3,384,128]{3,2,1,0:T(8,128)S(1)}, f32[2,3,384,128]{3,2,1,0:T(8,128)S(1)}, f32[2,256,256]{2,1,0:T(8,128)S(1)}) custom-call(f32[2,256,256]{2,1,0:T(8,128)} %bitcast.22, f32[2,256,256]{2,1,0:T(8,128)} %bitcast.24, f32[2,256,256]{2,1,0:T(8,128)} %bitcast.20), custom_call_target="tpu_custom_call" | custom-call | flops 720896 | bytes 1572864 | tf_op jit(solution)/shard_map/stage/pallas_call | solution.py:475
  9.7 0.7 %collective-permute-start.3 = (bf16[256,128]{1,0:T(8,128)(2,1)S(1)}, bf16[256,128]{1,0:T(8,128)(2,1)S(1)}, u32[]{:S(2)}, u32[]{:S(2)}) collective-permute-start(bf16[256,128]{1,0:T(8,128)(2,1)S(1)} %collective-permute-done.1.below0.rest_2_.rest_8_), channel_id=1, source_target_pairs={{0,12},{4,0},{8,4},{12,8},{16,28},{20,16},{24,20},{28,24},{1,13},{... | collective-permute-start | bytes 196616 | tf_op jit(solution)/shard_map/ppermute | solution.py:51
  10.5 3.7 %collective-permute-done.2.below1.rest_3_.rest_12_ = bf16[272,128]{1,0:T(8,128)(2,1)S(1)} collective-permute-done((bf16[272,128]{1,0:T(8,128)(2,1)S(1)}, bf16[272,128]{1,0:T(8,128)(2,1)S(1)}, u32[]{:S(2)}, u32[]{:S(2)}) %collective-permute-start.2) | collective-permute-done | bytes 69664 | tf_op jit(solution)/shard_map/ppermute | solution.py:51
  14.3 6.9 %first_pass.1 = (f32[2,3,384,128]{3,2,1,0:T(8,128)S(1)}, f32[2,3,384,128]{3,2,1,0:T(8,128)S(1)}, f32[3,256,256]{2,1,0:T(8,128)S(1)}, bf16[800,128]{1,0:T(8,128)(...) custom-call(s32[9]{0:T(128)S(1)} %pad_add_fusion.meta, ...), custom_call_target="tpu_custom_call", output_to_operand_aliasing={{0}: (6, {}), {1}: (7, {})} | custom-call | flops 2147483648 | bytes 1572864 | tf_op jit(solution)/shard_map/first_pass/pallas_call | solution.py:475
  21.2 0.7 collective-permute-start.5
  22.0 5.2 %collective-permute-done.6.rest_5_.rest_6_.rest_10_.rest_11_.mid_above.mid_below = bf16[2,128,128]{2,1,0:T(8,128)(2,1)S(1)} collective-permute-done((bf16[2,128,128]{2,1,0:T(8,128)(2,1)S(1)}, bf16[2,128,128]{2,1,0:T(8,128)(2,1)S(1)}, u32[]{:S(2)}, u32[]{:S(2)}) %collective-permute-start.6) | collective-permute-done | bytes 65568 | tf_op jit(solution)/shard_map/ppermute | solution.py:51
  27.4 2.5 %weigh.1 = (f32[3,384,128]{2,1,0:T(8,128)S(1)}, f32[2,256,256]{2,1,0:T(8,128)S(1)}, f32[2,256,256]{2,1,0:T(8,128)S(1)}, f32[2,256,256]{2,1,0:T(8,128)S(1)}, bf16...) custom-call(bf16[16,128]{1,0:T(8,128)(2,1)S(1)} %fusion.5.rest_0_, ...), custom_call_target="tpu_custom_call" | custom-call | flops 1327104 | bytes 3145728 | tf_op jit(solution)/shard_map/weigh/pallas_call | solution.py:475
  29.9 3.3 %collective-permute-done.7.from_above.from_below = bf16[2,2,128,128]{3,2,1,0:T(8,128)(2,1)S(1)} collective-permute-done((bf16[2,2,128,128]{3,2,1,0:T(8,128)(2,1)S(1)}, bf16[2,2,128,128]{3,2,1,0:T(8,128)(2,1)S(1)}, u32[]{:S(2)}, u32[]{:S(2)}) %collective-permute-start.7) | collective-permute-done | bytes 131104 | tf_op jit(solution)/shard_map/ppermute | solution.py:51
  33.2 6.3 %second_pass.1 = (f32[2,256,256]{2,1,0:T(8,128)S(1)}, f32[2,256,128]{2,1,0:T(8,128)S(1)}, bf16[2,384,128]{2,1,0:T(8,128)(2,1)S(1)}, f32[2,128,128]{2,1,0:T(8,128...) custom-call(s32[9]{0:T(128)S(1)} %pad_add_fusion.meta, ...), custom_call_target="tpu_custom_call" | custom-call | flops 2147483648 | tf_op jit(solution)/shard_map/second_pass/pallas_call | solution.py:475
  39.6 0.5 collective-permute-start.8
  40.1 0.9 %collective-permute-done.11.came = bf16[3,128,256]{2,1,0:T(8,128)(2,1)S(1)} collective-permute-done((bf16[3,128,256]{2,1,0:T(8,128)(2,1)S(1)}, bf16[3,128,256]{2,1,0:T(8,128)(2,1)S(1)}, u32[]{:S(2)}, u32[]{:S(2)}) %collective-permute-start.11) | collective-permute-done | bytes 196640 | tf_op jit(solution)/shard_map/ppermute | solution.py:56
  41.0 0.1 halve.1.rest_0_.held
  41.1 1.3 %collective-permute-start.16 = (bf16[3,128,256]{2,1,0:T(8,128)(2,1)S(1)}, bf16[3,128,256]{2,1,0:T(8,128)(2,1)S(1)}, u32[]{:S(2)}, u32[]{:S(2)}) collective-permute-start(bf16[3,128,256]{2,1,0:T(8,128)(2,1)S(1)} %halve.1.rest_0_.held), channel_id=1, source_target_pairs={{0,8},{4,12},{8,0},{12,4},{16,24},{20,28},{24,16},{28,20},{1,9},{5... | collective-permute-start | bytes 589832 | tf_op jit(solution)/shard_map/ppermute | solution.py:56
  42.5 1.3 %collective-permute-start.10 = (bf16[2,128,128]{2,1,0:T(8,128)(2,1)S(1)}, bf16[2,128,128]{2,1,0:T(8,128)(2,1)S(1)}, u32[]{:S(2)}, u32[]{:S(2)}) collective-permute-start(bf16[2,128,128]{2,1,0:T(8,128)(2,1)S(1)} %get-tuple-element.51), channel_id=1, source_target_pairs={{0,16},{4,20},{8,24},{12,28},{16,0},{20,4},{24,8},{28,12},{1,17},{... | collective-permute-start | bytes 196616 | tf_op jit(solution)/shard_map/ppermute | solution.py:51
  43.7 1.1 %collective-permute-done.8.from_left = bf16[2,384,128]{2,1,0:T(8,128)(2,1)S(1)} collective-permute-done((bf16[2,384,128]{2,1,0:T(8,128)(2,1)S(1)}, bf16[2,384,128]{2,1,0:T(8,128)(2,1)S(1)}, u32[]{:S(2)}, u32[]{:S(2)}) %collective-permute-start.8) | collective-permute-done | bytes 196640 | tf_op jit(solution)/shard_map/ppermute | solution.py:51
  44.8 1.1 %collective-permute-start.9 = (bf16[2,128,128]{2,1,0:T(8,128)(2,1)S(1)}, bf16[2,128,128]{2,1,0:T(8,128)(2,1)S(1)}, u32[]{:S(2)}, u32[]{:S(2)}) collective-permute-start(bf16[2,128,128]{2,1,0:T(8,128)(2,1)S(1)} %add_rim.1), channel_id=1, source_target_pairs={{0,16},{4,20},{8,24},{12,28},{16,0},{20,4},{24,8},{28,12},{1,17},{... | collective-permute-start | bytes 196616 | tf_op jit(solution)/shard_map/ppermute | solution.py:51
  45.9 3.3 %collective-permute-done.10.above1 = bf16[2,128,128]{2,1,0:T(8,128)(2,1)S(1)} collective-permute-done((bf16[2,128,128]{2,1,0:T(8,128)(2,1)S(1)}, bf16[2,128,128]{2,1,0:T(8,128)(2,1)S(1)}, u32[]{:S(2)}, u32[]{:S(2)}) %collective-permute-start.10) | collective-permute-done | bytes 65568 | tf_op jit(solution)/shard_map/ppermute | solution.py:51
  49.2 3.4 %collective-permute-done.9.above0 = bf16[2,128,128]{2,1,0:T(8,128)(2,1)S(1)} collective-permute-done((bf16[2,128,128]{2,1,0:T(8,128)(2,1)S(1)}, bf16[2,128,128]{2,1,0:T(8,128)(2,1)S(1)}, u32[]{:S(2)}, u32[]{:S(2)}) %collective-permute-start.9) | collective-permute-done | bytes 65568 | tf_op jit(solution)/shard_map/ppermute | solution.py:51
  52.8 6.9 %collective-permute-start.12 = (bf16[2,128,256]{2,1,0:T(8,128)(2,1)S(1)}, bf16[2,128,256]{2,1,0:T(8,128)(2,1)S(1)}, u32[]{:S(2)}, u32[]{:S(2)}) collective-permute-start(bf16[2,128,256]{2,1,0:T(8,128)(2,1)S(1)} %get-tuple-element.54.refs_0_.rest_0_), channel_id=1, source_target_pairs={{0,1},{1,0},{2,3},{3,2},{4,5},{5,4},{6,7},{7,6},{8,9},{9,8},{10,11... | collective-permute-start | bytes 393224 | tf_op jit(solution)/shard_map/ppermute | solution.py:56
  59.9 2.8 %collective-permute-done.12.refs_1_ = bf16[2,128,256]{2,1,0:T(8,128)(2,1)S(1)} collective-permute-done((bf16[2,128,256]{2,1,0:T(8,128)(2,1)S(1)}, bf16[2,128,256]{2,1,0:T(8,128)(2,1)S(1)}, u32[]{:S(2)}, u32[]{:S(2)}) %collective-permute-start.12) | collective-permute-done | bytes 131104 | tf_op jit(solution)/shard_map/ppermute | solution.py:56
  62.7 0.1 collective-permute-start.14
  62.9 2.0 %collective-permute-start.15 = (bf16[2,128,256]{2,1,0:T(8,128)(2,1)S(1)}, bf16[2,128,256]{2,1,0:T(8,128)(2,1)S(1)}, u32[]{:S(2)}, u32[]{:S(2)}) collective-permute-start(bf16[2,128,256]{2,1,0:T(8,128)(2,1)S(1)} %get-tuple-element.57.second), channel_id=1, source_target_pairs={{0,1},{1,0},{2,3},{3,2},{4,5},{5,4},{6,7},{7,6},{8,9},{9,8},{10,11... | collective-permute-start | bytes 393224 | tf_op jit(solution)/shard_map/ppermute | solution.py:56
  64.9 2.9 %collective-permute-done.14.first_came.rest_0_ = bf16[2,128,256]{2,1,0:T(8,128)(2,1)S(1)} collective-permute-done((bf16[2,128,256]{2,1,0:T(8,128)(2,1)S(1)}, bf16[2,128,256]{2,1,0:T(8,128)(2,1)S(1)}, u32[]{:S(2)}, u32[]{:S(2)}) %collective-permute-start.14) | collective-permute-done | bytes 131104 | tf_op jit(solution)/shard_map/ppermute | solution.py:56
  67.9 1.2 %settle.1 = (f32[2,256,256]{2,1,0:T(8,128)}, f32[2,256,256]{2,1,0:T(8,128)}) custom-call(bf16[2,128,256]{2,1,0:T(8,128)(2,1)S(1)} %get-tuple-element.56.first, bf16[2,128,256]{2,1,0:T(8,128)(2,1)S(1)} %collective-permute-done.14.first_came.rest_0_, bf16[2,128,256]{2,1,0:T(8,128)(2,1)S(1)} %get-tuple-element.57.second, ...), custom_call_target="tpu_custom_call" | custom-call | flops 262144 | tf_op jit(solution)/shard_map/settle/pallas_call | solution.py:475
  69.1 0.1 collective-permute-done.18
  69.3 0.9 %convert_add_fusion = f32[1,2,256,256]{3,2,1,0:T(8,128)} fusion(f32[1,2,256,256]{3,2,1,0:T(8,128)S(1)} %copy-done, bf16[1,2,128,256]{3,2,1,0:T(8,128)(2,1)S(1)} %bitcast.19, bf16[1,2,128,256]{3,2,1,0:T(8,128)(2,1)S(1)} %bitcast.29, pred[]{:T(512)} %eq.8), kind=kLoop, calls=%fused_computation | loop fusion | flops 1441792 | bytes 1310721 | tf_op jit(solution)/shard_map/add | solution.py:608
  (37 shorter events, 1.5 us)
Async XLA Ops:
  0.6 6.7 %copy-start.1 = (s32[1,1,4,2]{2,3,1,0:T(2,128)S(1)}, s32[1,1,4,2]{2,3,1,0:T(2,128)}, u32[]{:S(2)}) copy-start(s32[1,1,4,2]{2,3,1,0:T(2,128)} %param.12) | copy-start | bytes 100
  1.8 7.9 %collective-permute-start.1 = (bf16[256,128]{1,0:T(8,128)(2,1)S(1)}, bf16[256,128]{1,0:T(8,128)(2,1)S(1)}, u32[]{:S(2)}, u32[]{:S(2)}) collective-permute-start(bf16[256,128]{1,0:T(8,128)(2,1)S(1)} %bitcast.30), channel_id=1, source_target_pairs={{0,16},{4,20},{8,24},{12,28},{16,0},{20,4},{24,8},{28,12},{1,17},{... | collective-permute-start | bytes 196616 | tf_op jit(solution)/shard_map/ppermute | solution.py:51
  5.9 8.3 %collective-permute-start = (bf16[2,256,128]{2,1,0:T(8,128)(2,1)S(1)}, bf16[2,256,128]{2,1,0:T(8,128)(2,1)S(1)}, u32[]{:S(2)}, u32[]{:S(2)}) collective-permute-start(bf16[2,256,128]{2,1,0:T(8,128)(2,1)S(1)} %slice.12), channel_id=1, source_target_pairs={{0,12},{4,0},{8,4},{12,8},{16,28},{20,16},{24,20},{28,24},{1,13},{... | collective-permute-start | bytes 393224 | tf_op jit(solution)/shard_map/ppermute | solution.py:51
  7.6 6.6 %collective-permute-start.2 = (bf16[272,128]{1,0:T(8,128)(2,1)S(1)}, bf16[272,128]{1,0:T(8,128)(2,1)S(1)}, u32[]{:S(2)}, u32[]{:S(2)}) collective-permute-start(bf16[272,128]{1,0:T(8,128)(2,1)S(1)} %pad_maximum_fusion), channel_id=1, source_target_pairs={{0,16},{4,20},{8,24},{12,28},{16,0},{20,4},{24,8},{28,12},{1,17},{... | collective-permute-start | bytes 208904 | tf_op jit(solution)/shard_map/ppermute | solution.py:51
  9.7 4.5 %collective-permute-start.3 = (bf16[256,128]{1,0:T(8,128)(2,1)S(1)}, bf16[256,128]{1,0:T(8,128)(2,1)S(1)}, u32[]{:S(2)}, u32[]{:S(2)}) collective-permute-start(bf16[256,128]{1,0:T(8,128)(2,1)S(1)} %collective-permute-done.1.below0.rest_2_.rest_8_), channel_id=1, source_target_pairs={{0,12},{4,0},{8,4},{12,8},{16,28},{20,16},{24,20},{28,24},{1,13},{... | collective-permute-start | bytes 196616 | tf_op jit(solution)/shard_map/ppermute | solution.py:51
  21.2 6.0 %collective-permute-start.4 = (bf16[800,128]{1,0:T(8,128)(2,1)S(1)}, bf16[800,128]{1,0:T(8,128)(2,1)S(1)}, u32[]{:S(2)}, u32[]{:S(2)}) collective-permute-start(bf16[800,128]{1,0:T(8,128)(2,1)S(1)} %get-tuple-element.36), channel_id=1, source_target_pairs={{0,4},{4,0},{8,12},{12,8},{16,20},{20,16},{24,28},{28,24},{1,5},{5... | collective-permute-start | bytes 614408 | tf_op jit(solution)/shard_map/ppermute | solution.py:56
  21.2 6.0 %collective-permute-start.5 = (bf16[800,128]{1,0:T(8,128)(2,1)S(1)}, bf16[800,128]{1,0:T(8,128)(2,1)S(1)}, u32[]{:S(2)}, u32[]{:S(2)}) collective-permute-start(bf16[800,128]{1,0:T(8,128)(2,1)S(1)} %get-tuple-element.37), channel_id=1, source_target_pairs={{0,0},{4,8},{8,4},{12,12},{16,16},{20,24},{24,20},{28,28},{1,1},{5... | collective-permute-start | bytes 614408 | tf_op jit(solution)/shard_map/ppermute | solution.py:65
  21.9 5.3 %collective-permute-start.6 = (bf16[2,128,128]{2,1,0:T(8,128)(2,1)S(1)}, bf16[2,128,128]{2,1,0:T(8,128)(2,1)S(1)}, u32[]{:S(2)}, u32[]{:S(2)}) collective-permute-start(bf16[2,128,128]{2,1,0:T(8,128)(2,1)S(1)} %get-tuple-element.38), channel_id=1, source_target_pairs={{0,16},{4,20},{8,24},{12,28},{16,0},{20,4},{24,8},{28,12},{1,17},{... | collective-permute-start | bytes 196616 | tf_op jit(solution)/shard_map/ppermute | solution.py:51
  27.3 5.9 %collective-permute-start.7 = (bf16[2,2,128,128]{3,2,1,0:T(8,128)(2,1)S(1)}, bf16[2,2,128,128]{3,2,1,0:T(8,128)(2,1)S(1)}, u32[]{:S(2)}, u32[]{:S(2)}) collective-permute-start(bf16[2,2,128,128]{3,2,1,0:T(8,128)(2,1)S(1)} %between.1.rest_4_), channel_id=1, source_target_pairs={{0,16},{4,20},{8,24},{12,28},{16,0},{20,4},{24,8},{28,12},{1,17},{... | collective-permute-start | bytes 393224 | tf_op jit(solution)/shard_map/ppermute | solution.py:51
  39.5 1.5 %collective-permute-start.11 = (bf16[3,128,256]{2,1,0:T(8,128)(2,1)S(1)}, bf16[3,128,256]{2,1,0:T(8,128)(2,1)S(1)}, u32[]{:S(2)}, u32[]{:S(2)}) collective-permute-start(bf16[3,128,256]{2,1,0:T(8,128)(2,1)S(1)} %get-tuple-element.53), channel_id=1, source_target_pairs={{0,4},{4,0},{8,12},{12,8},{16,20},{20,16},{24,28},{28,24},{1,5},{5... | collective-permute-start | bytes 589832 | tf_op jit(solution)/shard_map/ppermute | solution.py:56
  39.6 5.1 %collective-permute-start.8 = (bf16[2,384,128]{2,1,0:T(8,128)(2,1)S(1)}, bf16[2,384,128]{2,1,0:T(8,128)(2,1)S(1)}, u32[]{:S(2)}, u32[]{:S(2)}) collective-permute-start(bf16[2,384,128]{2,1,0:T(8,128)(2,1)S(1)} %get-tuple-element.49), channel_id=1, source_target_pairs={{0,4},{4,8},{8,12},{12,0},{16,20},{20,24},{24,28},{28,16},{1,5},{5... | collective-permute-start | bytes 589832 | tf_op jit(solution)/shard_map/ppermute | solution.py:51
  41.1 18.6 %collective-permute-start.16 = (bf16[3,128,256]{2,1,0:T(8,128)(2,1)S(1)}, bf16[3,128,256]{2,1,0:T(8,128)(2,1)S(1)}, u32[]{:S(2)}, u32[]{:S(2)}) collective-permute-start(bf16[3,128,256]{2,1,0:T(8,128)(2,1)S(1)} %halve.1.rest_0_.held), channel_id=1, source_target_pairs={{0,8},{4,12},{8,0},{12,4},{16,24},{20,28},{24,16},{28,20},{1,9},{5... | collective-permute-start | bytes 589832 | tf_op jit(solution)/shard_map/ppermute | solution.py:56
  42.5 6.8 %collective-permute-start.10 = (bf16[2,128,128]{2,1,0:T(8,128)(2,1)S(1)}, bf16[2,128,128]{2,1,0:T(8,128)(2,1)S(1)}, u32[]{:S(2)}, u32[]{:S(2)}) collective-permute-start(bf16[2,128,128]{2,1,0:T(8,128)(2,1)S(1)} %get-tuple-element.51), channel_id=1, source_target_pairs={{0,16},{4,20},{8,24},{12,28},{16,0},{20,4},{24,8},{28,12},{1,17},{... | collective-permute-start | bytes 196616 | tf_op jit(solution)/shard_map/ppermute | solution.py:51
  44.8 7.9 %collective-permute-start.9 = (bf16[2,128,128]{2,1,0:T(8,128)(2,1)S(1)}, bf16[2,128,128]{2,1,0:T(8,128)(2,1)S(1)}, u32[]{:S(2)}, u32[]{:S(2)}) collective-permute-start(bf16[2,128,128]{2,1,0:T(8,128)(2,1)S(1)} %add_rim.1), channel_id=1, source_target_pairs={{0,16},{4,20},{8,24},{12,28},{16,0},{20,4},{24,8},{28,12},{1,17},{... | collective-permute-start | bytes 196616 | tf_op jit(solution)/shard_map/ppermute | solution.py:51
  52.7 7.1 %collective-permute-start.13 = (bf16[2,128,256]{2,1,0:T(8,128)(2,1)S(1)}, bf16[2,128,256]{2,1,0:T(8,128)(2,1)S(1)}, u32[]{:S(2)}, u32[]{:S(2)}) collective-permute-start(bf16[2,128,256]{2,1,0:T(8,128)(2,1)S(1)} %get-tuple-element.55.refs_2_), channel_id=1, source_target_pairs={{0,2},{1,3},{2,0},{3,1},{4,6},{5,7},{6,4},{7,5},{8,10},{9,11},{10,... | collective-permute-start | bytes 393224 | tf_op jit(solution)/shard_map/ppermute | solution.py:56
  52.8 9.8 %collective-permute-start.12 = (bf16[2,128,256]{2,1,0:T(8,128)(2,1)S(1)}, bf16[2,128,256]{2,1,0:T(8,128)(2,1)S(1)}, u32[]{:S(2)}, u32[]{:S(2)}) collective-permute-start(bf16[2,128,256]{2,1,0:T(8,128)(2,1)S(1)} %get-tuple-element.54.refs_0_.rest_0_), channel_id=1, source_target_pairs={{0,1},{1,0},{2,3},{3,2},{4,5},{5,4},{6,7},{7,6},{8,9},{9,8},{10,11... | collective-permute-start | bytes 393224 | tf_op jit(solution)/shard_map/ppermute | solution.py:56
  59.8 9.5 %copy-start = (f32[1,2,256,256]{3,2,1,0:T(8,128)S(1)}, f32[1,2,256,256]{3,2,1,0:T(8,128)}, u32[]{:S(2)}) copy-start(f32[1,2,256,256]{3,2,1,0:T(8,128)} %param.10) | copy-start | bytes 1572868
  59.8 8.0 %collective-permute-start.17 = (bf16[3,128,256]{2,1,0:T(8,128)(2,1)S(1)}, bf16[3,128,256]{2,1,0:T(8,128)(2,1)S(1)}, u32[]{:S(2)}, u32[]{:S(2)}) collective-permute-start(bf16[3,128,256]{2,1,0:T(8,128)(2,1)S(1)} %add.23.held), channel_id=1, source_target_pairs={{0,24},{4,28},{8,16},{12,20},{16,8},{20,12},{24,0},{28,4},{1,25},{... | collective-permute-start | bytes 589832 | tf_op jit(solution)/shard_map/ppermute | solution.py:56
  62.7 5.0 %collective-permute-start.14 = (bf16[2,128,256]{2,1,0:T(8,128)(2,1)S(1)}, bf16[2,128,256]{2,1,0:T(8,128)(2,1)S(1)}, u32[]{:S(2)}, u32[]{:S(2)}) collective-permute-start(bf16[2,128,256]{2,1,0:T(8,128)(2,1)S(1)} %get-tuple-element.56.first), channel_id=1, source_target_pairs={{0,2},{1,3},{2,0},{3,1},{4,6},{5,7},{6,4},{7,5},{8,10},{9,11},{10,... | collective-permute-start | bytes 393224 | tf_op jit(solution)/shard_map/ppermute | solution.py:56
  62.9 5.0 %collective-permute-start.15 = (bf16[2,128,256]{2,1,0:T(8,128)(2,1)S(1)}, bf16[2,128,256]{2,1,0:T(8,128)(2,1)S(1)}, u32[]{:S(2)}, u32[]{:S(2)}) collective-permute-start(bf16[2,128,256]{2,1,0:T(8,128)(2,1)S(1)} %get-tuple-element.57.second), channel_id=1, source_target_pairs={{0,1},{1,0},{2,3},{3,2},{4,5},{5,4},{6,7},{7,6},{8,9},{9,8},{10,11... | collective-permute-start | bytes 393224 | tf_op jit(solution)/shard_map/ppermute | solution.py:56
  67.8 1.4 %collective-permute-start.18 = (bf16[2,128,256]{2,1,0:T(8,128)(2,1)S(1)}, bf16[2,128,256]{2,1,0:T(8,128)(2,1)S(1)}, u32[]{:S(2)}, u32[]{:S(2)}) collective-permute-start(bf16[2,128,256]{2,1,0:T(8,128)(2,1)S(1)} %update.1), channel_id=1, source_target_pairs={{0,4},{4,0},{8,12},{12,8},{16,20},{20,16},{24,28},{28,24},{1,5},{5... | collective-permute-start | bytes 393224 | tf_op jit(solution)/shard_map/ppermute | solution.py:56

commit v5 on v4

--- a/solution.py
+++ b/solution.py
@@ -17,6 +17,7 @@
 SLOTS = 4
 SPAN = TS + OVER
 L = 128
+HALF = PS // 2
 CH = 32
 COUNT = 2 * SLOTS
 CARD = 16
@@ -37,9 +38,9 @@
     scale = np.float32(1.0 / math.sqrt(PS))
     re = (np.cos(angles) * scale).astype(ml_dtypes.bfloat16)
     im = (-np.sin(angles) * scale).astype(ml_dtypes.bfloat16)
-    fwd = np.block([[re, -im], [im, re]])
-    bwd = np.block([[re, im], [-im, re]])
-    return jnp.asarray(fwd), jnp.asarray(bwd)
+    half = np.concatenate([re[:HALF], re[HALF : HALF + 1], im[1:HALF]])
+    order = np.concatenate([indices[: HALF + 1], indices[:HALF:-1]])
+    return jnp.asarray(half), jnp.asarray(half.T), jnp.asarray(np.eye(PS, dtype=half.dtype)[order])
 
 
 def shifted(value, rows, cols):
@@ -103,7 +104,21 @@
     return [jnp.where(past, r[0], z), jnp.where(past, r[1], r[0]), jnp.where(past, z, r[1])]
 
 
-def visit_pair(p, meta, ext, probe, amps, fwd, bwd, acc, pnum, win, X, Y, W):
+def split(pr, pi, qr, qi, first):
+    planes = (pr - qi, pr + qi, pi + qr, pi - qr)
+    if first is None:
+        return planes
+    return [jnp.where(first, v, w) for v, w in zip((pr, qr, pi, qi), planes)]
+
+
+def joined(lr, hr, li, hi, first):
+    planes = (lr + hr, li - hi, li + hi, hr - lr)
+    if first is None:
+        return planes
+    return [jnp.where(first, v, w) for v, w in zip((lr, hr, li, hi), planes)]
+
+
+def visit_pair(p, meta, ext, probe, amps, half, turned, acc, pnum, win, X, Y, W):
     N = PS
     used = jnp.where(2 * p + 1 < meta[COUNT], 1.0, 0.0).astype(f32)
     corners = [(meta[4 * p + 2 * i], meta[4 * p + 2 * i + 1]) for i in range(2)]
@@ -120,31 +135,58 @@
             pr, pi = probe[0, rows, :], probe[1, rows, :]
             win[i, 0, rows, :] = w[0]
             win[i, 1, rows, :] = w[1]
-            X[i, rows, :] = (pr * w[0] - pi * w[1]).astype(bf16)
-            X[i, N + k : N + k + CH, :] = (pr * w[1] + pi * w[0]).astype(bf16)
+            X[i, rows, :N] = (pr * w[0] - pi * w[1]).astype(bf16)
+            X[i, rows, N:] = (pr * w[1] + pi * w[0]).astype(bf16)
             pnum[2, rows, :] += w[0] * w[0] + w[1] * w[1]
 
-    def columns(i, table):
-        t = jnp.dot(table[...], X[i], preferred_element_type=f32)
-        Y[i, :, :N] = t[:N].astype(bf16)
-        Y[i, :, N:] = t[N:].astype(bf16)
-
-    def rows_of(i, table):
-        W[i] = jnp.dot(Y[i], table[...], preferred_element_type=f32)
+    def columns(i):
+        t = jnp.dot(half[...], X[i], preferred_element_type=f32)
+        for k in range(0, HALF, CH):
+            p, q = t[k : k + CH], t[HALF + k : HALF + k + CH]
+            first = lax.broadcasted_iota(jnp.int32, (CH, N), 0) == 0 if k == 0 else None
+            planes = split(p[:, :N], p[:, N:], q[:, :N], q[:, N:], first)
+            for j, v in enumerate(planes):
+                Y[i, j * HALF + k : j * HALF + k + CH, :] = v.astype(bf16)
+
+    def rows_of(i):
+        W[i] = jnp.dot(Y[i], turned[...], preferred_element_type=f32)
 
     def compare(i):
+        first = lax.broadcasted_iota(jnp.int32, (CH, L), 1) == 0
+        top = lax.broadcasted_iota(jnp.int32, (CH, N), 0) == 0
+        for k in range(0, HALF, CH):
+            resid = []
+            for h in range(2):
+                rows = slice(h * HALF + k, h * HALF + k + CH)
+                at = slice(N + h * HALF + k, N + h * HALF + k + CH)
+                planes = split(W[i, rows, :L], W[i, at, :L], W[i, rows, L:], W[i, at, L:], first)
+                a = amps[2 * p + i, rows, :].astype(f32)
+                wr = jnp.concatenate([planes[0], planes[1]], 1)
+                wi = jnp.concatenate([planes[2], planes[3]], 1)
+                f = a * lax.rsqrt(wr * wr + wi * wi + smoothing) - 1.0
+                resid.append((wr * f, wi * f))
+            (lr, li), (hr, hi) = resid
+            for j, v in enumerate(joined(lr, hr, li, hi, top if k == 0 else None)):
+                X[i, j % 2 * HALF + k : j % 2 * HALF + k + CH, j // 2 * N : j // 2 * N + N] = v.astype(bf16)
+
+    def columns_back(i):
+        t = jnp.dot(turned[...], X[i], preferred_element_type=f32)
+        first = lax.broadcasted_iota(jnp.int32, (CH, L), 1) == 0
         for k in range(0, N, CH):
-            wr, wi = W[i, k : k + CH, :N], W[i, k : k + CH, N:]
-            a = amps[2 * p + i, k : k + CH, :].astype(f32)
-            f = a * lax.rsqrt(wr * wr + wi * wi + smoothing) - 1.0
-            X[i, k : k + CH, :] = (wr * f).astype(bf16)
-            X[i, N + k : N + k + CH, :] = (wi * f).astype(bf16)
+            v = t[k : k + CH]
+            planes = joined(v[:, :L], v[:, L:N], v[:, N : N + L], v[:, N + L :], first)
+            for j, v in enumerate(planes):
+                at = j // 2 * N + k
+                Y[i, at : at + CH, j % 2 * L : j % 2 * L + L] = v.astype(bf16)
+
+    def rows_back(i):
+        W[i] = jnp.dot(Y[i], half[...], preferred_element_type=f32)
 
     def gather(i):
         r, c = corners[i]
         for k in range(0, N, CH):
             rows = slice(k, k + CH)
-            br, bi = W[i, rows, :N], W[i, rows, N:]
+            br, bi = W[i, rows, :], W[i, N + k : N + k + CH, :]
             pr, pi = probe[0, rows, :], probe[1, rows, :]
             wr, wi = win[i, 0, rows, :], win[i, 1, rows, :]
             pnum[0, rows, :] += wr * br + wi * bi
@@ -154,18 +196,18 @@
                     acc[ch, j, pl.ds(r + k, CH), :] += u
 
     leave(0)
-    columns(0, fwd)
+    columns(0)
     leave(1)
-    rows_of(0, bwd)
-    columns(1, fwd)
+    rows_of(0)
+    columns(1)
     compare(0)
-    rows_of(1, bwd)
-    columns(0, bwd)
+    rows_of(1)
+    columns_back(0)
     compare(1)
-    rows_of(0, fwd)
-    columns(1, bwd)
+    rows_back(0)
+    columns_back(1)
     gather(0)
-    rows_of(1, fwd)
+    rows_back(1)
     gather(1)
 
 
@@ -176,8 +218,12 @@
     return copies
 
 
-def stage(own_h, dual_h, probe_h, ext, acc, probe, sems, own, dual):
-    copies = fetch([(own_h, own), (dual_h, dual), (probe_h, probe)], sems)
+def stage(
+    below, own_h, dual_h, probe_h, amps_h, order_h, ext, acc, probe, ordered, sems, own, dual, amps, order
+):
+    copies = fetch(
+        [(own_h, own), (dual_h, dual), (probe_h, probe), (amps_h, amps), (order_h, order)], sems
+    )
     acc[:, 2] = jnp.zeros((2, SPAN, L), f32)
     copies[0].wait()
     for j in range(2):
@@ -188,7 +234,11 @@
     for j in range(2):
         cols = slice(j * L, (j + 1) * L)
         acc[:, j, :TS, :] = -penalty * dual[:, :, cols]
-    copies[2].wait()
+    for copy in copies[2:]:
+        copy.wait()
+    for k in range(SLOTS):
+        rows = jnp.dot(order[...], amps[k], preferred_element_type=f32).astype(bf16)
+        ordered[k] = jnp.dot(rows, order[...], preferred_element_type=f32).astype(bf16)
 
 
 def first_pass(
@@ -464,7 +514,7 @@
     return pltpu.with_memory_space_constraint(value, pltpu.VMEM)
 
 
-def call(body, name, outs, scratch=(), scalars=0, far=0, copies=0, aliases=None, held=False, flops=0):
+def call(body, name, outs, scratch=(), scalars=0, far=0, copies=0, aliases=None, held=0, flops=0):
     def run(*operands):
         near = len(operands) - scalars - far
         spaces = [None] * (scalars + near) + [pltpu.HBM] * far
@@ -477,8 +527,8 @@
             in_specs=[S] * scalars + [V] * near + [H] * far,
             out_specs=[V] * len(outs),
             out_shape=[
-                pltpu.VMEM(shape, dtype) if held else jax.ShapeDtypeStruct(shape, dtype)
-                for shape, dtype in outs
+                pltpu.VMEM(shape, dtype) if k < held else jax.ShapeDtypeStruct(shape, dtype)
+                for k, (shape, dtype) in enumerate(outs)
             ],
             scratch_shapes=[
                 pltpu.SemaphoreType.DMA((copies,)) if one is None else pltpu.VMEM(*one)
@@ -499,20 +549,20 @@
 
 
 PLANES = ((2, PS, PS), f32)
-PASS = SLOTS * 4 * 8 * PS**3
+PASS = SLOTS * 4 * 4 * PS**3
 WORK = [
     ((2, 2, PS, PS), f32),
+    ((2, PS, 2 * PS), bf16),
     ((2, 2 * PS, PS), bf16),
-    ((2, PS, 2 * PS), bf16),
-    ((2, PS, 2 * PS), f32),
+    ((2, 2 * PS, PS), f32),
 ]
-TABLE = ((2 * PS, 2 * PS), bf16)
+TABLE = ((PS, PS), bf16)
 WIDE = ((2, 3, SPAN, L), f32)
 SUMS = ((3, PS, PS), f32)
 
 
 def shards(consensus, duals, probes, amplitudes, offsets, counts):
-    fwd, bwd = dft_tables()
+    fwd, bwd, order = dft_tables()
     n = lax.axis_size("tile")
     index = lax.axis_index("tile")
     own = consensus[0]
@@ -537,11 +587,12 @@
     below.append(shifted(below[0], 0, -1))
     cards = [card] if two else [card, shifted(card, 1, 0)]
 
+    *staged, amps = call(
+        stage, "stage", [WIDE, WIDE, PLANES, measured], [None, PLANES, PLANES, measured, TABLE], 0, 5, 5,
+        held=3,
+    )(below[0], own, dual, probe, amps, order)
+    staged = [pinned(v) for v in staged]
     inputs = (own, dual, probe, amps, fwd, bwd)
-    staged = call(
-        stage, "stage", [WIDE, WIDE, PLANES], [None, PLANES, PLANES], 0, 3, 3, held=True
-    )(own, dual, probe)
-    staged = [pinned(v) for v in staged]
     rim = ((2, OVER, L), bf16)
     ext, acc, pnum, side, inner, *mids = call(
         functools.partial(first_pass, two), "first_pass",
@@ -566,7 +617,7 @@
         [((3, SPAN, L), f32), PLANES, PLANES, PLANES, measured, TABLE, TABLE],
         [None, ((2, PS, L), f32), ((3, SPAN + 2 * OVER, L), f32), ((24, L), f32),
          pltpu.SMEM((24, L), f32)],
-        0, 6, 7, held=True,
+        0, 6, 7, held=7,
     )(*cards, flags, side, inner, rims[0], acc, pnum, right, below[0], below[2], mid_above, mid_below,
       below[1], *inputs)
     weight, *inputs = [pinned(v) for v in (weight, *inputs)]

time: 70.2 us -> 67.4 us (0.960)
  the two profiles are of different devices: /device:TPU:0 before, /device:TPU:9 now
where the time goes in v5:
time: 67.4 us; the launch traced here: 66.9 us
  starting transfers between devices  29 us (43%)
  waiting for transfers between devices  19.4 us (29%)
  Pallas kernels  13.6 us (20%)
  other arithmetic  2.11 us (3%)
  between operations  1.45 us (2%)
  local copies, waits for them, and re-layouts  1.38 us (2%)
    ppermute x9, starting transfers between devices, shifted(): return lax.ppermute(value, 'tile', pairs)  17.2 us
    pallas_call x12, Pallas kernels, run(): pl.pallas_call(body, in_specs=[S] * scalars + [V] * near + [H] * far, out...  13.6 us
    ppermute x9, starting transfers between devices, swapped(): return lax.ppermute(value, axis, [(i, i ^ bit) for i in range(n)])  11.2 us
    ppermute x9, waiting for transfers between devices, swapped(): return lax.ppermute(value, axis, [(i, i ^ bit) for i in range(n)])  9.85 us
    ppermute x9, waiting for transfers between devices, shifted(): return lax.ppermute(value, 'tile', pairs)  9.52 us
  transfers between devices with their start and end apart: 19, of which 9 were waited for; matrix products, arithmetic and copies ran while one was open for 1% of the time, Pallas kernels for 9%

profile of v5, /device:TPU:9, one launch (start us, length us, event | category | flops | bytes accessed | tf_op | source)
XLA Modules:
  0.0 66.9 jit_solution(14221734651685016944)
XLA Ops:
  0.6 1.1 %bitcast_convert_fusion = bf16[2,256,256]{2,1,0:T(8,128)(2,1)S(1)} fusion(f32[1,2,256,256]{3,2,1,0:T(8,128)} %param.9), kind=kLoop, calls=%fused_computation.12 | loop fusion | flops 131072 | bytes 786432 | tf_op jit(solution)/shard_map/convert_element_type | solution.py:574
  1.8 2.4 %collective-permute-start.1 = (bf16[256,128]{1,0:T(8,128)(2,1)S(1)}, bf16[256,128]{1,0:T(8,128)(2,1)S(1)}, u32[]{:S(2)}, u32[]{:S(2)}) collective-permute-start(bf16[256,128]{1,0:T(8,128)(2,1)S(1)} %bitcast.29), channel_id=1, source_target_pairs={{0,16},{4,20},{8,24},{12,28},{16,0},{20,4},{24,8},{28,12},{1,17},{... | collective-permute-start | bytes 196616 | tf_op jit(solution)/shard_map/ppermute | solution.py:52
  4.1 1.0 %collective-permute-start = (bf16[2,256,128]{2,1,0:T(8,128)(2,1)S(1)}, bf16[2,256,128]{2,1,0:T(8,128)(2,1)S(1)}, u32[]{:S(2)}, u32[]{:S(2)}) collective-permute-start(bf16[2,256,128]{2,1,0:T(8,128)(2,1)S(1)} %slice.12), channel_id=1, source_target_pairs={{0,12},{4,0},{8,4},{12,8},{16,28},{20,16},{24,20},{28,24},{1,13},{... | collective-permute-start | bytes 393224 | tf_op jit(solution)/shard_map/ppermute | solution.py:52
  6.1 0.1 collective-permute-start.2
  6.5 0.2 collective-permute-done.1.below.below0.rest_2_.rest_8_
  6.7 2.0 %collective-permute-start.3 = (bf16[256,128]{1,0:T(8,128)(2,1)S(1)}, bf16[256,128]{1,0:T(8,128)(2,1)S(1)}, u32[]{:S(2)}, u32[]{:S(2)}) collective-permute-start(bf16[256,128]{1,0:T(8,128)(2,1)S(1)} %collective-permute-done.1.below.below0.rest_2_.rest_8_), channel_id=1, source_target_pairs={{0,12},{4,0},{8,4},{12,8},{16,28},{20,16},{24,20},{28,24},{1,13},{... | collective-permute-start | bytes 196616 | tf_op jit(solution)/shard_map/ppermute | solution.py:52
  8.8 2.1 %stage.1 = (f32[2,3,384,128]{3,2,1,0:T(8,128)S(1)}, f32[2,3,384,128]{3,2,1,0:T(8,128)S(1)}, f32[2,256,256]{2,1,0:T(8,128)S(1)}, bf16[4,256,256]{2,1,0:T(8,128)(2,1)S(1)}) custom-call(bf16[256,128]{1,0:T(8,128)(2,1)S(1)} %collective-permute-done.1.below.below0.rest_2_.rest_8_, f32[2,256,256]{2,1,0:T(8,128)} %bitcast.22, f32[2,256,256]{2,1,0:T(8,128)} %bitcast.24, ...), custom_call_target="tpu_custom_call" | custom-call | flops 983040 | bytes 2228224 | tf_op jit(solution)/shard_map/stage/pallas_call | solution.py:525
  11.0 0.8 %copy-done = bf16[4,256,256]{2,1,0:T(8,128)(2,1)} copy-done((bf16[4,256,256]{2,1,0:T(8,128)(2,1)}, bf16[4,256,256]{2,1,0:T(8,128)(2,1)S(1)}, u32[]{:S(2)}) %copy-start) | copy-done | bytes 524312
  11.9 3.9 %first_pass.1 = (f32[2,3,384,128]{3,2,1,0:T(8,128)S(1)}, f32[2,3,384,128]{3,2,1,0:T(8,128)S(1)}, f32[3,256,256]{2,1,0:T(8,128)S(1)}, bf16[800,128]{1,0:T(8,128)(...) custom-call(s32[9]{0:T(128)S(1)} %pad_add_fusion.meta, ...), custom_call_target="tpu_custom_call", output_to_operand_aliasing={{0}: (6, {}), {1}: (7, {})} | custom-call | flops 1073741824 | bytes 786432 | tf_op jit(solution)/shard_map/first_pass/pallas_call | solution.py:525
  15.8 0.7 %collective-permute-start.5 = (bf16[800,128]{1,0:T(8,128)(2,1)S(1)}, bf16[800,128]{1,0:T(8,128)(2,1)S(1)}, u32[]{:S(2)}, u32[]{:S(2)}) collective-permute-start(bf16[800,128]{1,0:T(8,128)(2,1)S(1)} %get-tuple-element.39), channel_id=1, source_target_pairs={{0,0},{4,8},{8,4},{12,12},{16,16},{20,24},{24,20},{28,28},{1,1},{5... | collective-permute-start | bytes 614408 | tf_op jit(solution)/shard_map/ppermute | solution.py:66
  16.5 5.4 %collective-permute-start.6 = (bf16[2,128,128]{2,1,0:T(8,128)(2,1)S(1)}, bf16[2,128,128]{2,1,0:T(8,128)(2,1)S(1)}, u32[]{:S(2)}, u32[]{:S(2)}) collective-permute-start(bf16[2,128,128]{2,1,0:T(8,128)(2,1)S(1)} %get-tuple-element.40), channel_id=1, source_target_pairs={{0,16},{4,20},{8,24},{12,28},{16,0},{20,4},{24,8},{28,12},{1,17},{... | collective-permute-start | bytes 196616 | tf_op jit(solution)/shard_map/ppermute | solution.py:52
  21.9 1.7 %collective-permute-done.6.rest_5_.rest_6_.rest_10_.rest_11_.mid_above.mid_below = bf16[2,128,128]{2,1,0:T(8,128)(2,1)S(1)} collective-permute-done((bf16[2,128,128]{2,1,0:T(8,128)(2,1)S(1)}, bf16[2,128,128]{2,1,0:T(8,128)(2,1)S(1)}, u32[]{:S(2)}, u32[]{:S(2)}) %collective-permute-start.6) | collective-permute-done | bytes 65568 | tf_op jit(solution)/shard_map/ppermute | solution.py:52
  23.7 2.9 %collective-permute-start.7 = (bf16[2,2,128,128]{3,2,1,0:T(8,128)(2,1)S(1)}, bf16[2,2,128,128]{3,2,1,0:T(8,128)(2,1)S(1)}, u32[]{:S(2)}, u32[]{:S(2)}) collective-permute-start(bf16[2,2,128,128]{3,2,1,0:T(8,128)(2,1)S(1)} %between.1.rest_4_), channel_id=1, source_target_pairs={{0,16},{4,20},{8,24},{12,28},{16,0},{20,4},{24,8},{28,12},{1,17},{... | collective-permute-start | bytes 393224 | tf_op jit(solution)/shard_map/ppermute | solution.py:52
  26.6 2.4 %weigh.1 = (f32[3,384,128]{2,1,0:T(8,128)S(1)}, f32[2,256,256]{2,1,0:T(8,128)S(1)}, f32[2,256,256]{2,1,0:T(8,128)S(1)}, f32[2,256,256]{2,1,0:T(8,128)S(1)}, bf16...) custom-call(bf16[16,128]{1,0:T(8,128)(2,1)S(1)} %fusion.5.rest_0_, ...), custom_call_target="tpu_custom_call" | custom-call | flops 933888 | bytes 2359296 | tf_op jit(solution)/shard_map/weigh/pallas_call | solution.py:525
  29.0 3.6 %second_pass.1 = (f32[2,256,256]{2,1,0:T(8,128)S(1)}, f32[2,256,128]{2,1,0:T(8,128)S(1)}, bf16[2,384,128]{2,1,0:T(8,128)(2,1)S(1)}, f32[2,128,128]{2,1,0:T(8,128...) custom-call(s32[9]{0:T(128)S(1)} %pad_add_fusion.meta, ...), custom_call_target="tpu_custom_call" | custom-call | flops 1073741824 | tf_op jit(solution)/shard_map/second_pass/pallas_call | solution.py:525
  32.5 5.4 %collective-permute-start.11 = (bf16[3,128,256]{2,1,0:T(8,128)(2,1)S(1)}, bf16[3,128,256]{2,1,0:T(8,128)(2,1)S(1)}, u32[]{:S(2)}, u32[]{:S(2)}) collective-permute-start(bf16[3,128,256]{2,1,0:T(8,128)(2,1)S(1)} %get-tuple-element.55), channel_id=1, source_target_pairs={{0,4},{4,0},{8,12},{12,8},{16,20},{20,16},{24,28},{28,24},{1,5},{5... | collective-permute-start | bytes 589832 | tf_op jit(solution)/shard_map/ppermute | solution.py:57
  38.0 1.0 %collective-permute-done.11.came = bf16[3,128,256]{2,1,0:T(8,128)(2,1)S(1)} collective-permute-done((bf16[3,128,256]{2,1,0:T(8,128)(2,1)S(1)}, bf16[3,128,256]{2,1,0:T(8,128)(2,1)S(1)}, u32[]{:S(2)}, u32[]{:S(2)}) %collective-permute-start.11) | collective-permute-done | bytes 196640 | tf_op jit(solution)/shard_map/ppermute | solution.py:57
  39.1 0.4 collective-permute-start.16
  39.5 2.0 %collective-permute-start.10 = (bf16[2,128,128]{2,1,0:T(8,128)(2,1)S(1)}, bf16[2,128,128]{2,1,0:T(8,128)(2,1)S(1)}, u32[]{:S(2)}, u32[]{:S(2)}) collective-permute-start(bf16[2,128,128]{2,1,0:T(8,128)(2,1)S(1)} %get-tuple-element.53), channel_id=1, source_target_pairs={{0,16},{4,20},{8,24},{12,28},{16,0},{20,4},{24,8},{28,12},{1,17},{... | collective-permute-start | bytes 196616 | tf_op jit(solution)/shard_map/ppermute | solution.py:52
  41.6 1.2 %collective-permute-start.9 = (bf16[2,128,128]{2,1,0:T(8,128)(2,1)S(1)}, bf16[2,128,128]{2,1,0:T(8,128)(2,1)S(1)}, u32[]{:S(2)}, u32[]{:S(2)}) collective-permute-start(bf16[2,128,128]{2,1,0:T(8,128)(2,1)S(1)} %add_rim.1), channel_id=1, source_target_pairs={{0,16},{4,20},{8,24},{12,28},{16,0},{20,4},{24,8},{28,12},{1,17},{... | collective-permute-start | bytes 196616 | tf_op jit(solution)/shard_map/ppermute | solution.py:52
  42.8 6.2 %collective-permute-done.10.above1 = bf16[2,128,128]{2,1,0:T(8,128)(2,1)S(1)} collective-permute-done((bf16[2,128,128]{2,1,0:T(8,128)(2,1)S(1)}, bf16[2,128,128]{2,1,0:T(8,128)(2,1)S(1)}, u32[]{:S(2)}, u32[]{:S(2)}) %collective-permute-start.10) | collective-permute-done | bytes 65568 | tf_op jit(solution)/shard_map/ppermute | solution.py:52
  49.0 1.4 %collective-permute-done.9.above0 = bf16[2,128,128]{2,1,0:T(8,128)(2,1)S(1)} collective-permute-done((bf16[2,128,128]{2,1,0:T(8,128)(2,1)S(1)}, bf16[2,128,128]{2,1,0:T(8,128)(2,1)S(1)}, u32[]{:S(2)}, u32[]{:S(2)}) %collective-permute-start.9) | collective-permute-done | bytes 65568 | tf_op jit(solution)/shard_map/ppermute | solution.py:52
  50.5 3.2 %collective-permute-start.13 = (bf16[2,128,256]{2,1,0:T(8,128)(2,1)S(1)}, bf16[2,128,256]{2,1,0:T(8,128)(2,1)S(1)}, u32[]{:S(2)}, u32[]{:S(2)}) collective-permute-start(bf16[2,128,256]{2,1,0:T(8,128)(2,1)S(1)} %get-tuple-element.57.refs_2_), channel_id=1, source_target_pairs={{0,2},{1,3},{2,0},{3,1},{4,6},{5,7},{6,4},{7,5},{8,10},{9,11},{10,... | collective-permute-start | bytes 393224 | tf_op jit(solution)/shard_map/ppermute | solution.py:57
  53.8 3.4 %collective-permute-done.13.refs_3_ = bf16[2,128,256]{2,1,0:T(8,128)(2,1)S(1)} collective-permute-done((bf16[2,128,256]{2,1,0:T(8,128)(2,1)S(1)}, bf16[2,128,256]{2,1,0:T(8,128)(2,1)S(1)}, u32[]{:S(2)}, u32[]{:S(2)}) %collective-permute-start.13) | collective-permute-done | bytes 131104 | tf_op jit(solution)/shard_map/ppermute | solution.py:57
  57.2 0.8 %collective-permute-done.12.refs_1_ = bf16[2,128,256]{2,1,0:T(8,128)(2,1)S(1)} collective-permute-done((bf16[2,128,256]{2,1,0:T(8,128)(2,1)S(1)}, bf16[2,128,256]{2,1,0:T(8,128)(2,1)S(1)}, u32[]{:S(2)}, u32[]{:S(2)}) %collective-permute-start.12) | collective-permute-done | bytes 131104 | tf_op jit(solution)/shard_map/ppermute | solution.py:57
  58.1 0.5 collective-permute-start.14
  58.6 0.3 collective-permute-start.15
  58.9 3.4 %collective-permute-done.14.first_came.rest_0_ = bf16[2,128,256]{2,1,0:T(8,128)(2,1)S(1)} collective-permute-done((bf16[2,128,256]{2,1,0:T(8,128)(2,1)S(1)}, bf16[2,128,256]{2,1,0:T(8,128)(2,1)S(1)}, u32[]{:S(2)}, u32[]{:S(2)}) %collective-permute-start.14) | collective-permute-done | bytes 131104 | tf_op jit(solution)/shard_map/ppermute | solution.py:57
  62.3 1.2 %collective-permute-done.17.came = bf16[3,128,256]{2,1,0:T(8,128)(2,1)S(1)} collective-permute-done((bf16[3,128,256]{2,1,0:T(8,128)(2,1)S(1)}, bf16[3,128,256]{2,1,0:T(8,128)(2,1)S(1)}, u32[]{:S(2)}, u32[]{:S(2)}) %collective-permute-start.17) | collective-permute-done | bytes 196640 | tf_op jit(solution)/shard_map/ppermute | solution.py:57
  63.6 1.2 %collective-permute-start.18 = (bf16[2,128,256]{2,1,0:T(8,128)(2,1)S(1)}, bf16[2,128,256]{2,1,0:T(8,128)(2,1)S(1)}, u32[]{:S(2)}, u32[]{:S(2)}) collective-permute-start(bf16[2,128,256]{2,1,0:T(8,128)(2,1)S(1)} %update.1), channel_id=1, source_target_pairs={{0,4},{4,0},{8,12},{12,8},{16,20},{20,16},{24,28},{28,24},{1,5},{5... | collective-permute-start | bytes 393224 | tf_op jit(solution)/shard_map/ppermute | solution.py:57
  64.8 1.2 %settle.1 = (f32[2,256,256]{2,1,0:T(8,128)}, f32[2,256,256]{2,1,0:T(8,128)}) custom-call(bf16[2,128,256]{2,1,0:T(8,128)(2,1)S(1)} %get-tuple-element.58.first, bf16[2,128,256]{2,1,0:T(8,128)(2,1)S(1)} %collective-permute-done.14.first_came.rest_0_, bf16[2,128,256]{2,1,0:T(8,128)(2,1)S(1)} %get-tuple-element.59.second, ...), custom_call_target="tpu_custom_call" | custom-call | flops 262144 | tf_op jit(solution)/shard_map/settle/pallas_call | solution.py:525
  66.0 0.9 %convert_add_fusion = f32[1,2,256,256]{3,2,1,0:T(8,128)} fusion(f32[1,2,256,256]{3,2,1,0:T(8,128)S(1)} %copy-done.1, bf16[1,2,128,256]{3,2,1,0:T(8,128)(2,1)S(1)} %bitcast.19, bf16[1,2,128,256]{3,2,1,0:T(8,128)(2,1)S(1)} %bitcast.28, pred[]{:T(512)} %eq.8), kind=kLoop, calls=%fused_computation | loop fusion | flops 1441792 | bytes 1310721 | tf_op jit(solution)/shard_map/add | solution.py:659
  (39 shorter events, 1.5 us)
Async XLA Ops:
  0.6 5.2 %copy-start.2 = (s32[1,1,4,2]{2,3,1,0:T(2,128)S(1)}, s32[1,1,4,2]{2,3,1,0:T(2,128)}, u32[]{:S(2)}) copy-start(s32[1,1,4,2]{2,3,1,0:T(2,128)} %param.13) | copy-start | bytes 100
  1.8 5.0 %collective-permute-start.1 = (bf16[256,128]{1,0:T(8,128)(2,1)S(1)}, bf16[256,128]{1,0:T(8,128)(2,1)S(1)}, u32[]{:S(2)}, u32[]{:S(2)}) collective-permute-start(bf16[256,128]{1,0:T(8,128)(2,1)S(1)} %bitcast.29), channel_id=1, source_target_pairs={{0,16},{4,20},{8,24},{12,28},{16,0},{20,4},{24,8},{28,12},{1,17},{... | collective-permute-start | bytes 196616 | tf_op jit(solution)/shard_map/ppermute | solution.py:52
  4.1 7.6 %collective-permute-start = (bf16[2,256,128]{2,1,0:T(8,128)(2,1)S(1)}, bf16[2,256,128]{2,1,0:T(8,128)(2,1)S(1)}, u32[]{:S(2)}, u32[]{:S(2)}) collective-permute-start(bf16[2,256,128]{2,1,0:T(8,128)(2,1)S(1)} %slice.12), channel_id=1, source_target_pairs={{0,12},{4,0},{8,4},{12,8},{16,28},{20,16},{24,20},{28,24},{1,13},{... | collective-permute-start | bytes 393224 | tf_op jit(solution)/shard_map/ppermute | solution.py:52
  6.1 5.7 %collective-permute-start.2 = (bf16[272,128]{1,0:T(8,128)(2,1)S(1)}, bf16[272,128]{1,0:T(8,128)(2,1)S(1)}, u32[]{:S(2)}, u32[]{:S(2)}) collective-permute-start(bf16[272,128]{1,0:T(8,128)(2,1)S(1)} %pad_maximum_fusion), channel_id=1, source_target_pairs={{0,16},{4,20},{8,24},{12,28},{16,0},{20,4},{24,8},{28,12},{1,17},{... | collective-permute-start | bytes 208904 | tf_op jit(solution)/shard_map/ppermute | solution.py:52
  6.7 5.0 %collective-permute-start.3 = (bf16[256,128]{1,0:T(8,128)(2,1)S(1)}, bf16[256,128]{1,0:T(8,128)(2,1)S(1)}, u32[]{:S(2)}, u32[]{:S(2)}) collective-permute-start(bf16[256,128]{1,0:T(8,128)(2,1)S(1)} %collective-permute-done.1.below.below0.rest_2_.rest_8_), channel_id=1, source_target_pairs={{0,12},{4,0},{8,4},{12,8},{16,28},{20,16},{24,20},{28,24},{1,13},{... | collective-permute-start | bytes 196616 | tf_op jit(solution)/shard_map/ppermute | solution.py:52
  11.0 0.8 %copy-start = (bf16[4,256,256]{2,1,0:T(8,128)(2,1)}, bf16[4,256,256]{2,1,0:T(8,128)(2,1)S(1)}, u32[]{:S(2)}) copy-start(bf16[4,256,256]{2,1,0:T(8,128)(2,1)S(1)} %get-tuple-element.36.rest_3_.rest_16_) | copy-start | bytes 1572868
  15.7 7.9 %collective-permute-start.4 = (bf16[800,128]{1,0:T(8,128)(2,1)S(1)}, bf16[800,128]{1,0:T(8,128)(2,1)S(1)}, u32[]{:S(2)}, u32[]{:S(2)}) collective-permute-start(bf16[800,128]{1,0:T(8,128)(2,1)S(1)} %get-tuple-element.38), channel_id=1, source_target_pairs={{0,4},{4,0},{8,12},{12,8},{16,20},{20,16},{24,28},{28,24},{1,5},{5... | collective-permute-start | bytes 614408 | tf_op jit(solution)/shard_map/ppermute | solution.py:57
  15.8 7.8 %collective-permute-start.5 = (bf16[800,128]{1,0:T(8,128)(2,1)S(1)}, bf16[800,128]{1,0:T(8,128)(2,1)S(1)}, u32[]{:S(2)}, u32[]{:S(2)}) collective-permute-start(bf16[800,128]{1,0:T(8,128)(2,1)S(1)} %get-tuple-element.39), channel_id=1, source_target_pairs={{0,0},{4,8},{8,4},{12,12},{16,16},{20,24},{24,20},{28,28},{1,1},{5... | collective-permute-start | bytes 614408 | tf_op jit(solution)/shard_map/ppermute | solution.py:66
  16.5 7.1 %collective-permute-start.6 = (bf16[2,128,128]{2,1,0:T(8,128)(2,1)S(1)}, bf16[2,128,128]{2,1,0:T(8,128)(2,1)S(1)}, u32[]{:S(2)}, u32[]{:S(2)}) collective-permute-start(bf16[2,128,128]{2,1,0:T(8,128)(2,1)S(1)} %get-tuple-element.40), channel_id=1, source_target_pairs={{0,16},{4,20},{8,24},{12,28},{16,0},{20,4},{24,8},{28,12},{1,17},{... | collective-permute-start | bytes 196616 | tf_op jit(solution)/shard_map/ppermute | solution.py:52
  23.7 5.3 %collective-permute-start.7 = (bf16[2,2,128,128]{3,2,1,0:T(8,128)(2,1)S(1)}, bf16[2,2,128,128]{3,2,1,0:T(8,128)(2,1)S(1)}, u32[]{:S(2)}, u32[]{:S(2)}) collective-permute-start(bf16[2,2,128,128]{3,2,1,0:T(8,128)(2,1)S(1)} %between.1.rest_4_), channel_id=1, source_target_pairs={{0,16},{4,20},{8,24},{12,28},{16,0},{20,4},{24,8},{28,12},{1,17},{... | collective-permute-start | bytes 393224 | tf_op jit(solution)/shard_map/ppermute | solution.py:52
  32.5 6.4 %collective-permute-start.11 = (bf16[3,128,256]{2,1,0:T(8,128)(2,1)S(1)}, bf16[3,128,256]{2,1,0:T(8,128)(2,1)S(1)}, u32[]{:S(2)}, u32[]{:S(2)}) collective-permute-start(bf16[3,128,256]{2,1,0:T(8,128)(2,1)S(1)} %get-tuple-element.55), channel_id=1, source_target_pairs={{0,4},{4,0},{8,12},{12,8},{16,20},{20,16},{24,28},{28,24},{1,5},{5... | collective-permute-start | bytes 589832 | tf_op jit(solution)/shard_map/ppermute | solution.py:57
  37.9 3.6 %collective-permute-start.8 = (bf16[2,384,128]{2,1,0:T(8,128)(2,1)S(1)}, bf16[2,384,128]{2,1,0:T(8,128)(2,1)S(1)}, u32[]{:S(2)}, u32[]{:S(2)}) collective-permute-start(bf16[2,384,128]{2,1,0:T(8,128)(2,1)S(1)} %get-tuple-element.51), channel_id=1, source_target_pairs={{0,4},{4,8},{8,12},{12,0},{16,20},{20,24},{24,28},{28,16},{1,5},{5... | collective-permute-start | bytes 589832 | tf_op jit(solution)/shard_map/ppermute | solution.py:52
  39.1 14.6 %collective-permute-start.16 = (bf16[3,128,256]{2,1,0:T(8,128)(2,1)S(1)}, bf16[3,128,256]{2,1,0:T(8,128)(2,1)S(1)}, u32[]{:S(2)}, u32[]{:S(2)}) collective-permute-start(bf16[3,128,256]{2,1,0:T(8,128)(2,1)S(1)} %halve.1.rest_0_.held), channel_id=1, source_target_pairs={{0,8},{4,12},{8,0},{12,4},{16,24},{20,28},{24,16},{28,20},{1,9},{5... | collective-permute-start | bytes 589832 | tf_op jit(solution)/shard_map/ppermute | solution.py:57
  39.5 9.5 %collective-permute-start.10 = (bf16[2,128,128]{2,1,0:T(8,128)(2,1)S(1)}, bf16[2,128,128]{2,1,0:T(8,128)(2,1)S(1)}, u32[]{:S(2)}, u32[]{:S(2)}) collective-permute-start(bf16[2,128,128]{2,1,0:T(8,128)(2,1)S(1)} %get-tuple-element.53), channel_id=1, source_target_pairs={{0,16},{4,20},{8,24},{12,28},{16,0},{20,4},{24,8},{28,12},{1,17},{... | collective-permute-start | bytes 196616 | tf_op jit(solution)/shard_map/ppermute | solution.py:52
  41.6 8.8 %collective-permute-start.9 = (bf16[2,128,128]{2,1,0:T(8,128)(2,1)S(1)}, bf16[2,128,128]{2,1,0:T(8,128)(2,1)S(1)}, u32[]{:S(2)}, u32[]{:S(2)}) collective-permute-start(bf16[2,128,128]{2,1,0:T(8,128)(2,1)S(1)} %add_rim.1), channel_id=1, source_target_pairs={{0,16},{4,20},{8,24},{12,28},{16,0},{20,4},{24,8},{28,12},{1,17},{... | collective-permute-start | bytes 196616 | tf_op jit(solution)/shard_map/ppermute | solution.py:52
  50.5 6.8 %collective-permute-start.13 = (bf16[2,128,256]{2,1,0:T(8,128)(2,1)S(1)}, bf16[2,128,256]{2,1,0:T(8,128)(2,1)S(1)}, u32[]{:S(2)}, u32[]{:S(2)}) collective-permute-start(bf16[2,128,256]{2,1,0:T(8,128)(2,1)S(1)} %get-tuple-element.57.refs_2_), channel_id=1, source_target_pairs={{0,2},{1,3},{2,0},{3,1},{4,6},{5,7},{6,4},{7,5},{8,10},{9,11},{10,... | collective-permute-start | bytes 393224 | tf_op jit(solution)/shard_map/ppermute | solution.py:57
  53.7 4.4 %collective-permute-start.12 = (bf16[2,128,256]{2,1,0:T(8,128)(2,1)S(1)}, bf16[2,128,256]{2,1,0:T(8,128)(2,1)S(1)}, u32[]{:S(2)}, u32[]{:S(2)}) collective-permute-start(bf16[2,128,256]{2,1,0:T(8,128)(2,1)S(1)} %get-tuple-element.56.refs_0_.rest_0_), channel_id=1, source_target_pairs={{0,1},{1,0},{2,3},{3,2},{4,5},{5,4},{6,7},{7,6},{8,9},{9,8},{10,11... | collective-permute-start | bytes 393224 | tf_op jit(solution)/shard_map/ppermute | solution.py:57
  53.7 12.3 %copy-start.1 = (f32[1,2,256,256]{3,2,1,0:T(8,128)S(1)}, f32[1,2,256,256]{3,2,1,0:T(8,128)}, u32[]{:S(2)}) copy-start(f32[1,2,256,256]{3,2,1,0:T(8,128)} %param.11) | copy-start | bytes 1572868
  53.8 9.8 %collective-permute-start.17 = (bf16[3,128,256]{2,1,0:T(8,128)(2,1)S(1)}, bf16[3,128,256]{2,1,0:T(8,128)(2,1)S(1)}, u32[]{:S(2)}, u32[]{:S(2)}) collective-permute-start(bf16[3,128,256]{2,1,0:T(8,128)(2,1)S(1)} %add.23.held), channel_id=1, source_target_pairs={{0,24},{4,28},{8,16},{12,20},{16,8},{20,12},{24,0},{28,4},{1,25},{... | collective-permute-start | bytes 589832 | tf_op jit(solution)/shard_map/ppermute | solution.py:57
  58.1 4.2 %collective-permute-start.14 = (bf16[2,128,256]{2,1,0:T(8,128)(2,1)S(1)}, bf16[2,128,256]{2,1,0:T(8,128)(2,1)S(1)}, u32[]{:S(2)}, u32[]{:S(2)}) collective-permute-start(bf16[2,128,256]{2,1,0:T(8,128)(2,1)S(1)} %get-tuple-element.58.first), channel_id=1, source_target_pairs={{0,2},{1,3},{2,0},{3,1},{4,6},{5,7},{6,4},{7,5},{8,10},{9,11},{10,... | collective-permute-start | bytes 393224 | tf_op jit(solution)/shard_map/ppermute | solution.py:57
  58.6 6.3 %collective-permute-start.15 = (bf16[2,128,256]{2,1,0:T(8,128)(2,1)S(1)}, bf16[2,128,256]{2,1,0:T(8,128)(2,1)S(1)}, u32[]{:S(2)}, u32[]{:S(2)}) collective-permute-start(bf16[2,128,256]{2,1,0:T(8,128)(2,1)S(1)} %get-tuple-element.59.second), channel_id=1, source_target_pairs={{0,1},{1,0},{2,3},{3,2},{4,5},{5,4},{6,7},{7,6},{8,9},{9,8},{10,11... | collective-permute-start | bytes 393224 | tf_op jit(solution)/shard_map/ppermute | solution.py:57
  63.6 2.4 %collective-permute-start.18 = (bf16[2,128,256]{2,1,0:T(8,128)(2,1)S(1)}, bf16[2,128,256]{2,1,0:T(8,128)(2,1)S(1)}, u32[]{:S(2)}, u32[]{:S(2)}) collective-permute-start(bf16[2,128,256]{2,1,0:T(8,128)(2,1)S(1)} %update.1), channel_id=1, source_target_pairs={{0,4},{4,0},{8,12},{12,8},{16,20},{20,16},{24,28},{28,24},{1,5},{5... | collective-permute-start | bytes 393224 | tf_op jit(solution)/shard_map/ppermute | solution.py:57

commit v6 on v5

--- a/solution.py
+++ b/solution.py
@@ -218,12 +218,8 @@
     return copies
 
 
-def stage(
-    below, own_h, dual_h, probe_h, amps_h, order_h, ext, acc, probe, ordered, sems, own, dual, amps, order
-):
-    copies = fetch(
-        [(own_h, own), (dual_h, dual), (probe_h, probe), (amps_h, amps), (order_h, order)], sems
-    )
+def stage(own_h, dual_h, probe_h, ext, acc, probe, sems, own, dual):
+    copies = fetch([(own_h, own), (dual_h, dual), (probe_h, probe)], sems)
     acc[:, 2] = jnp.zeros((2, SPAN, L), f32)
     copies[0].wait()
     for j in range(2):
@@ -234,18 +230,26 @@
     for j in range(2):
         cols = slice(j * L, (j + 1) * L)
         acc[:, j, :TS, :] = -penalty * dual[:, :, cols]
-    for copy in copies[2:]:
+    copies[2].wait()
+
+
+def reorder(below, amps_h, order_h, ordered_h, sems, amps, order, ordered):
+    copies = fetch([(order_h, order), (amps_h, amps)], sems)
+    for copy in copies:
         copy.wait()
     for k in range(SLOTS):
         rows = jnp.dot(order[...], amps[k], preferred_element_type=f32).astype(bf16)
         ordered[k] = jnp.dot(rows, order[...], preferred_element_type=f32).astype(bf16)
+    back = pltpu.make_async_copy(ordered, ordered_h, sems.at[2])
+    back.start()
+    back.wait()
 
 
 def first_pass(
     two, meta, flags, right, below0, below1, diag, ext0, acc0, probe, *rest,
 ):
     *cards, fwd_h, bwd_h, amps_h = rest[: 4 if two else 5]
-    ext, acc, pnum, side, inner, *mids, fwd, bwd, amps, sems, win, X, Y, W = rest[4 if two else 5 :]
+    ext, acc, pnum, side, *inner, fwd, bwd, amps, sems, win, X, Y, W = rest[4 if two else 5 :]
     copies = fetch([(fwd_h, fwd), (bwd_h, bwd), (amps_h, amps)], sems)
     has_right = flags[HAS_RIGHT : HAS_RIGHT + 1, :]
     has_below = flags[HAS_BELOW : HAS_BELOW + 1, :]
@@ -266,16 +270,36 @@
     odd = flags[ODD : ODD + 1, :] > 0.0
     column = [card[...] for card in cards] + [below1[2 * OVER :, :]]
     side[2 * SPAN :, :] = jnp.concatenate(column, 0)
-    inner[2 * SPAN :, :] = jnp.concatenate(column, 0)
+    inner[0][2 * (OVER if two else SPAN) :, :] = jnp.concatenate(column, 0)
     for ch in range(2):
         side[plane(ch, SPAN), :] = jnp.where(odd, acc[ch, 0], acc[ch, 2]).astype(bf16)
-        inner[plane(ch, SPAN), :] = jnp.where(odd, acc[ch, 2], acc[ch, 0]).astype(bf16)
-        for rim, mid in zip(rims_of(two, flags, lambda rows: acc[ch, 1, rows, :]), mids):
-            mid[ch] = rim.astype(bf16)
+        other = [jnp.where(odd, acc[ch, 2, rows, :], acc[ch, 0, rows, :]) for rows in BANDS]
+        for part, values in zip(inner, parted(two, flags, other)):
+            rows = values.shape[0]
+            part[plane(ch, rows), :] = values.astype(bf16)
 
 
 def plane(ch, rows, start=0, count=None):
     return slice(ch * rows + start, ch * rows + start + (rows if count is None else count))
+
+
+def parted(two, flags, bands):
+    if not two:
+        return [jnp.concatenate(bands, 0)]
+    lower = flags[HAS_BELOW : HAS_BELOW + 1, :] > 0.0
+    rest = [jnp.where(lower, bands[k], bands[k + 1]) for k in range(2)]
+    return [jnp.where(lower, bands[2], bands[0]), jnp.concatenate(rest, 0)]
+
+
+def from_inner(two, flags, inner, ch, start, count):
+    if not two:
+        return inner[0][plane(ch, SPAN, start, count), :]
+    band, at = divmod(start, OVER)
+    lower = flags[HAS_BELOW : HAS_BELOW + 1, :] > 0.0
+    rim = inner[0][plane(ch, OVER, at, count), :]
+    first, second = [inner[1][plane(ch, TS, k * OVER + at, count), :] for k in range(2)]
+    on_top = (first, second, rim)[band].astype(f32)
+    return jnp.where(lower, on_top, (rim, first, second)[band].astype(f32))
 
 
 def rims_of(two, flags, get):
@@ -291,17 +315,21 @@
 
 
 def between(two, flags, acc, side, inner, *rest):
-    outs = rest[-1:] if two else rest[-2:]
+    outs = rest[-3:] if two else rest[-6:]
     for ch in range(2):
-        for at in range(2):
-
-            def total(rows):
-                where = plane(ch, SPAN, rows.start, OVER)
-                came = from_sides(flags, side[where, :], inner[where, :])[at]
-                return acc[ch, 2 * at, rows, :] + came
-
-            for rim, out in zip(rims_of(two, flags, total), outs):
-                out[ch, at] = rim.astype(bf16)
+        for j in range(3):
+            rims = rims_of(two, flags, lambda rows: acc[ch, j, rows, :])
+            if j != 1:
+                sides = rims_of(
+                    two, flags, lambda rows: side[plane(ch, SPAN, rows.start, OVER), :].astype(f32)
+                )
+                size = OVER if two else SPAN
+                starts = [0] if two else [TS, 0]
+                for k, start in enumerate(starts):
+                    other = inner[plane(ch, size, start, OVER), :]
+                    rims[k] = rims[k] + from_sides(flags, sides[k], other)[j // 2]
+            for k, rim in enumerate(rims):
+                outs[3 * k + j][ch] = rim.astype(bf16)
 
 
 def weigh(two, *rest):
@@ -314,9 +342,11 @@
     blocks = [card[...].astype(f32) for card in cards] + [below1[last:, :].astype(f32)]
     for k, block in enumerate(blocks):
         held[k : k + 1, :] = block[:1]
-        at = 2 * SPAN + k * CARD
+        ends = [2 * SPAN + k * CARD, 2 * (OVER if two else SPAN) + k * CARD]
         odd = flags[ODD : ODD + 1, :] > 0.0
-        by_side, by_inner = [v[at : at + CARD, :].astype(f32)[:1] for v in (side, inner)]
+        by_side, by_inner = [
+            v[at : at + CARD, :].astype(f32)[:1] for v, at in zip((side, inner), ends)
+        ]
         held[4 + k : 5 + k, :] = jnp.where(odd, by_side, by_inner)
         held[8 + k : 9 + k, :] = jnp.where(odd, by_inner, by_side)
     held[16:24, :] = flags[...]
@@ -362,11 +392,13 @@
 
 
 def second_pass(
-    meta, flags, right, below0, below1, diag, acc1, side, inner, mid_above, mid_below, from_above, from_below,
-    weight, pnum1, own, dual, probe, amps, fwd, bwd,
-    base, shrink, to_right, lower, to_below, pnum, to_swap,
-    partial, ext, acc, win, X, Y, W,
+    two, meta, flags, right, below0, below1, diag, acc1, side, *rest,
 ):
+    inner, rest = rest[: 2 if two else 1], rest[2 if two else 1 :]
+    from_above, from_below, rest = rest[:3], rest[3:6], rest[6:]
+    weight, pnum1, own, dual, probe, amps, fwd, bwd = rest[:8]
+    base, shrink, to_right, to_corner, lower, to_below, pnum, to_swap = rest[8:16]
+    partial, ext, acc, win, X, Y, W = rest[16:]
     has_right = flags[HAS_RIGHT : HAS_RIGHT + 1, :]
     has_below = flags[HAS_BELOW : HAS_BELOW + 1, :]
     has_above = flags[HAS_ABOVE : HAS_ABOVE + 1, :]
@@ -380,13 +412,15 @@
                 total = acc1[ch, j, rows, :]
                 if j != 1:
                     at = plane(ch, SPAN, k, 64)
-                    total = total + from_sides(flags, side[at, :], inner[at, :])[j // 2]
+                    total = total + from_sides(
+                        flags, side[at, :], from_inner(two, flags, inner, ch, k, 64)
+                    )[j // 2]
                 if k < OVER:
-                    came = mid_above[ch, rows, :] if j == 1 else from_above[ch, j // 2, rows, :]
+                    came = from_above[j][ch, rows, :]
                     total = total + came.astype(f32) * has_above
                 if k >= TS:
                     rim = slice(k - TS, k - TS + 64)
-                    came = mid_below[ch, rim, :] if j == 1 else from_below[ch, j // 2, rim, :]
+                    came = from_below[j][ch, rim, :]
                     total = total + came.astype(f32)
                 step = total / (weight[j, rows, :] + penalty)
                 if j < 2 and k < TS:
@@ -409,7 +443,8 @@
     def _(p):
         visit_pair(p, meta, ext, probe, amps, fwd, bwd, acc, pnum, win, X, Y, W)
 
-    to_right[...] = acc[:, 2].astype(bf16)
+    to_corner[...] = acc[:, 2, TS:, :].astype(bf16)
+    to_right[...] = acc[:, 2, :TS, :].astype(bf16)
     to_below[...] = acc[:, 1, TS:, :].astype(bf16)
     lower[...] = acc[:, 0, TS:, :]
     odd = flags[ODD : ODD + 1, :1] > 0.0
@@ -444,7 +479,7 @@
 def add_rim(flags, rim, from_left, *rest):
     has_left = flags[HAS_LEFT : HAS_LEFT + 1, :]
     for ch in range(2):
-        rest[-1][ch] = (rim[ch] + from_left[ch, TS:, :].astype(f32) * has_left).astype(bf16)
+        rest[-1][ch] = (rim[ch] + from_left[ch].astype(f32) * has_left).astype(bf16)
 
 
 def finish_estimate(flags, base, shrink, from_left, above0, above1, *rest):
@@ -505,6 +540,7 @@
         dual_new[1, rows, :] = combined[1, rows, :] - im
 
 
+BANDS = [slice(k, k + OVER) for k in range(0, SPAN, OVER)]
 V = pl.BlockSpec(memory_space=pltpu.VMEM)
 S = pl.BlockSpec(memory_space=pltpu.SMEM)
 H = pl.BlockSpec(memory_space=pltpu.HBM)
@@ -517,6 +553,7 @@
 def call(body, name, outs, scratch=(), scalars=0, far=0, copies=0, aliases=None, held=0, flops=0):
     def run(*operands):
         near = len(operands) - scalars - far
+        place = pltpu.HBM if held < 0 else pltpu.VMEM
         spaces = [None] * (scalars + near) + [pltpu.HBM] * far
         operands = [
             v if space is None else pltpu.with_memory_space_constraint(v, space)
@@ -525,9 +562,9 @@
         return pl.pallas_call(
             body,
             in_specs=[S] * scalars + [V] * near + [H] * far,
-            out_specs=[V] * len(outs),
+            out_specs=[H if held < 0 else V] * len(outs),
             out_shape=[
-                pltpu.VMEM(shape, dtype) if k < held else jax.ShapeDtypeStruct(shape, dtype)
+                place(shape, dtype) if k < abs(held) else jax.ShapeDtypeStruct(shape, dtype)
                 for k, (shape, dtype) in enumerate(outs)
             ],
             scratch_shapes=[
@@ -587,51 +624,51 @@
     below.append(shifted(below[0], 0, -1))
     cards = [card] if two else [card, shifted(card, 1, 0)]
 
-    *staged, amps = call(
-        stage, "stage", [WIDE, WIDE, PLANES, measured], [None, PLANES, PLANES, measured, TABLE], 0, 5, 5,
-        held=3,
-    )(below[0], own, dual, probe, amps, order)
+    staged = call(
+        stage, "stage", [WIDE, WIDE, PLANES], [None, PLANES, PLANES], 0, 3, 3, held=3
+    )(own, dual, probe)
     staged = [pinned(v) for v in staged]
+    (amps,) = call(
+        reorder, "reorder", [measured], [None, measured, TABLE, measured], 0, 2, 3, held=-1
+    )(below[0], amps, order)
     inputs = (own, dual, probe, amps, fwd, bwd)
-    rim = ((2, OVER, L), bf16)
-    ext, acc, pnum, side, inner, *mids = call(
+    more = (len(cards) + 1) * CARD
+    sent = [(SPAN, more)] + ([(OVER, more), (TS, 0)] if two else [(SPAN, more)])
+    ext, acc, pnum, side, *inner = call(
         functools.partial(first_pass, two), "first_pass",
-        [WIDE, WIDE, SUMS] + [((2 * SPAN + (len(cards) + 1) * CARD, L), bf16)] * 2
-        + [rim] * (1 if two else 2),
+        [WIDE, WIDE, SUMS] + [((2 * rows + more, L), bf16) for rows, more in sent],
         [TABLE, TABLE, measured, None] + WORK, 1, 3, 3, aliases={6: 0, 7: 1}, flops=PASS,
     )(meta, flags, right, *below, *staged, *cards, fwd, bwd, amps)
     side = swapped(side, "tile", 1)
-    inner = inner_swapped(inner)
-
-    def down_and_up(rims):
-        down = shifted(rims[0], 1, 0)
-        return down, down if two else shifted(rims[1], -1, 0)
-
-    mid_above, mid_below = down_and_up(mids)
+    inner = [inner_swapped(part) for part in inner]
+
     rims = call(
-        functools.partial(between, two), "between", [((2, 2, OVER, L), bf16)] * (1 if two else 2)
-    )(flags, acc, side, inner, pnum, right, *below, mid_above, mid_below)
-    from_above, from_below = down_and_up(rims)
+        functools.partial(between, two), "between", [((2, OVER, L), bf16)] * (3 if two else 6)
+    )(flags, acc, side, inner[0], pnum, right, *below)
+    from_above = [shifted(rim, 1, 0) for rim in rims[:3]]
+    from_below = from_above if two else [shifted(rim, -1, 0) for rim in rims[3:]]
     weight, *inputs = call(
         functools.partial(weigh, two), "weigh",
         [((3, SPAN, L), f32), PLANES, PLANES, PLANES, measured, TABLE, TABLE],
         [None, ((2, PS, L), f32), ((3, SPAN + 2 * OVER, L), f32), ((24, L), f32),
          pltpu.SMEM((24, L), f32)],
         0, 6, 7, held=7,
-    )(*cards, flags, side, inner, rims[0], acc, pnum, right, below[0], below[2], mid_above, mid_below,
+    )(*cards, flags, side, inner[0], rims[0], acc, pnum, right, below[0], below[2],
       below[1], *inputs)
     weight, *inputs = [pinned(v) for v in (weight, *inputs)]
 
-    base, shrink, to_right, rim, to_below, pnum, to_swap = call(
-        second_pass, "second_pass",
-        [PLANES, ((2, TS, L), f32), ((2, SPAN, L), bf16), ((2, OVER, L), f32), ((2, OVER, L), bf16),
+    base, shrink, to_right, to_corner, rim, to_below, pnum, to_swap = call(
+        functools.partial(second_pass, two), "second_pass",
+        [PLANES, ((2, TS, L), f32), ((2, TS, L), bf16), ((2, OVER, L), bf16), ((2, OVER, L), f32),
+         ((2, OVER, L), bf16),
          SUMS, ((3, PS // 2, PS), bf16)],
         [PLANES, WIDE, WIDE] + WORK, 1, flops=PASS,
-    )(meta, flags, right, *below, acc, side, inner, mid_above, mid_below, from_above,
-      from_below, weight, pnum, *inputs)
+    )(meta, flags, right, *below, acc, side, *inner, *from_above,
+      *from_below, weight, pnum, *inputs)
+    corner = shifted(to_corner, 0, 1)
     from_left = shifted(to_right, 0, 1)
     above1 = shifted(to_below, 1, 0)
-    (to_below,) = call(add_rim, "add_rim", [((2, OVER, L), bf16)])(flags, rim, from_left, base, shrink)
+    (to_below,) = call(add_rim, "add_rim", [((2, OVER, L), bf16)])(flags, rim, corner, base, shrink)
     above0 = shifted(to_below, 1, 0)
 
     eight = n == 8

time: 67.4 us -> 67.3 us (level)
  the two profiles are of different devices: /device:TPU:9 before, /device:TPU:0 now
where the time goes in v6:
time: 67.3 us; the launch traced here: 66.5 us
  starting transfers between devices  29.5 us (44%)
  Pallas kernels  20.1 us (30%)
  waiting for transfers between devices  12.7 us (19%)
  other arithmetic  2.11 us (3%)
  between operations  1.49 us (2%)
    pallas_call x13, Pallas kernels, run(): pl.pallas_call(body, in_specs=[S] * scalars + [V] * near + [H] * far, out...  20.1 us
    ppermute x11, starting transfers between devices, shifted(): return lax.ppermute(value, 'tile', pairs)  14.7 us
    ppermute x9, starting transfers between devices, swapped(): return lax.ppermute(value, axis, [(i, i ^ bit) for i in range(n)])  13.5 us
    ppermute x11, waiting for transfers between devices, shifted(): return lax.ppermute(value, 'tile', pairs)  8.39 us
    ppermute x9, waiting for transfers between devices, swapped(): return lax.ppermute(value, axis, [(i, i ^ bit) for i in range(n)])  4.3 us
  transfers between devices with their start and end apart: 22, of which 8 were waited for; matrix products, arithmetic and copies ran while one was open for 1% of the time, Pallas kernels for 13%

profile of v6, /device:TPU:0, one launch (start us, length us, event | category | flops | bytes accessed | tf_op | source)
XLA Modules:
  0.0 66.5 jit_solution(4464784458686318499)
XLA Ops:
  0.6 1.1 %bitcast_convert_fusion = bf16[2,256,256]{2,1,0:T(8,128)(2,1)S(1)} fusion(f32[1,2,256,256]{3,2,1,0:T(8,128)} %param.9), kind=kLoop, calls=%fused_computation.12 | loop fusion | flops 131072 | bytes 786432 | tf_op jit(solution)/shard_map/convert_element_type | solution.py:611
  1.8 4.1 %collective-permute-start.1 = (bf16[256,128]{1,0:T(8,128)(2,1)S(1)}, bf16[256,128]{1,0:T(8,128)(2,1)S(1)}, u32[]{:S(2)}, u32[]{:S(2)}) collective-permute-start(bf16[256,128]{1,0:T(8,128)(2,1)S(1)} %bitcast.29), channel_id=1, source_target_pairs={{0,16},{4,20},{8,24},{12,28},{16,0},{20,4},{24,8},{28,12},{1,17},{... | collective-permute-start | bytes 196616 | tf_op jit(solution)/shard_map/ppermute | solution.py:52
  5.9 0.8 %collective-permute-start = (bf16[2,256,128]{2,1,0:T(8,128)(2,1)S(1)}, bf16[2,256,128]{2,1,0:T(8,128)(2,1)S(1)}, u32[]{:S(2)}, u32[]{:S(2)}) collective-permute-start(bf16[2,256,128]{2,1,0:T(8,128)(2,1)S(1)} %slice.12), channel_id=1, source_target_pairs={{0,12},{4,0},{8,4},{12,8},{16,28},{20,16},{24,20},{28,24},{1,13},{... | collective-permute-start | bytes 393224 | tf_op jit(solution)/shard_map/ppermute | solution.py:52
  8.3 1.4 %stage.1 = (f32[2,3,384,128]{3,2,1,0:T(8,128)S(1)}, f32[2,3,384,128]{3,2,1,0:T(8,128)S(1)}, f32[2,256,256]{2,1,0:T(8,128)S(1)}) custom-call(f32[2,256,256]{2,1,0:T(8,128)} %bitcast.22, f32[2,256,256]{2,1,0:T(8,128)} %bitcast.24, f32[2,256,256]{2,1,0:T(8,128)} %bitcast.20), custom_call_target="tpu_custom_call" | custom-call | flops 720896 | bytes 1572864 | tf_op jit(solution)/shard_map/stage/pallas_call | solution.py:562
  9.7 0.7 %collective-permute-start.3 = (bf16[256,128]{1,0:T(8,128)(2,1)S(1)}, bf16[256,128]{1,0:T(8,128)(2,1)S(1)}, u32[]{:S(2)}, u32[]{:S(2)}) collective-permute-start(bf16[256,128]{1,0:T(8,128)(2,1)S(1)} %collective-permute-done.1.below.below0.rest_2_.rest_8_), channel_id=1, source_target_pairs={{0,12},{4,0},{8,4},{12,8},{16,28},{20,16},{24,20},{28,24},{1,13},{... | collective-permute-start | bytes 196616 | tf_op jit(solution)/shard_map/ppermute | solution.py:52
  10.5 2.5 %reorder.1.rest_3_.rest_14_ = bf16[4,256,256]{2,1,0:T(8,128)(2,1)} custom-call(bf16[256,128]{1,0:T(8,128)(2,1)S(1)} %collective-permute-done.1.below.below0.rest_2_.rest_8_, bf16[4,256,256]{2,1,0:T(8,128)(2,1)} %bitcast.26, bf16[256,256]{1,0:T(8,128)(2,1)} %constant.65.clone.order_h), custom_call_target="tpu_custom_call" | custom-call | flops 262144 | bytes 655360 | tf_op jit(solution)/shard_map/reorder/pallas_call | solution.py:562
  13.0 1.2 %collective-permute-done.2.below1.rest_3_.rest_10_ = bf16[272,128]{1,0:T(8,128)(2,1)S(1)} collective-permute-done((bf16[272,128]{1,0:T(8,128)(2,1)S(1)}, bf16[272,128]{1,0:T(8,128)(2,1)S(1)}, u32[]{:S(2)}, u32[]{:S(2)}) %collective-permute-start.2) | collective-permute-done | bytes 69664 | tf_op jit(solution)/shard_map/ppermute | solution.py:52
  14.3 6.0 %first_pass.1 = (f32[2,3,384,128]{3,2,1,0:T(8,128)S(1)}, f32[2,3,384,128]{3,2,1,0:T(8,128)S(1)}, f32[3,256,256]{2,1,0:T(8,128)S(1)}, bf16[800,128]{1,0:T(8,128)(...) custom-call(s32[9]{0:T(128)S(1)} %pad_add_fusion.meta, ...), custom_call_target="tpu_custom_call", output_to_operand_aliasing={{0}: (6, {}), {1}: (7, {})} | custom-call | flops 1073741824 | bytes 786432 | tf_op jit(solution)/shard_map/first_pass/pallas_call | solution.py:562
  20.3 0.7 %collective-permute-start.5 = (bf16[288,128]{1,0:T(8,128)(2,1)S(1)}, bf16[288,128]{1,0:T(8,128)(2,1)S(1)}, u32[]{:S(2)}, u32[]{:S(2)}) collective-permute-start(bf16[288,128]{1,0:T(8,128)(2,1)S(1)} %get-tuple-element.41), channel_id=1, source_target_pairs={{0,0},{4,8},{8,4},{12,12},{16,16},{20,24},{24,20},{28,28},{1,1},{5... | collective-permute-start | bytes 221192 | tf_op jit(solution)/shard_map/ppermute | solution.py:66
  21.0 0.7 %collective-permute-start.6 = (bf16[512,128]{1,0:T(8,128)(2,1)S(1)}, bf16[512,128]{1,0:T(8,128)(2,1)S(1)}, u32[]{:S(2)}, u32[]{:S(2)}) collective-permute-start(bf16[512,128]{1,0:T(8,128)(2,1)S(1)} %get-tuple-element.42), channel_id=1, source_target_pairs={{0,0},{4,8},{8,4},{12,12},{16,16},{20,24},{24,20},{28,28},{1,1},{5... | collective-permute-start | bytes 393224 | tf_op jit(solution)/shard_map/ppermute | solution.py:66
  21.8 0.4 collective-permute-start.8
  22.3 2.6 %collective-permute-start.9 = (bf16[2,128,128]{2,1,0:T(8,128)(2,1)S(1)}, bf16[2,128,128]{2,1,0:T(8,128)(2,1)S(1)}, u32[]{:S(2)}, u32[]{:S(2)}) collective-permute-start(bf16[2,128,128]{2,1,0:T(8,128)(2,1)S(1)} %get-tuple-element.46), channel_id=1, source_target_pairs={{0,16},{4,20},{8,24},{12,28},{16,0},{20,4},{24,8},{28,12},{1,17},{... | collective-permute-start | bytes 196616 | tf_op jit(solution)/shard_map/ppermute | solution.py:52
  25.2 2.8 %weigh.1 = (f32[3,384,128]{2,1,0:T(8,128)S(1)}, f32[2,256,256]{2,1,0:T(8,128)S(1)}, f32[2,256,256]{2,1,0:T(8,128)S(1)}, f32[2,256,256]{2,1,0:T(8,128)S(1)}, bf16...) custom-call(bf16[16,128]{1,0:T(8,128)(2,1)S(1)} %fusion.5.rest_0_, ...), custom_call_target="tpu_custom_call" | custom-call | flops 933888 | bytes 2359296 | tf_op jit(solution)/shard_map/weigh/pallas_call | solution.py:562
  28.0 2.2 %collective-permute-done.7.rest_2_.rest_5_ = bf16[2,128,128]{2,1,0:T(8,128)(2,1)S(1)} collective-permute-done((bf16[2,128,128]{2,1,0:T(8,128)(2,1)S(1)}, bf16[2,128,128]{2,1,0:T(8,128)(2,1)S(1)}, u32[]{:S(2)}, u32[]{:S(2)}) %collective-permute-start.7) | collective-permute-done | bytes 65568 | tf_op jit(solution)/shard_map/ppermute | solution.py:52
  30.2 5.8 %second_pass.1 = (f32[2,256,256]{2,1,0:T(8,128)S(1)}, f32[2,256,128]{2,1,0:T(8,128)S(1)}, bf16[2,256,128]{2,1,0:T(8,128)(2,1)S(1)}, bf16[2,128,128]{2,1,0:T(8,12...) custom-call(s32[9]{0:T(128)S(1)} %pad_add_fusion.meta, ...), custom_call_target="tpu_custom_call" | custom-call | flops 1073741824 | tf_op jit(solution)/shard_map/second_pass/pallas_call | solution.py:562
  36.0 4.3 %collective-permute-start.14 = (bf16[3,128,256]{2,1,0:T(8,128)(2,1)S(1)}, bf16[3,128,256]{2,1,0:T(8,128)(2,1)S(1)}, u32[]{:S(2)}, u32[]{:S(2)}) collective-permute-start(bf16[3,128,256]{2,1,0:T(8,128)(2,1)S(1)} %get-tuple-element.61), channel_id=1, source_target_pairs={{0,4},{4,0},{8,12},{12,8},{16,20},{20,16},{24,28},{28,24},{1,5},{5... | collective-permute-start | bytes 589832 | tf_op jit(solution)/shard_map/ppermute | solution.py:57
  40.4 1.0 %collective-permute-start.10 = (bf16[2,256,128]{2,1,0:T(8,128)(2,1)S(1)}, bf16[2,256,128]{2,1,0:T(8,128)(2,1)S(1)}, u32[]{:S(2)}, u32[]{:S(2)}) collective-permute-start(bf16[2,256,128]{2,1,0:T(8,128)(2,1)S(1)} %get-tuple-element.56), channel_id=1, source_target_pairs={{0,4},{4,8},{8,12},{12,0},{16,20},{20,24},{24,28},{28,16},{1,5},{5... | collective-permute-start | bytes 393224 | tf_op jit(solution)/shard_map/ppermute | solution.py:52
  41.6 1.3 %collective-permute-start.19 = (bf16[3,128,256]{2,1,0:T(8,128)(2,1)S(1)}, bf16[3,128,256]{2,1,0:T(8,128)(2,1)S(1)}, u32[]{:S(2)}, u32[]{:S(2)}) collective-permute-start(bf16[3,128,256]{2,1,0:T(8,128)(2,1)S(1)} %halve.1.rest_0_.held), channel_id=1, source_target_pairs={{0,8},{4,12},{8,0},{12,4},{16,24},{20,28},{24,16},{28,20},{1,9},{5... | collective-permute-start | bytes 589832 | tf_op jit(solution)/shard_map/ppermute | solution.py:57
  42.9 3.7 %collective-permute-start.13 = (bf16[2,128,128]{2,1,0:T(8,128)(2,1)S(1)}, bf16[2,128,128]{2,1,0:T(8,128)(2,1)S(1)}, u32[]{:S(2)}, u32[]{:S(2)}) collective-permute-start(bf16[2,128,128]{2,1,0:T(8,128)(2,1)S(1)} %get-tuple-element.59), channel_id=1, source_target_pairs={{0,16},{4,20},{8,24},{12,28},{16,0},{20,4},{24,8},{28,12},{1,17},{... | collective-permute-start | bytes 196616 | tf_op jit(solution)/shard_map/ppermute | solution.py:52
  46.7 0.5 collective-permute-start.12
  47.2 2.5 %collective-permute-done.13.above1 = bf16[2,128,128]{2,1,0:T(8,128)(2,1)S(1)} collective-permute-done((bf16[2,128,128]{2,1,0:T(8,128)(2,1)S(1)}, bf16[2,128,128]{2,1,0:T(8,128)(2,1)S(1)}, u32[]{:S(2)}, u32[]{:S(2)}) %collective-permute-start.13) | collective-permute-done | bytes 65568 | tf_op jit(solution)/shard_map/ppermute | solution.py:52
  49.7 2.5 %collective-permute-done.12.above0 = bf16[2,128,128]{2,1,0:T(8,128)(2,1)S(1)} collective-permute-done((bf16[2,128,128]{2,1,0:T(8,128)(2,1)S(1)}, bf16[2,128,128]{2,1,0:T(8,128)(2,1)S(1)}, u32[]{:S(2)}, u32[]{:S(2)}) %collective-permute-start.12) | collective-permute-done | bytes 65568 | tf_op jit(solution)/shard_map/ppermute | solution.py:52
  52.3 1.0 %collective-permute-start.16 = (bf16[2,128,256]{2,1,0:T(8,128)(2,1)S(1)}, bf16[2,128,256]{2,1,0:T(8,128)(2,1)S(1)}, u32[]{:S(2)}, u32[]{:S(2)}) collective-permute-start(bf16[2,128,256]{2,1,0:T(8,128)(2,1)S(1)} %get-tuple-element.63.refs_2_), channel_id=1, source_target_pairs={{0,2},{1,3},{2,0},{3,1},{4,6},{5,7},{6,4},{7,5},{8,10},{9,11},{10,... | collective-permute-start | bytes 393224 | tf_op jit(solution)/shard_map/ppermute | solution.py:57
  53.3 1.4 %collective-permute-start.15 = (bf16[2,128,256]{2,1,0:T(8,128)(2,1)S(1)}, bf16[2,128,256]{2,1,0:T(8,128)(2,1)S(1)}, u32[]{:S(2)}, u32[]{:S(2)}) collective-permute-start(bf16[2,128,256]{2,1,0:T(8,128)(2,1)S(1)} %get-tuple-element.62.refs_0_.rest_0_), channel_id=1, source_target_pairs={{0,1},{1,0},{2,3},{3,2},{4,5},{5,4},{6,7},{7,6},{8,9},{9,8},{10,11... | collective-permute-start | bytes 393224 | tf_op jit(solution)/shard_map/ppermute | solution.py:57
  54.7 2.8 %collective-permute-start.20 = (bf16[3,128,256]{2,1,0:T(8,128)(2,1)S(1)}, bf16[3,128,256]{2,1,0:T(8,128)(2,1)S(1)}, u32[]{:S(2)}, u32[]{:S(2)}) collective-permute-start(bf16[3,128,256]{2,1,0:T(8,128)(2,1)S(1)} %add.23.held), channel_id=1, source_target_pairs={{0,24},{4,28},{8,16},{12,20},{16,8},{20,12},{24,0},{28,4},{1,25},{... | collective-permute-start | bytes 589832 | tf_op jit(solution)/shard_map/ppermute | solution.py:57
  57.5 0.7 %collective-permute-done.15.refs_1_ = bf16[2,128,256]{2,1,0:T(8,128)(2,1)S(1)} collective-permute-done((bf16[2,128,256]{2,1,0:T(8,128)(2,1)S(1)}, bf16[2,128,256]{2,1,0:T(8,128)(2,1)S(1)}, u32[]{:S(2)}, u32[]{:S(2)}) %collective-permute-start.15) | collective-permute-done | bytes 131104 | tf_op jit(solution)/shard_map/ppermute | solution.py:57
  58.3 1.1 %collective-permute-start.17 = (bf16[2,128,256]{2,1,0:T(8,128)(2,1)S(1)}, bf16[2,128,256]{2,1,0:T(8,128)(2,1)S(1)}, u32[]{:S(2)}, u32[]{:S(2)}) collective-permute-start(bf16[2,128,256]{2,1,0:T(8,128)(2,1)S(1)} %get-tuple-element.64.first), channel_id=1, source_target_pairs={{0,2},{1,3},{2,0},{3,1},{4,6},{5,7},{6,4},{7,5},{8,10},{9,11},{10,... | collective-permute-start | bytes 393224 | tf_op jit(solution)/shard_map/ppermute | solution.py:57
  59.4 1.3 %collective-permute-start.18 = (bf16[2,128,256]{2,1,0:T(8,128)(2,1)S(1)}, bf16[2,128,256]{2,1,0:T(8,128)(2,1)S(1)}, u32[]{:S(2)}, u32[]{:S(2)}) collective-permute-start(bf16[2,128,256]{2,1,0:T(8,128)(2,1)S(1)} %get-tuple-element.65.second), channel_id=1, source_target_pairs={{0,1},{1,0},{2,3},{3,2},{4,5},{5,4},{6,7},{7,6},{8,9},{9,8},{10,11... | collective-permute-start | bytes 393224 | tf_op jit(solution)/shard_map/ppermute | solution.py:57
  60.8 2.6 %collective-permute-done.17.first_came.rest_0_ = bf16[2,128,256]{2,1,0:T(8,128)(2,1)S(1)} collective-permute-done((bf16[2,128,256]{2,1,0:T(8,128)(2,1)S(1)}, bf16[2,128,256]{2,1,0:T(8,128)(2,1)S(1)}, u32[]{:S(2)}, u32[]{:S(2)}) %collective-permute-start.17) | collective-permute-done | bytes 131104 | tf_op jit(solution)/shard_map/ppermute | solution.py:57
  63.5 0.9 %collective-permute-done.18.second_came = bf16[2,128,256]{2,1,0:T(8,128)(2,1)S(1)} collective-permute-done((bf16[2,128,256]{2,1,0:T(8,128)(2,1)S(1)}, bf16[2,128,256]{2,1,0:T(8,128)(2,1)S(1)}, u32[]{:S(2)}, u32[]{:S(2)}) %collective-permute-start.18) | collective-permute-done | bytes 131104 | tf_op jit(solution)/shard_map/ppermute | solution.py:57
  64.4 1.2 %settle.1 = (f32[2,256,256]{2,1,0:T(8,128)}, f32[2,256,256]{2,1,0:T(8,128)}) custom-call(bf16[2,128,256]{2,1,0:T(8,128)(2,1)S(1)} %get-tuple-element.64.first, bf16[2,128,256]{2,1,0:T(8,128)(2,1)S(1)} %collective-permute-done.17.first_came.rest_0_, bf16[2,128,256]{2,1,0:T(8,128)(2,1)S(1)} %get-tuple-element.65.second, ...), custom_call_target="tpu_custom_call" | custom-call | flops 262144 | tf_op jit(solution)/shard_map/settle/pallas_call | solution.py:562
  65.6 0.9 %convert_add_fusion = f32[1,2,256,256]{3,2,1,0:T(8,128)} fusion(f32[1,2,256,256]{3,2,1,0:T(8,128)S(1)} %copy-done, bf16[1,2,128,256]{3,2,1,0:T(8,128)(2,1)S(1)} %bitcast.19, bf16[1,2,128,256]{3,2,1,0:T(8,128)(2,1)S(1)} %bitcast.28, pred[]{:T(512)} %eq.8), kind=kLoop, calls=%fused_computation | loop fusion | flops 1441792 | bytes 1310721 | tf_op jit(solution)/shard_map/add | solution.py:696
  (44 shorter events, 2.3 us)
Async XLA Ops:
  0.6 6.7 %copy-start.1 = (s32[1,1,4,2]{2,3,1,0:T(2,128)S(1)}, s32[1,1,4,2]{2,3,1,0:T(2,128)}, u32[]{:S(2)}) copy-start(s32[1,1,4,2]{2,3,1,0:T(2,128)} %param.13) | copy-start | bytes 100
  1.8 7.9 %collective-permute-start.1 = (bf16[256,128]{1,0:T(8,128)(2,1)S(1)}, bf16[256,128]{1,0:T(8,128)(2,1)S(1)}, u32[]{:S(2)}, u32[]{:S(2)}) collective-permute-start(bf16[256,128]{1,0:T(8,128)(2,1)S(1)} %bitcast.29), channel_id=1, source_target_pairs={{0,16},{4,20},{8,24},{12,28},{16,0},{20,4},{24,8},{28,12},{1,17},{... | collective-permute-start | bytes 196616 | tf_op jit(solution)/shard_map/ppermute | solution.py:52
  5.9 8.3 %collective-permute-start = (bf16[2,256,128]{2,1,0:T(8,128)(2,1)S(1)}, bf16[2,256,128]{2,1,0:T(8,128)(2,1)S(1)}, u32[]{:S(2)}, u32[]{:S(2)}) collective-permute-start(bf16[2,256,128]{2,1,0:T(8,128)(2,1)S(1)} %slice.12), channel_id=1, source_target_pairs={{0,12},{4,0},{8,4},{12,8},{16,28},{20,16},{24,20},{28,24},{1,13},{... | collective-permute-start | bytes 393224 | tf_op jit(solution)/shard_map/ppermute | solution.py:52
  7.6 6.6 %collective-permute-start.2 = (bf16[272,128]{1,0:T(8,128)(2,1)S(1)}, bf16[272,128]{1,0:T(8,128)(2,1)S(1)}, u32[]{:S(2)}, u32[]{:S(2)}) collective-permute-start(bf16[272,128]{1,0:T(8,128)(2,1)S(1)} %pad_maximum_fusion), channel_id=1, source_target_pairs={{0,16},{4,20},{8,24},{12,28},{16,0},{20,4},{24,8},{28,12},{1,17},{... | collective-permute-start | bytes 208904 | tf_op jit(solution)/shard_map/ppermute | solution.py:52
  9.7 4.5 %collective-permute-start.3 = (bf16[256,128]{1,0:T(8,128)(2,1)S(1)}, bf16[256,128]{1,0:T(8,128)(2,1)S(1)}, u32[]{:S(2)}, u32[]{:S(2)}) collective-permute-start(bf16[256,128]{1,0:T(8,128)(2,1)S(1)} %collective-permute-done.1.below.below0.rest_2_.rest_8_), channel_id=1, source_target_pairs={{0,12},{4,0},{8,4},{12,8},{16,28},{20,16},{24,20},{28,24},{1,13},{... | collective-permute-start | bytes 196616 | tf_op jit(solution)/shard_map/ppermute | solution.py:52
  20.3 1.5 %collective-permute-start.4 = (bf16[800,128]{1,0:T(8,128)(2,1)S(1)}, bf16[800,128]{1,0:T(8,128)(2,1)S(1)}, u32[]{:S(2)}, u32[]{:S(2)}) collective-permute-start(bf16[800,128]{1,0:T(8,128)(2,1)S(1)} %get-tuple-element.40), channel_id=1, source_target_pairs={{0,4},{4,0},{8,12},{12,8},{16,20},{20,16},{24,28},{28,24},{1,5},{5... | collective-permute-start | bytes 614408 | tf_op jit(solution)/shard_map/ppermute | solution.py:57
  20.3 1.4 %collective-permute-start.5 = (bf16[288,128]{1,0:T(8,128)(2,1)S(1)}, bf16[288,128]{1,0:T(8,128)(2,1)S(1)}, u32[]{:S(2)}, u32[]{:S(2)}) collective-permute-start(bf16[288,128]{1,0:T(8,128)(2,1)S(1)} %get-tuple-element.41), channel_id=1, source_target_pairs={{0,0},{4,8},{8,4},{12,12},{16,16},{20,24},{24,20},{28,28},{1,1},{5... | collective-permute-start | bytes 221192 | tf_op jit(solution)/shard_map/ppermute | solution.py:66
  21.0 7.0 %collective-permute-start.6 = (bf16[512,128]{1,0:T(8,128)(2,1)S(1)}, bf16[512,128]{1,0:T(8,128)(2,1)S(1)}, u32[]{:S(2)}, u32[]{:S(2)}) collective-permute-start(bf16[512,128]{1,0:T(8,128)(2,1)S(1)} %get-tuple-element.42), channel_id=1, source_target_pairs={{0,0},{4,8},{8,4},{12,12},{16,16},{20,24},{24,20},{28,28},{1,1},{5... | collective-permute-start | bytes 393224 | tf_op jit(solution)/shard_map/ppermute | solution.py:66
  21.8 6.2 %collective-permute-start.8 = (bf16[2,128,128]{2,1,0:T(8,128)(2,1)S(1)}, bf16[2,128,128]{2,1,0:T(8,128)(2,1)S(1)}, u32[]{:S(2)}, u32[]{:S(2)}) collective-permute-start(bf16[2,128,128]{2,1,0:T(8,128)(2,1)S(1)} %get-tuple-element.45), channel_id=1, source_target_pairs={{0,16},{4,20},{8,24},{12,28},{16,0},{20,4},{24,8},{28,12},{1,17},{... | collective-permute-start | bytes 196616 | tf_op jit(solution)/shard_map/ppermute | solution.py:52
  22.3 5.8 %collective-permute-start.9 = (bf16[2,128,128]{2,1,0:T(8,128)(2,1)S(1)}, bf16[2,128,128]{2,1,0:T(8,128)(2,1)S(1)}, u32[]{:S(2)}, u32[]{:S(2)}) collective-permute-start(bf16[2,128,128]{2,1,0:T(8,128)(2,1)S(1)} %get-tuple-element.46), channel_id=1, source_target_pairs={{0,16},{4,20},{8,24},{12,28},{16,0},{20,4},{24,8},{28,12},{1,17},{... | collective-permute-start | bytes 196616 | tf_op jit(solution)/shard_map/ppermute | solution.py:52
  24.8 5.4 %collective-permute-start.7 = (bf16[2,128,128]{2,1,0:T(8,128)(2,1)S(1)}, bf16[2,128,128]{2,1,0:T(8,128)(2,1)S(1)}, u32[]{:S(2)}, u32[]{:S(2)}) collective-permute-start(bf16[2,128,128]{2,1,0:T(8,128)(2,1)S(1)} %get-tuple-element.44.rest_4_), channel_id=1, source_target_pairs={{0,16},{4,20},{8,24},{12,28},{16,0},{20,4},{24,8},{28,12},{1,17},{... | collective-permute-start | bytes 196616 | tf_op jit(solution)/shard_map/ppermute | solution.py:52
  36.0 5.5 %collective-permute-start.14 = (bf16[3,128,256]{2,1,0:T(8,128)(2,1)S(1)}, bf16[3,128,256]{2,1,0:T(8,128)(2,1)S(1)}, u32[]{:S(2)}, u32[]{:S(2)}) collective-permute-start(bf16[3,128,256]{2,1,0:T(8,128)(2,1)S(1)} %get-tuple-element.61), channel_id=1, source_target_pairs={{0,4},{4,0},{8,12},{12,8},{16,20},{20,16},{24,28},{28,24},{1,5},{5... | collective-permute-start | bytes 589832 | tf_op jit(solution)/shard_map/ppermute | solution.py:57
  40.3 6.3 %collective-permute-start.11 = (bf16[2,128,128]{2,1,0:T(8,128)(2,1)S(1)}, bf16[2,128,128]{2,1,0:T(8,128)(2,1)S(1)}, u32[]{:S(2)}, u32[]{:S(2)}) collective-permute-start(bf16[2,128,128]{2,1,0:T(8,128)(2,1)S(1)} %get-tuple-element.58), channel_id=1, source_target_pairs={{0,4},{4,8},{8,12},{12,0},{16,20},{20,24},{24,28},{28,16},{1,5},{5... | collective-permute-start | bytes 196616 | tf_op jit(solution)/shard_map/ppermute | solution.py:52
  40.4 11.7 %collective-permute-start.10 = (bf16[2,256,128]{2,1,0:T(8,128)(2,1)S(1)}, bf16[2,256,128]{2,1,0:T(8,128)(2,1)S(1)}, u32[]{:S(2)}, u32[]{:S(2)}) collective-permute-start(bf16[2,256,128]{2,1,0:T(8,128)(2,1)S(1)} %get-tuple-element.56), channel_id=1, source_target_pairs={{0,4},{4,8},{8,12},{12,0},{16,20},{20,24},{24,28},{28,16},{1,5},{5... | collective-permute-start | bytes 393224 | tf_op jit(solution)/shard_map/ppermute | solution.py:52
  41.6 13.1 %collective-permute-start.19 = (bf16[3,128,256]{2,1,0:T(8,128)(2,1)S(1)}, bf16[3,128,256]{2,1,0:T(8,128)(2,1)S(1)}, u32[]{:S(2)}, u32[]{:S(2)}) collective-permute-start(bf16[3,128,256]{2,1,0:T(8,128)(2,1)S(1)} %halve.1.rest_0_.held), channel_id=1, source_target_pairs={{0,8},{4,12},{8,0},{12,4},{16,24},{20,28},{24,16},{28,20},{1,9},{5... | collective-permute-start | bytes 589832 | tf_op jit(solution)/shard_map/ppermute | solution.py:57
  42.9 6.8 %collective-permute-start.13 = (bf16[2,128,128]{2,1,0:T(8,128)(2,1)S(1)}, bf16[2,128,128]{2,1,0:T(8,128)(2,1)S(1)}, u32[]{:S(2)}, u32[]{:S(2)}) collective-permute-start(bf16[2,128,128]{2,1,0:T(8,128)(2,1)S(1)} %get-tuple-element.59), channel_id=1, source_target_pairs={{0,16},{4,20},{8,24},{12,28},{16,0},{20,4},{24,8},{28,12},{1,17},{... | collective-permute-start | bytes 196616 | tf_op jit(solution)/shard_map/ppermute | solution.py:52
  46.7 5.5 %collective-permute-start.12 = (bf16[2,128,128]{2,1,0:T(8,128)(2,1)S(1)}, bf16[2,128,128]{2,1,0:T(8,128)(2,1)S(1)}, u32[]{:S(2)}, u32[]{:S(2)}) collective-permute-start(bf16[2,128,128]{2,1,0:T(8,128)(2,1)S(1)} %add_rim.1), channel_id=1, source_target_pairs={{0,16},{4,20},{8,24},{12,28},{16,0},{20,4},{24,8},{28,12},{1,17},{... | collective-permute-start | bytes 196616 | tf_op jit(solution)/shard_map/ppermute | solution.py:52
  52.3 5.3 %collective-permute-start.16 = (bf16[2,128,256]{2,1,0:T(8,128)(2,1)S(1)}, bf16[2,128,256]{2,1,0:T(8,128)(2,1)S(1)}, u32[]{:S(2)}, u32[]{:S(2)}) collective-permute-start(bf16[2,128,256]{2,1,0:T(8,128)(2,1)S(1)} %get-tuple-element.63.refs_2_), channel_id=1, source_target_pairs={{0,2},{1,3},{2,0},{3,1},{4,6},{5,7},{6,4},{7,5},{8,10},{9,11},{10,... | collective-permute-start | bytes 393224 | tf_op jit(solution)/shard_map/ppermute | solution.py:57
  53.3 5.0 %collective-permute-start.15 = (bf16[2,128,256]{2,1,0:T(8,128)(2,1)S(1)}, bf16[2,128,256]{2,1,0:T(8,128)(2,1)S(1)}, u32[]{:S(2)}, u32[]{:S(2)}) collective-permute-start(bf16[2,128,256]{2,1,0:T(8,128)(2,1)S(1)} %get-tuple-element.62.refs_0_.rest_0_), channel_id=1, source_target_pairs={{0,1},{1,0},{2,3},{3,2},{4,5},{5,4},{6,7},{7,6},{8,9},{9,8},{10,11... | collective-permute-start | bytes 393224 | tf_op jit(solution)/shard_map/ppermute | solution.py:57
  54.7 10.9 %copy-start = (f32[1,2,256,256]{3,2,1,0:T(8,128)S(1)}, f32[1,2,256,256]{3,2,1,0:T(8,128)}, u32[]{:S(2)}) copy-start(f32[1,2,256,256]{3,2,1,0:T(8,128)} %param.11) | copy-start | bytes 1572868
  54.7 8.6 %collective-permute-start.20 = (bf16[3,128,256]{2,1,0:T(8,128)(2,1)S(1)}, bf16[3,128,256]{2,1,0:T(8,128)(2,1)S(1)}, u32[]{:S(2)}, u32[]{:S(2)}) collective-permute-start(bf16[3,128,256]{2,1,0:T(8,128)(2,1)S(1)} %add.23.held), channel_id=1, source_target_pairs={{0,24},{4,28},{8,16},{12,20},{16,8},{20,12},{24,0},{28,4},{1,25},{... | collective-permute-start | bytes 589832 | tf_op jit(solution)/shard_map/ppermute | solution.py:57
  58.3 5.0 %collective-permute-start.17 = (bf16[2,128,256]{2,1,0:T(8,128)(2,1)S(1)}, bf16[2,128,256]{2,1,0:T(8,128)(2,1)S(1)}, u32[]{:S(2)}, u32[]{:S(2)}) collective-permute-start(bf16[2,128,256]{2,1,0:T(8,128)(2,1)S(1)} %get-tuple-element.64.first), channel_id=1, source_target_pairs={{0,2},{1,3},{2,0},{3,1},{4,6},{5,7},{6,4},{7,5},{8,10},{9,11},{10,... | collective-permute-start | bytes 393224 | tf_op jit(solution)/shard_map/ppermute | solution.py:57
  59.4 5.0 %collective-permute-start.18 = (bf16[2,128,256]{2,1,0:T(8,128)(2,1)S(1)}, bf16[2,128,256]{2,1,0:T(8,128)(2,1)S(1)}, u32[]{:S(2)}, u32[]{:S(2)}) collective-permute-start(bf16[2,128,256]{2,1,0:T(8,128)(2,1)S(1)} %get-tuple-element.65.second), channel_id=1, source_target_pairs={{0,1},{1,0},{2,3},{3,2},{4,5},{5,4},{6,7},{7,6},{8,9},{9,8},{10,11... | collective-permute-start | bytes 393224 | tf_op jit(solution)/shard_map/ppermute | solution.py:57
  63.4 2.2 %collective-permute-start.21 = (bf16[2,128,256]{2,1,0:T(8,128)(2,1)S(1)}, bf16[2,128,256]{2,1,0:T(8,128)(2,1)S(1)}, u32[]{:S(2)}, u32[]{:S(2)}) collective-permute-start(bf16[2,128,256]{2,1,0:T(8,128)(2,1)S(1)} %update.1), channel_id=1, source_target_pairs={{0,4},{4,0},{8,12},{12,8},{16,20},{20,16},{24,28},{28,24},{1,5},{5... | collective-permute-start | bytes 393224 | tf_op jit(solution)/shard_map/ppermute | solution.py:57

commit v7 on v6

--- a/solution.py
+++ b/solution.py
@@ -271,6 +271,8 @@
     column = [card[...] for card in cards] + [below1[2 * OVER :, :]]
     side[2 * SPAN :, :] = jnp.concatenate(column, 0)
     inner[0][2 * (OVER if two else SPAN) :, :] = jnp.concatenate(column, 0)
+    if two:
+        inner[1][2 * TS :, :] = cards[0][...]
     for ch in range(2):
         side[plane(ch, SPAN), :] = jnp.where(odd, acc[ch, 0], acc[ch, 2]).astype(bf16)
         other = [jnp.where(odd, acc[ch, 2, rows, :], acc[ch, 0, rows, :]) for rows in BANDS]
@@ -315,7 +317,7 @@
 
 
 def between(two, flags, acc, side, inner, *rest):
-    outs = rest[-3:] if two else rest[-6:]
+    outs = rest[-2:] if two else rest[-4:]
     for ch in range(2):
         for j in range(3):
             rims = rims_of(two, flags, lambda rows: acc[ch, j, rows, :])
@@ -329,7 +331,10 @@
                     other = inner[plane(ch, size, start, OVER), :]
                     rims[k] = rims[k] + from_sides(flags, sides[k], other)[j // 2]
             for k, rim in enumerate(rims):
-                outs[3 * k + j][ch] = rim.astype(bf16)
+                if j < 2:
+                    outs[2 * k][ch, j] = rim.astype(bf16)
+                else:
+                    outs[2 * k + 1][ch] = rim.astype(bf16)
 
 
 def weigh(two, *rest):
@@ -395,7 +400,7 @@
     two, meta, flags, right, below0, below1, diag, acc1, side, *rest,
 ):
     inner, rest = rest[: 2 if two else 1], rest[2 if two else 1 :]
-    from_above, from_below, rest = rest[:3], rest[3:6], rest[6:]
+    from_above, from_below, rest = rest[:2], rest[2:4], rest[4:]
     weight, pnum1, own, dual, probe, amps, fwd, bwd = rest[:8]
     base, shrink, to_right, to_corner, lower, to_below, pnum, to_swap = rest[8:16]
     partial, ext, acc, win, X, Y, W = rest[16:]
@@ -416,11 +421,11 @@
                         flags, side[at, :], from_inner(two, flags, inner, ch, k, 64)
                     )[j // 2]
                 if k < OVER:
-                    came = from_above[j][ch, rows, :]
+                    came = from_above[0][ch, j, rows, :] if j < 2 else from_above[1][ch, rows, :]
                     total = total + came.astype(f32) * has_above
                 if k >= TS:
                     rim = slice(k - TS, k - TS + 64)
-                    came = from_below[j][ch, rim, :]
+                    came = from_below[0][ch, j, rim, :] if j < 2 else from_below[1][ch, rim, :]
                     total = total + came.astype(f32)
                 step = total / (weight[j, rows, :] + penalty)
                 if j < 2 and k < TS:
@@ -633,7 +638,7 @@
     )(below[0], amps, order)
     inputs = (own, dual, probe, amps, fwd, bwd)
     more = (len(cards) + 1) * CARD
-    sent = [(SPAN, more)] + ([(OVER, more), (TS, 0)] if two else [(SPAN, more)])
+    sent = [(SPAN, more)] + ([(OVER, more), (TS, CARD)] if two else [(SPAN, more)])
     ext, acc, pnum, side, *inner = call(
         functools.partial(first_pass, two), "first_pass",
         [WIDE, WIDE, SUMS] + [((2 * rows + more, L), bf16) for rows, more in sent],
@@ -643,10 +648,10 @@
     inner = [inner_swapped(part) for part in inner]
 
     rims = call(
-        functools.partial(between, two), "between", [((2, OVER, L), bf16)] * (3 if two else 6)
+        functools.partial(between, two), "between", [((2, 2, OVER, L), bf16), ((2, OVER, L), bf16)] * (1 if two else 2)
     )(flags, acc, side, inner[0], pnum, right, *below)
-    from_above = [shifted(rim, 1, 0) for rim in rims[:3]]
-    from_below = from_above if two else [shifted(rim, -1, 0) for rim in rims[3:]]
+    from_above = [shifted(rim, 1, 0) for rim in rims[:2]]
+    from_below = from_above if two else [shifted(rim, -1, 0) for rim in rims[2:]]
     weight, *inputs = call(
         functools.partial(weigh, two), "weigh",
         [((3, SPAN, L), f32), PLANES, PLANES, PLANES, measured, TABLE, TABLE],

time: 67.3 us -> 66.5 us (0.988)
  the two profiles are of different devices: /device:TPU:0 before, /device:TPU:9 now
where the time goes in v7:
time: 66.5 us; the launch traced here: 65.8 us
  starting transfers between devices  27.3 us (41%)
  waiting for transfers between devices  18.7 us (28%)
  Pallas kernels  15.6 us (23%)
  other arithmetic  2.11 us (3%)
  between operations  1.51 us (2%)
    ppermute x9, starting transfers between devices, swapped(): return lax.ppermute(value, axis, [(i, i ^ bit) for i in range(n)])  15.6 us
    pallas_call x13, Pallas kernels, run(): pl.pallas_call(body, in_specs=[S] * scalars + [V] * near + [H] * far, out...  15.6 us
    ppermute x10, starting transfers between devices, shifted(): return lax.ppermute(value, 'tile', pairs)  10.4 us
    ppermute x10, waiting for transfers between devices, shifted(): return lax.ppermute(value, 'tile', pairs)  9.71 us
    ppermute x9, waiting for transfers between devices, swapped(): return lax.ppermute(value, axis, [(i, i ^ bit) for i in range(n)])  9.02 us
  transfers between devices with their start and end apart: 21, of which 9 were waited for; matrix products, arithmetic and copies ran while one was open for 1% of the time, Pallas kernels for 12%

profile of v7, /device:TPU:9, one launch (start us, length us, event | category | flops | bytes accessed | tf_op | source)
XLA Modules:
  0.0 65.8 jit_solution(14804353885735111891)
XLA Ops:
  0.6 1.1 %bitcast_convert_fusion = bf16[2,256,256]{2,1,0:T(8,128)(2,1)S(1)} fusion(f32[1,2,256,256]{3,2,1,0:T(8,128)} %param.9), kind=kLoop, calls=%fused_computation.12 | loop fusion | flops 131072 | bytes 786432 | tf_op jit(solution)/shard_map/convert_element_type | solution.py:616
  1.8 2.4 %collective-permute-start.1 = (bf16[256,128]{1,0:T(8,128)(2,1)S(1)}, bf16[256,128]{1,0:T(8,128)(2,1)S(1)}, u32[]{:S(2)}, u32[]{:S(2)}) collective-permute-start(bf16[256,128]{1,0:T(8,128)(2,1)S(1)} %bitcast.29), channel_id=1, source_target_pairs={{0,16},{4,20},{8,24},{12,28},{16,0},{20,4},{24,8},{28,12},{1,17},{... | collective-permute-start | bytes 196616 | tf_op jit(solution)/shard_map/ppermute | solution.py:52
  4.1 1.0 %collective-permute-start = (bf16[2,256,128]{2,1,0:T(8,128)(2,1)S(1)}, bf16[2,256,128]{2,1,0:T(8,128)(2,1)S(1)}, u32[]{:S(2)}, u32[]{:S(2)}) collective-permute-start(bf16[2,256,128]{2,1,0:T(8,128)(2,1)S(1)} %slice.12), channel_id=1, source_target_pairs={{0,12},{4,0},{8,4},{12,8},{16,28},{20,16},{24,20},{28,24},{1,13},{... | collective-permute-start | bytes 393224 | tf_op jit(solution)/shard_map/ppermute | solution.py:52
  5.8 0.1 copy.17
  6.1 0.1 collective-permute-start.2
  6.5 1.4 %stage.1 = (f32[2,3,384,128]{3,2,1,0:T(8,128)S(1)}, f32[2,3,384,128]{3,2,1,0:T(8,128)S(1)}, f32[2,256,256]{2,1,0:T(8,128)S(1)}) custom-call(f32[2,256,256]{2,1,0:T(8,128)} %bitcast.22, f32[2,256,256]{2,1,0:T(8,128)} %bitcast.24, f32[2,256,256]{2,1,0:T(8,128)} %bitcast.20), custom_call_target="tpu_custom_call" | custom-call | flops 720896 | bytes 1572864 | tf_op jit(solution)/shard_map/stage/pallas_call | solution.py:567
  7.9 0.9 %collective-permute-start.3 = (bf16[256,128]{1,0:T(8,128)(2,1)S(1)}, bf16[256,128]{1,0:T(8,128)(2,1)S(1)}, u32[]{:S(2)}, u32[]{:S(2)}) collective-permute-start(bf16[256,128]{1,0:T(8,128)(2,1)S(1)} %collective-permute-done.1.below.below0.rest_2_.rest_8_), channel_id=1, source_target_pairs={{0,12},{4,0},{8,4},{12,8},{16,28},{20,16},{24,20},{28,24},{1,13},{... | collective-permute-start | bytes 196616 | tf_op jit(solution)/shard_map/ppermute | solution.py:52
  8.8 2.5 %reorder.1.rest_3_.rest_14_ = bf16[4,256,256]{2,1,0:T(8,128)(2,1)} custom-call(bf16[256,128]{1,0:T(8,128)(2,1)S(1)} %collective-permute-done.1.below.below0.rest_2_.rest_8_, bf16[4,256,256]{2,1,0:T(8,128)(2,1)} %bitcast.26, bf16[256,256]{1,0:T(8,128)(2,1)} %constant.65.clone.order_h), custom_call_target="tpu_custom_call" | custom-call | flops 262144 | bytes 655360 | tf_op jit(solution)/shard_map/reorder/pallas_call | solution.py:567
  11.3 0.3 collective-permute-done.3.diag.rest_4_.rest_9_
  11.7 3.8 %first_pass.1 = (f32[2,3,384,128]{3,2,1,0:T(8,128)S(1)}, f32[2,3,384,128]{3,2,1,0:T(8,128)S(1)}, f32[3,256,256]{2,1,0:T(8,128)S(1)}, bf16[800,128]{1,0:T(8,128)(...) custom-call(s32[9]{0:T(128)S(1)} %pad_add_fusion.meta, ...), custom_call_target="tpu_custom_call", output_to_operand_aliasing={{0}: (6, {}), {1}: (7, {})} | custom-call | flops 1073741824 | bytes 786432 | tf_op jit(solution)/shard_map/first_pass/pallas_call | solution.py:567
  15.5 2.2 %collective-permute-start.4 = (bf16[800,128]{1,0:T(8,128)(2,1)S(1)}, bf16[800,128]{1,0:T(8,128)(2,1)S(1)}, u32[]{:S(2)}, u32[]{:S(2)}) collective-permute-start(bf16[800,128]{1,0:T(8,128)(2,1)S(1)} %get-tuple-element.39), channel_id=1, source_target_pairs={{0,4},{4,0},{8,12},{12,8},{16,20},{20,16},{24,28},{28,24},{1,5},{5... | collective-permute-start | bytes 614408 | tf_op jit(solution)/shard_map/ppermute | solution.py:57
  17.7 0.7 collective-permute-start.5
  18.4 0.7 %collective-permute-start.6 = (bf16[528,128]{1,0:T(8,128)(2,1)S(1)}, bf16[528,128]{1,0:T(8,128)(2,1)S(1)}, u32[]{:S(2)}, u32[]{:S(2)}) collective-permute-start(bf16[528,128]{1,0:T(8,128)(2,1)S(1)} %get-tuple-element.41), channel_id=1, source_target_pairs={{0,0},{4,8},{8,4},{12,12},{16,16},{20,24},{24,20},{28,28},{1,1},{5... | collective-permute-start | bytes 405512 | tf_op jit(solution)/shard_map/ppermute | solution.py:66
  19.2 2.9 %collective-permute-start.7 = (bf16[2,2,128,128]{3,2,1,0:T(8,128)(2,1)S(1)}, bf16[2,2,128,128]{3,2,1,0:T(8,128)(2,1)S(1)}, u32[]{:S(2)}, u32[]{:S(2)}) collective-permute-start(bf16[2,2,128,128]{3,2,1,0:T(8,128)(2,1)S(1)} %get-tuple-element.43.rest_4_), channel_id=1, source_target_pairs={{0,16},{4,20},{8,24},{12,28},{16,0},{20,4},{24,8},{28,12},{1,17},{... | collective-permute-start | bytes 393224 | tf_op jit(solution)/shard_map/ppermute | solution.py:52
  22.1 2.7 %weigh.1 = (f32[3,384,128]{2,1,0:T(8,128)S(1)}, f32[2,256,256]{2,1,0:T(8,128)S(1)}, f32[2,256,256]{2,1,0:T(8,128)S(1)}, f32[2,256,256]{2,1,0:T(8,128)S(1)}, bf16...) custom-call(bf16[16,128]{1,0:T(8,128)(2,1)S(1)} %fusion.5.rest_0_, ...), custom_call_target="tpu_custom_call" | custom-call | flops 933888 | bytes 2359296 | tf_op jit(solution)/shard_map/weigh/pallas_call | solution.py:567
  24.8 1.7 %collective-permute-done.8.rest_3_.rest_5_ = bf16[2,128,128]{2,1,0:T(8,128)(2,1)S(1)} collective-permute-done((bf16[2,128,128]{2,1,0:T(8,128)(2,1)S(1)}, bf16[2,128,128]{2,1,0:T(8,128)(2,1)S(1)}, u32[]{:S(2)}, u32[]{:S(2)}) %collective-permute-start.8) | collective-permute-done | bytes 65568 | tf_op jit(solution)/shard_map/ppermute | solution.py:52
  26.5 3.6 %second_pass.1 = (f32[2,256,256]{2,1,0:T(8,128)S(1)}, f32[2,256,128]{2,1,0:T(8,128)S(1)}, bf16[2,256,128]{2,1,0:T(8,128)(2,1)S(1)}, bf16[2,128,128]{2,1,0:T(8,12...) custom-call(s32[9]{0:T(128)S(1)} %pad_add_fusion.meta, ...), custom_call_target="tpu_custom_call" | custom-call | flops 1073741824 | tf_op jit(solution)/shard_map/second_pass/pallas_call | solution.py:567
  30.1 7.7 %collective-permute-start.13 = (bf16[3,128,256]{2,1,0:T(8,128)(2,1)S(1)}, bf16[3,128,256]{2,1,0:T(8,128)(2,1)S(1)}, u32[]{:S(2)}, u32[]{:S(2)}) collective-permute-start(bf16[3,128,256]{2,1,0:T(8,128)(2,1)S(1)} %get-tuple-element.59), channel_id=1, source_target_pairs={{0,4},{4,0},{8,12},{12,8},{16,20},{20,16},{24,28},{28,24},{1,5},{5... | collective-permute-start | bytes 589832 | tf_op jit(solution)/shard_map/ppermute | solution.py:57
  37.8 1.1 %collective-permute-done.13.came = bf16[3,128,256]{2,1,0:T(8,128)(2,1)S(1)} collective-permute-done((bf16[3,128,256]{2,1,0:T(8,128)(2,1)S(1)}, bf16[3,128,256]{2,1,0:T(8,128)(2,1)S(1)}, u32[]{:S(2)}, u32[]{:S(2)}) %collective-permute-start.13) | collective-permute-done | bytes 196640 | tf_op jit(solution)/shard_map/ppermute | solution.py:57
  39.0 0.9 %collective-permute-start.18 = (bf16[3,128,256]{2,1,0:T(8,128)(2,1)S(1)}, bf16[3,128,256]{2,1,0:T(8,128)(2,1)S(1)}, u32[]{:S(2)}, u32[]{:S(2)}) collective-permute-start(bf16[3,128,256]{2,1,0:T(8,128)(2,1)S(1)} %halve.1.rest_0_.held), channel_id=1, source_target_pairs={{0,8},{4,12},{8,0},{12,4},{16,24},{20,28},{24,16},{28,20},{1,9},{5... | collective-permute-start | bytes 589832 | tf_op jit(solution)/shard_map/ppermute | solution.py:57
  39.8 3.0 %collective-permute-start.12 = (bf16[2,128,128]{2,1,0:T(8,128)(2,1)S(1)}, bf16[2,128,128]{2,1,0:T(8,128)(2,1)S(1)}, u32[]{:S(2)}, u32[]{:S(2)}) collective-permute-start(bf16[2,128,128]{2,1,0:T(8,128)(2,1)S(1)} %get-tuple-element.57), channel_id=1, source_target_pairs={{0,16},{4,20},{8,24},{12,28},{16,0},{20,4},{24,8},{28,12},{1,17},{... | collective-permute-start | bytes 196616 | tf_op jit(solution)/shard_map/ppermute | solution.py:52
  42.9 6.3 %collective-permute-done.12.above1 = bf16[2,128,128]{2,1,0:T(8,128)(2,1)S(1)} collective-permute-done((bf16[2,128,128]{2,1,0:T(8,128)(2,1)S(1)}, bf16[2,128,128]{2,1,0:T(8,128)(2,1)S(1)}, u32[]{:S(2)}, u32[]{:S(2)}) %collective-permute-start.12) | collective-permute-done | bytes 65568 | tf_op jit(solution)/shard_map/ppermute | solution.py:52
  49.2 1.4 %collective-permute-done.11.above0 = bf16[2,128,128]{2,1,0:T(8,128)(2,1)S(1)} collective-permute-done((bf16[2,128,128]{2,1,0:T(8,128)(2,1)S(1)}, bf16[2,128,128]{2,1,0:T(8,128)(2,1)S(1)}, u32[]{:S(2)}, u32[]{:S(2)}) %collective-permute-start.11) | collective-permute-done | bytes 65568 | tf_op jit(solution)/shard_map/ppermute | solution.py:52
  51.0 2.5 %collective-permute-start.19 = (bf16[3,128,256]{2,1,0:T(8,128)(2,1)S(1)}, bf16[3,128,256]{2,1,0:T(8,128)(2,1)S(1)}, u32[]{:S(2)}, u32[]{:S(2)}) collective-permute-start(bf16[3,128,256]{2,1,0:T(8,128)(2,1)S(1)} %add.23.held), channel_id=1, source_target_pairs={{0,24},{4,28},{8,16},{12,20},{16,8},{20,12},{24,0},{28,4},{1,25},{... | collective-permute-start | bytes 589832 | tf_op jit(solution)/shard_map/ppermute | solution.py:57
  53.5 1.1 %collective-permute-done.15.refs_3_ = bf16[2,128,256]{2,1,0:T(8,128)(2,1)S(1)} collective-permute-done((bf16[2,128,256]{2,1,0:T(8,128)(2,1)S(1)}, bf16[2,128,256]{2,1,0:T(8,128)(2,1)S(1)}, u32[]{:S(2)}, u32[]{:S(2)}) %collective-permute-start.15) | collective-permute-done | bytes 131104 | tf_op jit(solution)/shard_map/ppermute | solution.py:57
  54.6 0.4 collective-permute-done.14.refs_1_
  55.0 1.4 %collective-permute-start.16 = (bf16[2,128,256]{2,1,0:T(8,128)(2,1)S(1)}, bf16[2,128,256]{2,1,0:T(8,128)(2,1)S(1)}, u32[]{:S(2)}, u32[]{:S(2)}) collective-permute-start(bf16[2,128,256]{2,1,0:T(8,128)(2,1)S(1)} %get-tuple-element.62.first), channel_id=1, source_target_pairs={{0,2},{1,3},{2,0},{3,1},{4,6},{5,7},{6,4},{7,5},{8,10},{9,11},{10,... | collective-permute-start | bytes 393224 | tf_op jit(solution)/shard_map/ppermute | solution.py:57
  56.4 2.8 %collective-permute-done.16.first_came.rest_0_ = bf16[2,128,256]{2,1,0:T(8,128)(2,1)S(1)} collective-permute-done((bf16[2,128,256]{2,1,0:T(8,128)(2,1)S(1)}, bf16[2,128,256]{2,1,0:T(8,128)(2,1)S(1)}, u32[]{:S(2)}, u32[]{:S(2)}) %collective-permute-start.16) | collective-permute-done | bytes 131104 | tf_op jit(solution)/shard_map/ppermute | solution.py:57
  59.2 3.7 %collective-permute-done.19.came = bf16[3,128,256]{2,1,0:T(8,128)(2,1)S(1)} collective-permute-done((bf16[3,128,256]{2,1,0:T(8,128)(2,1)S(1)}, bf16[3,128,256]{2,1,0:T(8,128)(2,1)S(1)}, u32[]{:S(2)}, u32[]{:S(2)}) %collective-permute-start.19) | collective-permute-done | bytes 196640 | tf_op jit(solution)/shard_map/ppermute | solution.py:57
  63.0 0.7 %collective-permute-start.20 = (bf16[2,128,256]{2,1,0:T(8,128)(2,1)S(1)}, bf16[2,128,256]{2,1,0:T(8,128)(2,1)S(1)}, u32[]{:S(2)}, u32[]{:S(2)}) collective-permute-start(bf16[2,128,256]{2,1,0:T(8,128)(2,1)S(1)} %update.1), channel_id=1, source_target_pairs={{0,4},{4,0},{8,12},{12,8},{16,20},{20,16},{24,28},{28,24},{1,5},{5... | collective-permute-start | bytes 393224 | tf_op jit(solution)/shard_map/ppermute | solution.py:57
  63.7 1.2 %settle.1 = (f32[2,256,256]{2,1,0:T(8,128)}, f32[2,256,256]{2,1,0:T(8,128)}) custom-call(bf16[2,128,256]{2,1,0:T(8,128)(2,1)S(1)} %get-tuple-element.62.first, bf16[2,128,256]{2,1,0:T(8,128)(2,1)S(1)} %collective-permute-done.16.first_came.rest_0_, bf16[2,128,256]{2,1,0:T(8,128)(2,1)S(1)} %get-tuple-element.63.second, ...), custom_call_target="tpu_custom_call" | custom-call | flops 262144 | tf_op jit(solution)/shard_map/settle/pallas_call | solution.py:567
  64.9 0.9 %convert_add_fusion = f32[1,2,256,256]{3,2,1,0:T(8,128)} fusion(f32[1,2,256,256]{3,2,1,0:T(8,128)S(1)} %copy-done, bf16[1,2,128,256]{3,2,1,0:T(8,128)(2,1)S(1)} %bitcast.19, bf16[1,2,128,256]{3,2,1,0:T(8,128)(2,1)S(1)} %bitcast.28, pred[]{:T(512)} %eq.8), kind=kLoop, calls=%fused_computation | loop fusion | flops 1441792 | bytes 1310721 | tf_op jit(solution)/shard_map/add | solution.py:701
  (42 shorter events, 1.5 us)
Async XLA Ops:
  0.6 5.2 %copy-start.1 = (s32[1,1,4,2]{2,3,1,0:T(2,128)S(1)}, s32[1,1,4,2]{2,3,1,0:T(2,128)}, u32[]{:S(2)}) copy-start(s32[1,1,4,2]{2,3,1,0:T(2,128)} %param.13) | copy-start | bytes 100
  1.8 6.2 %collective-permute-start.1 = (bf16[256,128]{1,0:T(8,128)(2,1)S(1)}, bf16[256,128]{1,0:T(8,128)(2,1)S(1)}, u32[]{:S(2)}, u32[]{:S(2)}) collective-permute-start(bf16[256,128]{1,0:T(8,128)(2,1)S(1)} %bitcast.29), channel_id=1, source_target_pairs={{0,16},{4,20},{8,24},{12,28},{16,0},{20,4},{24,8},{28,12},{1,17},{... | collective-permute-start | bytes 196616 | tf_op jit(solution)/shard_map/ppermute | solution.py:52
  4.1 7.5 %collective-permute-start = (bf16[2,256,128]{2,1,0:T(8,128)(2,1)S(1)}, bf16[2,256,128]{2,1,0:T(8,128)(2,1)S(1)}, u32[]{:S(2)}, u32[]{:S(2)}) collective-permute-start(bf16[2,256,128]{2,1,0:T(8,128)(2,1)S(1)} %slice.12), channel_id=1, source_target_pairs={{0,12},{4,0},{8,4},{12,8},{16,28},{20,16},{24,20},{28,24},{1,13},{... | collective-permute-start | bytes 393224 | tf_op jit(solution)/shard_map/ppermute | solution.py:52
  6.1 5.2 %collective-permute-start.2 = (bf16[272,128]{1,0:T(8,128)(2,1)S(1)}, bf16[272,128]{1,0:T(8,128)(2,1)S(1)}, u32[]{:S(2)}, u32[]{:S(2)}) collective-permute-start(bf16[272,128]{1,0:T(8,128)(2,1)S(1)} %pad_maximum_fusion), channel_id=1, source_target_pairs={{0,16},{4,20},{8,24},{12,28},{16,0},{20,4},{24,8},{28,12},{1,17},{... | collective-permute-start | bytes 208904 | tf_op jit(solution)/shard_map/ppermute | solution.py:52
  7.9 3.7 %collective-permute-start.3 = (bf16[256,128]{1,0:T(8,128)(2,1)S(1)}, bf16[256,128]{1,0:T(8,128)(2,1)S(1)}, u32[]{:S(2)}, u32[]{:S(2)}) collective-permute-start(bf16[256,128]{1,0:T(8,128)(2,1)S(1)} %collective-permute-done.1.below.below0.rest_2_.rest_8_), channel_id=1, source_target_pairs={{0,12},{4,0},{8,4},{12,8},{16,28},{20,16},{24,20},{28,24},{1,13},{... | collective-permute-start | bytes 196616 | tf_op jit(solution)/shard_map/ppermute | solution.py:52
  15.5 3.6 %collective-permute-start.4 = (bf16[800,128]{1,0:T(8,128)(2,1)S(1)}, bf16[800,128]{1,0:T(8,128)(2,1)S(1)}, u32[]{:S(2)}, u32[]{:S(2)}) collective-permute-start(bf16[800,128]{1,0:T(8,128)(2,1)S(1)} %get-tuple-element.39), channel_id=1, source_target_pairs={{0,4},{4,0},{8,12},{12,8},{16,20},{20,16},{24,28},{28,24},{1,5},{5... | collective-permute-start | bytes 614408 | tf_op jit(solution)/shard_map/ppermute | solution.py:57
  17.7 1.3 %collective-permute-start.5 = (bf16[288,128]{1,0:T(8,128)(2,1)S(1)}, bf16[288,128]{1,0:T(8,128)(2,1)S(1)}, u32[]{:S(2)}, u32[]{:S(2)}) collective-permute-start(bf16[288,128]{1,0:T(8,128)(2,1)S(1)} %get-tuple-element.40), channel_id=1, source_target_pairs={{0,0},{4,8},{8,4},{12,12},{16,16},{20,24},{24,20},{28,28},{1,1},{5... | collective-permute-start | bytes 221192 | tf_op jit(solution)/shard_map/ppermute | solution.py:66
  18.4 6.4 %collective-permute-start.6 = (bf16[528,128]{1,0:T(8,128)(2,1)S(1)}, bf16[528,128]{1,0:T(8,128)(2,1)S(1)}, u32[]{:S(2)}, u32[]{:S(2)}) collective-permute-start(bf16[528,128]{1,0:T(8,128)(2,1)S(1)} %get-tuple-element.41), channel_id=1, source_target_pairs={{0,0},{4,8},{8,4},{12,12},{16,16},{20,24},{24,20},{28,28},{1,1},{5... | collective-permute-start | bytes 405512 | tf_op jit(solution)/shard_map/ppermute | solution.py:66
  19.2 7.3 %collective-permute-start.7 = (bf16[2,2,128,128]{3,2,1,0:T(8,128)(2,1)S(1)}, bf16[2,2,128,128]{3,2,1,0:T(8,128)(2,1)S(1)}, u32[]{:S(2)}, u32[]{:S(2)}) collective-permute-start(bf16[2,2,128,128]{3,2,1,0:T(8,128)(2,1)S(1)} %get-tuple-element.43.rest_4_), channel_id=1, source_target_pairs={{0,16},{4,20},{8,24},{12,28},{16,0},{20,4},{24,8},{28,12},{1,17},{... | collective-permute-start | bytes 393224 | tf_op jit(solution)/shard_map/ppermute | solution.py:52
  22.1 4.4 %collective-permute-start.8 = (bf16[2,128,128]{2,1,0:T(8,128)(2,1)S(1)}, bf16[2,128,128]{2,1,0:T(8,128)(2,1)S(1)}, u32[]{:S(2)}, u32[]{:S(2)}) collective-permute-start(bf16[2,128,128]{2,1,0:T(8,128)(2,1)S(1)} %get-tuple-element.44), channel_id=1, source_target_pairs={{0,16},{4,20},{8,24},{12,28},{16,0},{20,4},{24,8},{28,12},{1,17},{... | collective-permute-start | bytes 196616 | tf_op jit(solution)/shard_map/ppermute | solution.py:52
  30.1 8.8 %collective-permute-start.13 = (bf16[3,128,256]{2,1,0:T(8,128)(2,1)S(1)}, bf16[3,128,256]{2,1,0:T(8,128)(2,1)S(1)}, u32[]{:S(2)}, u32[]{:S(2)}) collective-permute-start(bf16[3,128,256]{2,1,0:T(8,128)(2,1)S(1)} %get-tuple-element.59), channel_id=1, source_target_pairs={{0,4},{4,0},{8,12},{12,8},{16,20},{20,16},{24,28},{28,24},{1,5},{5... | collective-permute-start | bytes 589832 | tf_op jit(solution)/shard_map/ppermute | solution.py:57
  37.8 5.0 %collective-permute-start.10 = (bf16[2,128,128]{2,1,0:T(8,128)(2,1)S(1)}, bf16[2,128,128]{2,1,0:T(8,128)(2,1)S(1)}, u32[]{:S(2)}, u32[]{:S(2)}) collective-permute-start(bf16[2,128,128]{2,1,0:T(8,128)(2,1)S(1)} %get-tuple-element.56), channel_id=1, source_target_pairs={{0,4},{4,8},{8,12},{12,0},{16,20},{20,24},{24,28},{28,16},{1,5},{5... | collective-permute-start | bytes 196616 | tf_op jit(solution)/shard_map/ppermute | solution.py:52
  37.8 12.8 %collective-permute-start.9 = (bf16[2,256,128]{2,1,0:T(8,128)(2,1)S(1)}, bf16[2,256,128]{2,1,0:T(8,128)(2,1)S(1)}, u32[]{:S(2)}, u32[]{:S(2)}) collective-permute-start(bf16[2,256,128]{2,1,0:T(8,128)(2,1)S(1)} %get-tuple-element.54), channel_id=1, source_target_pairs={{0,4},{4,8},{8,12},{12,0},{16,20},{20,24},{24,28},{28,16},{1,5},{5... | collective-permute-start | bytes 393224 | tf_op jit(solution)/shard_map/ppermute | solution.py:52
  39.0 11.9 %collective-permute-start.18 = (bf16[3,128,256]{2,1,0:T(8,128)(2,1)S(1)}, bf16[3,128,256]{2,1,0:T(8,128)(2,1)S(1)}, u32[]{:S(2)}, u32[]{:S(2)}) collective-permute-start(bf16[3,128,256]{2,1,0:T(8,128)(2,1)S(1)} %halve.1.rest_0_.held), channel_id=1, source_target_pairs={{0,8},{4,12},{8,0},{12,4},{16,24},{20,28},{24,16},{28,20},{1,9},{5... | collective-permute-start | bytes 589832 | tf_op jit(solution)/shard_map/ppermute | solution.py:57
  39.8 9.4 %collective-permute-start.12 = (bf16[2,128,128]{2,1,0:T(8,128)(2,1)S(1)}, bf16[2,128,128]{2,1,0:T(8,128)(2,1)S(1)}, u32[]{:S(2)}, u32[]{:S(2)}) collective-permute-start(bf16[2,128,128]{2,1,0:T(8,128)(2,1)S(1)} %get-tuple-element.57), channel_id=1, source_target_pairs={{0,16},{4,20},{8,24},{12,28},{16,0},{20,4},{24,8},{28,12},{1,17},{... | collective-permute-start | bytes 196616 | tf_op jit(solution)/shard_map/ppermute | solution.py:52
  42.8 7.8 %collective-permute-start.11 = (bf16[2,128,128]{2,1,0:T(8,128)(2,1)S(1)}, bf16[2,128,128]{2,1,0:T(8,128)(2,1)S(1)}, u32[]{:S(2)}, u32[]{:S(2)}) collective-permute-start(bf16[2,128,128]{2,1,0:T(8,128)(2,1)S(1)} %add_rim.1), channel_id=1, source_target_pairs={{0,16},{4,20},{8,24},{12,28},{16,0},{20,4},{24,8},{28,12},{1,17},{... | collective-permute-start | bytes 196616 | tf_op jit(solution)/shard_map/ppermute | solution.py:52
  50.7 3.9 %collective-permute-start.15 = (bf16[2,128,256]{2,1,0:T(8,128)(2,1)S(1)}, bf16[2,128,256]{2,1,0:T(8,128)(2,1)S(1)}, u32[]{:S(2)}, u32[]{:S(2)}) collective-permute-start(bf16[2,128,256]{2,1,0:T(8,128)(2,1)S(1)} %get-tuple-element.61.refs_2_), channel_id=1, source_target_pairs={{0,2},{1,3},{2,0},{3,1},{4,6},{5,7},{6,4},{7,5},{8,10},{9,11},{10,... | collective-permute-start | bytes 393224 | tf_op jit(solution)/shard_map/ppermute | solution.py:57
  50.8 4.2 %collective-permute-start.14 = (bf16[2,128,256]{2,1,0:T(8,128)(2,1)S(1)}, bf16[2,128,256]{2,1,0:T(8,128)(2,1)S(1)}, u32[]{:S(2)}, u32[]{:S(2)}) collective-permute-start(bf16[2,128,256]{2,1,0:T(8,128)(2,1)S(1)} %get-tuple-element.60.refs_0_.rest_0_), channel_id=1, source_target_pairs={{0,1},{1,0},{2,3},{3,2},{4,5},{5,4},{6,7},{7,6},{8,9},{9,8},{10,11... | collective-permute-start | bytes 393224 | tf_op jit(solution)/shard_map/ppermute | solution.py:57
  51.0 14.0 %copy-start = (f32[1,2,256,256]{3,2,1,0:T(8,128)S(1)}, f32[1,2,256,256]{3,2,1,0:T(8,128)}, u32[]{:S(2)}) copy-start(f32[1,2,256,256]{3,2,1,0:T(8,128)} %param.11) | copy-start | bytes 1572868
  51.0 12.0 %collective-permute-start.19 = (bf16[3,128,256]{2,1,0:T(8,128)(2,1)S(1)}, bf16[3,128,256]{2,1,0:T(8,128)(2,1)S(1)}, u32[]{:S(2)}, u32[]{:S(2)}) collective-permute-start(bf16[3,128,256]{2,1,0:T(8,128)(2,1)S(1)} %add.23.held), channel_id=1, source_target_pairs={{0,24},{4,28},{8,16},{12,20},{16,8},{20,12},{24,0},{28,4},{1,25},{... | collective-permute-start | bytes 589832 | tf_op jit(solution)/shard_map/ppermute | solution.py:57
  55.0 4.2 %collective-permute-start.16 = (bf16[2,128,256]{2,1,0:T(8,128)(2,1)S(1)}, bf16[2,128,256]{2,1,0:T(8,128)(2,1)S(1)}, u32[]{:S(2)}, u32[]{:S(2)}) collective-permute-start(bf16[2,128,256]{2,1,0:T(8,128)(2,1)S(1)} %get-tuple-element.62.first), channel_id=1, source_target_pairs={{0,2},{1,3},{2,0},{3,1},{4,6},{5,7},{6,4},{7,5},{8,10},{9,11},{10,... | collective-permute-start | bytes 393224 | tf_op jit(solution)/shard_map/ppermute | solution.py:57
  56.4 7.3 %collective-permute-start.17 = (bf16[2,128,256]{2,1,0:T(8,128)(2,1)S(1)}, bf16[2,128,256]{2,1,0:T(8,128)(2,1)S(1)}, u32[]{:S(2)}, u32[]{:S(2)}) collective-permute-start(bf16[2,128,256]{2,1,0:T(8,128)(2,1)S(1)} %get-tuple-element.63.second), channel_id=1, source_target_pairs={{0,1},{1,0},{2,3},{3,2},{4,5},{5,4},{6,7},{7,6},{8,9},{9,8},{10,11... | collective-permute-start | bytes 393224 | tf_op jit(solution)/shard_map/ppermute | solution.py:57
  63.0 1.9 %collective-permute-start.20 = (bf16[2,128,256]{2,1,0:T(8,128)(2,1)S(1)}, bf16[2,128,256]{2,1,0:T(8,128)(2,1)S(1)}, u32[]{:S(2)}, u32[]{:S(2)}) collective-permute-start(bf16[2,128,256]{2,1,0:T(8,128)(2,1)S(1)} %update.1), channel_id=1, source_target_pairs={{0,4},{4,0},{8,12},{12,8},{16,20},{20,16},{24,28},{28,24},{1,5},{5... | collective-permute-start | bytes 393224 | tf_op jit(solution)/shard_map/ppermute | solution.py:57
